TPU v7x, 32 devices: a whole 2x2x4 slice. The times are simulated.
32 devices in a mesh: tile: 8 (over y, x, core), member: 4 (over z).
Axes of the slice: x: 2, y: 2, z: 4, core: 2. Of those that a mesh axis runs over, the one named last changes fastest.
Arguments:
- residual_in: float32 [64, 128, 512], P(None, 'tile', 'member'), may hold values from -6 to 6
- members: bfloat16 [8, 64, 128, 512], P('member', None, 'tile'), may hold values from -6 to 6
- wind_x: float32 [64], replicated, may hold values from 0.05 to 0.25
- wind_y: float32 [64], replicated, may hold values from 0.05 to 0.25
Outputs:
- analysis: float32 [64, 128, 512], P(None, 'tile', 'member')
- residual: float32 [64, 128, 512], P(None, 'tile', 'member')
All inputs are finite; a program needn't handle non-finite values.
Results may differ from a plain program's by a relative error of at most 0.006.
Values may be sent and summed in bfloat16 or wider, within the bound.
No kernel may reach another device: no remote copies, remote signals or barrier semaphores. Data moves between devices by JAX's collectives and lax.ppermute only.
A program may use at most 64 MiB of HBM per device.

v0:
```python
import functools

import jax
import jax.numpy as jnp
from jax import lax
from jax.experimental import pallas as pl
from jax.experimental.pallas import tpu as pltpu
from jax.sharding import PartitionSpec as P

ITERS = 2
MODEL_STEPS = 4
DIFFUSION = 0.1
RELAX = 0.5
REACH = 16
TAPER_TOTAL = sum(1.0 - (k / 17.0) ** 2 for k in range(-REACH, REACH + 1))
F32 = jnp.float32
BF16 = jnp.bfloat16
LANES = 128
SUB = 8
GROUP = LANES // (2 * MODEL_STEPS)

VMEM = pl.BlockSpec(memory_space=pltpu.VMEM)
PARAMS = pltpu.CompilerParams(vmem_limit_bytes=48 * 1024 * 1024)


def call(body, out_shape, *args, in_specs=None, scratch=()):
    return pl.pallas_call(
        body,
        out_shape=out_shape,
        in_specs=in_specs or [VMEM] * len(args),
        out_specs=jax.tree.map(lambda _: VMEM, out_shape),
        scratch_shapes=scratch,
        compiler_params=PARAMS,
    )(*args)


def lane_iota(shape):
    return lax.broadcasted_iota(jnp.int32, shape, len(shape) - 1)


def sub_iota(shape):
    return lax.broadcasted_iota(jnp.int32, shape, len(shape) - 2)


def neighbor_of(step):
    parts = lax.axis_size("member")
    at = lax.axis_index("member") + step
    return jnp.where(at < 0, at + parts, jnp.where(at >= parts, at - parts, at))


def columns_split_body(in_ref, *out_refs):
    cols = out_refs[0].shape[-1]
    for r, out_ref in enumerate(out_refs):
        out_ref[...] = in_ref[:, :, :, pl.ds(pl.multiple_of(neighbor_of(r) * cols, cols), cols)]


def split_columns(members, parts):
    own, levels, rows, ny = members.shape
    out = jax.ShapeDtypeStruct((own, levels, rows, ny // parts), members.dtype)
    return call(columns_split_body, (out,) * parts, members, in_specs=[VMEM])


def left_slot(k):
    return 3 * SUB - 1 - k % SUB - GROUP * (k // SUB)


def put_left(x, k, total):
    here = lane_iota(x.shape) // MODEL_STEPS == left_slot(k)
    return jnp.where(here, pltpu.roll(x, (MODEL_STEPS * (left_slot(k) + 1)) % LANES, 1), total)


def put_right(x, k, total):
    here = lane_iota(x.shape) // MODEL_STEPS == left_slot(k) + SUB
    return jnp.where(here, pltpu.roll(x, MODEL_STEPS * (left_slot(k) + SUB), 1), total)


def sides_body(in_ref, out_ref):
    parts, own, groups, rows, _ = out_ref.shape
    cols = in_ref.shape[-1] // parts
    for r in range(parts):
        before, after = (pl.ds((r + parts + d) % parts * cols, cols) for d in (-1, 1))
        for m in range(own):

            def step(g, carry):
                total = jnp.zeros((rows, LANES), F32)
                for k in range(GROUP):
                    total = put_left(in_ref[m, g * GROUP + k, :, before].astype(F32), k, total)
                    total = put_right(in_ref[m, g * GROUP + k, :, after].astype(F32), k, total)
                out_ref[r, m, g] = total.astype(out_ref.dtype)
                return carry

            lax.fori_loop(0, groups, step, 0)


def side_columns(members, parts):
    own, levels, rows, ny = members.shape
    return call(sides_body, jax.ShapeDtypeStruct((parts, own, levels // GROUP, rows, LANES), members.dtype), members)


def pack_rows(ref, at, top_ref, bottom_ref):
    upper = sub_iota((SUB, LANES)) < MODEL_STEPS
    count, rows, _ = ref.shape
    for q in range(count // 2):
        top_ref[at + q] = jnp.where(upper, ref[2 * q, :SUB], pltpu.roll(ref[2 * q + 1, :SUB], MODEL_STEPS, 0))
        bottom_ref[at + q] = jnp.where(
            upper, pltpu.roll(ref[2 * q, rows - SUB :], MODEL_STEPS, 0), ref[2 * q + 1, rows - SUB :]
        )


def rows_body(x_ref, left_ref, right_ref, beside_ref, top_ref, bottom_ref):
    beside_ref[...] = left_ref[...] + right_ref[...]
    pack_rows(x_ref, 0, top_ref, bottom_ref)
    pack_rows(beside_ref, x_ref.shape[0] // 2, top_ref, bottom_ref)


def columns_edge_body(x_ref, first_ref, last_ref):
    levels, rows, cols = x_ref.shape
    for g in range(levels // GROUP):
        first = jnp.zeros((rows, LANES), F32)
        last = jnp.zeros((rows, LANES), F32)
        for k in range(GROUP):
            last = put_left(x_ref[g * GROUP + k], k, last)
            first = put_right(x_ref[g * GROUP + k], k, first)
        first_ref[g] = first
        last_ref[g] = last


def shift(x, axis, step):
    count = lax.axis_size(axis)
    pairs = [(i, i + step) for i in range(count) if 0 <= i + step < count]
    return lax.ppermute(x, axis, pairs)


def model_parts(wx_ref, wy_ref, x_ref, above_ref, below_ref, side_row, grad_ref):
    levels, rows, cols = x_ref.shape
    tile, tiles = lax.axis_index("tile"), lax.axis_size("tile")
    member, parts = lax.axis_index("member"), lax.axis_size("member")
    x_flat = x_ref.reshape(levels * rows, cols)
    grad_flat = grad_ref.reshape(levels * rows, cols)
    halo = MODEL_STEPS
    if above_ref is not None:
        pairs = above_ref.shape[0]
        above_flat = above_ref.reshape(pairs * SUB, LANES)
        below_flat = below_ref.reshape(pairs * SUB, LANES)

    half = LANES // 2
    lane = lane_iota((SUB, LANES))
    on_right = lane % half < halo
    first_of = (lane == 0, lane == half)
    last_of = (lane == LANES - 1, lane == half - 1)
    second = (lane >= half // 2) & (lane < half + half // 2)
    inside = (on_right & (member < parts - 1)) | ((lane % half >= half - halo) & (member > 0))
    side_mask = jnp.where(inside, 1.0, 0.0).astype(F32)
    has_above = jnp.where(tile > 0, 1.0, 0.0).astype(F32)
    has_below = jnp.where(tile < tiles - 1, 1.0, 0.0).astype(F32)

    def load(g, e):
        centers = []
        for q in (2 * g, 2 * g + 1):
            if e < 0:
                centers.append(above_flat[pl.ds(q * SUB * halo + e + halo, SUB, stride=halo), :])
            elif e < rows:
                centers.append(x_flat[pl.ds(q * SUB * rows + e, SUB, stride=rows), :])
            else:
                centers.append(below_flat[pl.ds(q * SUB * halo + e - rows, SUB, stride=halo), :])
        row = jnp.broadcast_to(side_row(g, e), (SUB, LANES))
        right = pltpu.roll(row, halo, 1, stride=halo, stride_axis=0)
        left = pltpu.roll(row, LANES // 4, 1, stride=halo, stride_axis=0)
        side = jnp.where(on_right, right, left) * side_mask
        return centers[0], pltpu.roll(centers[1], half, 1), side

    def advance(before, here, after, e, coefficients):
        fore = [pltpu.roll(x, LANES - 1, 1) for x in here]
        back = [pltpu.roll(x, 1, 1) for x in here]
        fore_side = jnp.where(last_of[0], fore[0], jnp.where(last_of[1], fore[1], fore[2]))
        back_side = jnp.where(first_of[0], back[0], jnp.where(first_of[1], back[1], back[2]))
        fores = [jnp.where(last_of[i], fore[2], fore[i]) for i in range(2)] + [fore_side]
        backs = [jnp.where(first_of[i], back[2], back[i]) for i in range(2)] + [back_side]
        result = []
        for i, (own, ahead_x, ahead_y) in enumerate(coefficients):
            value = own * here[i] + ahead_x * after[i] + ahead_y * fores[i] + DIFFUSION * (before[i] + backs[i])
            if e < 0:
                value = value * has_above
            if e >= rows:
                value = value * has_below
            result.append(value * side_mask if i == 2 else value)
        return tuple(result)

    def coefficients_of(g):
        coefficients = []
        for q in (2 * g, 2 * g + 1):
            at = pl.ds(pl.multiple_of(q * SUB, SUB), SUB)
            wx, wy = wx_ref[at, :], wy_ref[at, :]
            coefficients.append((1.0 - 4.0 * DIFFUSION - wx - wy, DIFFUSION + wx, DIFFUSION + wy))
        coefficients.append(tuple(jnp.where(second, b, a) for a, b in zip(*coefficients)))
        return coefficients

    def store(g, e, field):
        grad_flat[pl.ds(2 * g * SUB * rows + e, SUB, stride=rows), :] = field[0]
        grad_flat[pl.ds((2 * g + 1) * SUB * rows + e, SUB, stride=rows), :] = pltpu.roll(field[1], half, 1)

    return load, advance, coefficients_of, store


def sweep(x_ref, parts):
    levels, rows, cols = x_ref.shape
    load, advance, coefficients_of, store = parts
    halo = MODEL_STEPS

    def group(g, carry):
        coefficients = coefficients_of(g)
        fields = [{} for _ in range(halo + 1)]
        for front in range(-halo, rows + halo):
            fields[0][front] = load(g, front)
            for n in range(1, halo + 1):
                e = front - n
                if -halo + n <= e < rows + halo - n:
                    old = fields[n - 1]
                    fields[n][e] = advance(old[e - 1], old[e], old[e + 1], e, coefficients)
            e = front - halo
            if 0 <= e < rows:
                store(g, e, fields[halo][e])
        return carry

    lax.fori_loop(0, levels // GROUP, group, 0)


def kept_rows(rows):
    return [(n, e) for n in range(1, MODEL_STEPS) for e in (n, n + 1, rows - 2 - n, rows - 1 - n)]


def inner_sweep(x_ref, parts, kept_ref):
    levels, rows, cols = x_ref.shape
    load, advance, coefficients_of, store = parts
    halo = MODEL_STEPS

    def group(g, carry):
        coefficients = coefficients_of(g)
        fields = [{} for _ in range(halo + 1)]
        for front in range(rows):
            fields[0][front] = load(g, front)
            for n in range(1, halo + 1):
                e = front - n
                if n <= e < rows - n:
                    old = fields[n - 1]
                    fields[n][e] = advance(old[e - 1], old[e], old[e + 1], e, coefficients)
            e = front - halo
            if halo <= e < rows - halo:
                store(g, e, fields[halo][e])
        for i, (n, e) in enumerate(kept_rows(rows)):
            for j in range(3):
                kept_ref[g, i, j] = fields[n][e][j]
        return carry

    lax.fori_loop(0, levels // GROUP, group, 0)


def outer_sweep(x_ref, parts, kept_ref):
    levels, rows, cols = x_ref.shape
    load, advance, coefficients_of, store = parts
    halo = MODEL_STEPS

    def group(g, carry):
        coefficients = coefficients_of(g)
        fields = [{} for _ in range(halo + 1)]
        for i, (n, e) in enumerate(kept_rows(rows)):
            fields[n][e] = tuple(kept_ref[g, i, j] for j in range(3))
        for e in (*range(-halo, 2), *range(rows - 2, rows + halo)):
            fields[0][e] = load(g, e)
        for n in range(1, halo + 1):
            old = fields[n - 1]
            for e in (*range(n - halo, n), *range(rows - n, rows + halo - n)):
                fields[n][e] = advance(old[e - 1], old[e], old[e + 1], e, coefficients)
        for e in (*range(halo), *range(rows - halo, rows)):
            store(g, e, fields[halo][e])
        return carry

    lax.fori_loop(0, levels // GROUP, group, 0)


def side_rows(levels, rows, beside_ref, above_ref, below_ref):
    def side_row(g, e):
        if 0 <= e < rows:
            return beside_ref[g, pl.ds(e, 1), :]
        ref, row = (above_ref, e + MODEL_STEPS) if e < 0 else (below_ref, e - rows)
        flat = ref.reshape(ref.shape[0] * SUB, LANES)
        return flat[pl.ds((levels + g) * MODEL_STEPS + row, 1), :]

    return side_row


def first_model_body(wx_ref, wy_ref, x_ref, beside_ref, above_ref, below_ref, grad_ref):
    levels, rows, cols = x_ref.shape
    side_row = side_rows(levels, rows, beside_ref, above_ref, below_ref)
    sweep(x_ref, model_parts(wx_ref, wy_ref, x_ref, above_ref, below_ref, side_row, grad_ref))


def inner_model_body(wx_ref, wy_ref, x_ref, beside_ref, grad_ref, kept_ref):
    levels, rows, cols = x_ref.shape
    side_row = side_rows(levels, rows, beside_ref, None, None)
    inner_sweep(x_ref, model_parts(wx_ref, wy_ref, x_ref, None, None, side_row, grad_ref), kept_ref)


def outer_model_body(wx_ref, wy_ref, x_ref, beside_ref, above_thin_ref, below_thin_ref, inner_ref, kept_ref, *refs):
    *others, grad_ref, above_ref, below_ref = refs
    levels, rows, cols = x_ref.shape
    above_ref[...] = above_thin_ref[...].astype(F32).reshape(above_ref.shape)
    below_ref[...] = below_thin_ref[...].astype(F32).reshape(below_ref.shape)
    side_row = side_rows(levels, rows, beside_ref, above_ref, below_ref)
    outer_sweep(x_ref, model_parts(wx_ref, wy_ref, x_ref, above_ref, below_ref, side_row, grad_ref), kept_ref)
    row = sub_iota((rows, cols))
    inside = (row >= MODEL_STEPS) & (row < rows - MODEL_STEPS)
    project_levels(lambda level: jnp.where(inside, inner_ref[level], grad_ref[level]), levels, *others)


def project_body(grad_ref, *refs):
    project_levels(lambda level: grad_ref[level], grad_ref.shape[0], *refs)


def project_levels(grad, levels, *refs):
    *member_refs, wide_ref, thin_ref = refs
    own, _, rows, cols = member_refs[0].shape
    count = len(member_refs) * own

    def step(q, carry):
        carry = list(carry)
        for u in range(2):
            g = grad(2 * q + u)
            for m in range(count):
                carry[m] = carry[m] + member_refs[m // own][m % own, 2 * q + u].astype(F32) * g
        return tuple(carry)

    total = lax.fori_loop(0, levels // 2, step, (jnp.zeros((rows, cols), F32),) * count)
    for m in range(count):
        at = neighbor_of(-(m // own)) * own + m % own
        wide_ref[at] = total[m]
        thin_ref[at] = total[m].astype(BF16)


def taper(offset):
    k = offset.astype(F32)
    w = (1.0 - (k / 17.0) * (k / 17.0)) * (1.0 / TAPER_TOTAL)
    return jnp.where(jnp.abs(offset) <= REACH, w, 0.0)


def halves(x):
    high = x.astype(BF16)
    return high, (x - high.astype(F32)).astype(BF16)


def sharp_dot(a, b):
    ah, al = halves(a)
    bh, bl = halves(b)
    dot = functools.partial(jnp.dot, preferred_element_type=F32)
    return dot(ah, bh) + dot(al, bh) + dot(ah, bl)


def columns_body(left_ref, mid_ref, right_ref, wide_ref, thin_ref):
    count, rows, cols = mid_ref.shape
    wide = jnp.concatenate(
        [r[...].astype(F32).reshape(count * rows, cols) for r in (left_ref, mid_ref, right_ref)], axis=1
    )
    shape = (3 * cols, wide_ref.shape[0] // count * cols)
    lane = lane_iota(shape)
    beside = lane % MODEL_STEPS + jnp.where((lane // (SUB * MODEL_STEPS)) % 2 == 0, -MODEL_STEPS, cols)
    target = jnp.where(lane < cols, lane, beside)
    out = sharp_dot(wide, taper(sub_iota(shape) - cols - target))
    for i in range(shape[1] // cols):
        part = out[:, i * cols : (i + 1) * cols].reshape(count, rows, cols)
        wide_ref[i * count : (i + 1) * count] = part
        thin_ref[i * count : (i + 1) * count] = part.astype(BF16)


def smooth_rows(above_ref, mid_ref, below_ref):
    count, rows, cols = mid_ref.shape
    tall = jnp.concatenate(
        [
            jnp.concatenate([above_ref[m].astype(F32), mid_ref[m], below_ref[m].astype(F32)], axis=0)
            for m in range(count)
        ],
        axis=1,
    )
    shape = (rows, 3 * rows)
    out = sharp_dot(taper(lane_iota(shape) - sub_iota(shape) - rows), tall)
    return [out[:, m * cols : (m + 1) * cols] for m in range(count)]


def increments(member_refs, local_ref, levels, emit):
    own = member_refs[0].shape[0]
    count = len(member_refs) * own
    local = [local_ref[neighbor_of(-(m // own)) * own + m % own] for m in range(count)]

    def step(q, carry):
        for u in range(2):
            level = 2 * q + u
            total = member_refs[0][0, level].astype(F32) * local[0]
            for m in range(1, count):
                total = total + member_refs[m // own][m % own, level].astype(F32) * local[m]
            emit(level, total)
        return carry

    lax.fori_loop(0, levels // 2, step, 0)


def update_body(parts, residual_ref, around_ref, above_ref, mid_ref, below_ref, *refs):
    member_refs, sides_ref = refs[:parts], refs[parts]
    analysis_ref, out_ref, beside_ref, top_ref, bottom_ref, local_ref, top_wide_ref, bottom_wide_ref = refs[parts + 1 :]
    levels, rows, cols = residual_ref.shape
    own = member_refs[0].shape[0]
    count = parts * own
    for m, value in enumerate(smooth_rows(above_ref, mid_ref, below_ref)):
        local_ref[m] = value

    def emit(level, value):
        analysis_ref[level] = value
        out_ref[level] = residual_ref[level] - RELAX * value

    increments(member_refs, local_ref, levels, emit)
    for g in range(levels // GROUP):
        total = jnp.zeros((rows, LANES), F32)
        for m in range(count):
            total = total + sides_ref[m // own, m % own, g].astype(F32) * local_ref[count + m]
        beside_ref[g] = around_ref[g] - RELAX * total
    pack_rows(out_ref, 0, top_wide_ref, bottom_wide_ref)
    pack_rows(beside_ref, levels // 2, top_wide_ref, bottom_wide_ref)
    top_ref[...] = top_wide_ref[...].reshape(top_ref.shape).astype(BF16)
    bottom_ref[...] = bottom_wide_ref[...].reshape(bottom_ref.shape).astype(BF16)


def final_body(parts, residual_ref, before_ref, above_ref, mid_ref, below_ref, *refs):
    member_refs = refs[:parts]
    analysis_ref, out_ref, local_ref = refs[parts:]
    for m, value in enumerate(smooth_rows(above_ref, mid_ref, below_ref)):
        local_ref[m] = value

    def emit(level, value):
        analysis_ref[level] = before_ref[level] + value
        out_ref[level] = residual_ref[level] - RELAX * value

    increments(member_refs, local_ref, residual_ref.shape[0], emit)


def per_device(residual_in, members, wind_x, wind_y):
    levels, rows, cols = residual_in.shape
    parts = lax.axis_size("member")
    count = members.shape[0] * parts
    groups = levels // GROUP

    def shape(*dims, kind=F32):
        return jax.ShapeDtypeStruct(dims, kind)

    def both(*dims):
        return shape(*dims), shape(*dims, kind=BF16)

    def turned(x, step):
        return lax.ppermute(x, "member", [(i, (i + step) % parts) for i in range(parts)])

    def smoothed(wide, thin, planes):
        wide, thin = call(
            columns_body, both(planes, rows, cols), shift(thin, "member", 1), wide, shift(thin, "member", -1)
        )
        return shift(thin, "tile", 1), wide, shift(thin, "tile", -1)

    like = shape(levels, rows, cols)
    halo = shape((levels + groups) // 2, SUB, LANES)
    thin_halo = shape((levels + groups) // 4, 2 * SUB, LANES, kind=BF16)
    wide_halo = [pltpu.VMEM(halo.shape, F32)] * 2
    packed = shape(groups, rows, LANES)
    wind_x, wind_y = (jnp.broadcast_to(w[:, None], (levels, LANES)) for w in (wind_x, wind_y))

    first, last = call(columns_edge_body, (packed, packed), residual_in)
    left, right = shift(last, "member", 1), shift(first, "member", -1)
    blocks, left, right = lax.optimization_barrier((split_columns(members, parts), left, right))
    blocks = [turned(x, r) if r else x for r, x in enumerate(blocks)]
    around, top, bottom = call(rows_body, (packed, halo, halo), residual_in, left, right)
    members, around = lax.optimization_barrier((members, around))
    sides = side_columns(members, parts)
    above, below = shift(bottom, "tile", 1), shift(top, "tile", -1)
    grad = call(
        first_model_body, like,
        wind_x, wind_y, residual_in, around, above, below, in_specs=[VMEM] * 6,
    )
    grad, sides = lax.optimization_barrier((grad, sides))
    sides = lax.all_to_all(sides, "member", split_axis=0, concat_axis=0, tiled=True)
    grad, sides = lax.optimization_barrier((grad, sides))
    wide, thin = call(
        project_body, both(count, rows, cols), grad, *blocks, in_specs=[VMEM] * (1 + parts)
    )

    analysis, residual, beside, top, bottom = call(
        functools.partial(update_body, parts), (like, like, packed, thin_halo, thin_halo),
        residual_in, around, *smoothed(wide, thin, 2 * count), *blocks, sides,
        in_specs=[VMEM] * (6 + parts),
        scratch=[pltpu.VMEM((2 * count, rows, cols), F32)] + wide_halo,
    )
    above, below = shift(bottom, "tile", 1), shift(top, "tile", -1)
    kept = shape(groups, len(kept_rows(rows)), 3, SUB, LANES)
    inner, kept = call(inner_model_body, (like, kept), wind_x, wind_y, residual, beside)
    wide, thin = call(
        outer_model_body, both(count, rows, cols),
        wind_x, wind_y, residual, beside, above, below, inner, kept, *blocks,
        scratch=[pltpu.VMEM((levels, rows, cols), F32)] + wide_halo,
    )
    return call(
        functools.partial(final_body, parts), (like, like),
        residual, analysis, *smoothed(wide, thin, count), *blocks,
        in_specs=[VMEM] * (5 + parts), scratch=[pltpu.VMEM((count, rows, cols), F32)],
    )


def solution(mesh):
    return jax.shard_map(
        per_device,
        mesh=mesh,
        in_specs=(P(None, "tile", "member"), P("member", None, "tile", None), P(), P()),
        out_specs=(P(None, "tile", "member"), P(None, "tile", "member")),
        check_vma=False,
    )
```

profile of v0, /device:TPU:20, one launch (start us, length us, event | category | flops | bytes accessed | tf_op | source)
XLA Modules:
  0.0 111.3 jit_solution(10050435465988144186)
XLA Ops:
  0.6 1.0 copy-done.2
  2.0 3.5 %collective-permute-start = (f32[4,16,128]{2,1,0:T(8,128)S(1)}, f32[4,16,128]{2,1,0:T(8,128)S(1)}, u32[]{:S(2)}, u32[]{:S(2)}) collective-permute-start(f32[4,16,128]{2,1,0:T(8,128)S(1)} %get-tuple-element.42), channel_id=1, source_target_pairs={{0,1},{1,2},{2,3},{4,5},{5,6},{6,7},{8,9},{9,10},{10,11},{12,13},{... | collective-permute-start | bytes 98312 | tf_op jit(solution)/shard_map/ppermute | solution.py:131
  5.5 2.4 %collective-permute-start.1 = (f32[4,16,128]{2,1,0:T(8,128)S(1)}, f32[4,16,128]{2,1,0:T(8,128)S(1)}, u32[]{:S(2)}, u32[]{:S(2)}) collective-permute-start(f32[4,16,128]{2,1,0:T(8,128)S(1)} %get-tuple-element.43), channel_id=1, source_target_pairs={{1,0},{2,1},{3,2},{5,4},{6,5},{7,6},{9,8},{10,9},{11,10},{13,12},{... | collective-permute-start | bytes 98312 | tf_op jit(solution)/shard_map/ppermute | solution.py:131
  7.9 1.6 %copy-done = bf16[2,64,16,512]{3,2,1,0:T(8,128)(2,1)S(1)} copy-done((bf16[2,64,16,512]{3,2,1,0:T(8,128)(2,1)S(1)}, bf16[2,64,16,512]{3,2,1,0:T(8,128)(2,1)}, u32[]{:S(2)}) %copy-start) | copy-done | bytes 2097176
  9.8 1.5 %collective-permute-done.1.right_ref = f32[4,16,128]{2,1,0:T(8,128)S(1)} collective-permute-done((f32[4,16,128]{2,1,0:T(8,128)S(1)}, f32[4,16,128]{2,1,0:T(8,128)S(1)}, u32[]{:S(2)}, u32[]{:S(2)}) %collective-permute-start.1) | collective-permute-done | bytes 32800 | tf_op jit(solution)/shard_map/ppermute | solution.py:131
  11.5 1.7 %collective-permute-start.5 = (bf16[2,64,16,128]{3,2,1,0:T(8,128)(2,1)S(1)}, bf16[2,64,16,128]{3,2,1,0:T(8,128)(2,1)S(1)}, u32[]{:S(2)}, u32[]{:S(2)}) collective-permute-start(bf16[2,64,16,128]{3,2,1,0:T(8,128)(2,1)S(1)} %get-tuple-element.56), channel_id=1, source_target_pairs={{0,2},{1,3},{2,0},{3,1},{4,6},{5,7},{6,4},{7,5},{8,10},{9,11},{10,... | collective-permute-start | bytes 1572872 | tf_op jit(solution)/shard_map/ppermute | solution.py:456
  13.2 1.3 %collective-permute-start.6 = (bf16[2,64,16,128]{3,2,1,0:T(8,128)(2,1)S(1)}, bf16[2,64,16,128]{3,2,1,0:T(8,128)(2,1)S(1)}, u32[]{:S(2)}, u32[]{:S(2)}) collective-permute-start(bf16[2,64,16,128]{3,2,1,0:T(8,128)(2,1)S(1)} %get-tuple-element.57), channel_id=1, source_target_pairs={{0,3},{1,0},{2,1},{3,2},{4,7},{5,4},{6,5},{7,6},{8,11},{9,8},{10,9... | collective-permute-start | bytes 1572872 | tf_op jit(solution)/shard_map/ppermute | solution.py:456
  14.6 1.9 %collective-permute-start.2 = (f32[34,8,128]{2,1,0:T(8,128)S(1)}, f32[34,8,128]{2,1,0:T(8,128)S(1)}, u32[]{:S(2)}, u32[]{:S(2)}) collective-permute-start(f32[34,8,128]{2,1,0:T(8,128)S(1)} %get-tuple-element.48), channel_id=1, source_target_pairs={{0,4},{4,8},{8,12},{12,16},{16,20},{20,24},{24,28},{1,5},{5,9},{9,... | collective-permute-start | bytes 417800 | tf_op jit(solution)/shard_map/ppermute | solution.py:131
  16.5 4.5 %collective-permute-start.3 = (f32[34,8,128]{2,1,0:T(8,128)S(1)}, f32[34,8,128]{2,1,0:T(8,128)S(1)}, u32[]{:S(2)}, u32[]{:S(2)}) collective-permute-start(f32[34,8,128]{2,1,0:T(8,128)S(1)} %get-tuple-element.49), channel_id=1, source_target_pairs={{4,0},{8,4},{12,8},{16,12},{20,16},{24,20},{28,24},{5,1},{9,5},{13... | collective-permute-start | bytes 417800 | tf_op jit(solution)/shard_map/ppermute | solution.py:131
  21.1 3.4 %shard_map.63 = bf16[4,2,4,16,128]{4,3,2,1,0:T(8,128)(2,1)S(1)} custom-call(bf16[2,64,16,512]{3,2,1,0:T(8,128)(2,1)S(1)} %copy-done.1), custom_call_target="tpu_custom_call" | custom-call | tf_op jit(solution)/shard_map/pallas_call | solution.py:27
  24.7 4.8 %shard_map.62.grad_ref = f32[64,16,128]{2,1,0:T(8,128)S(1)} custom-call(f32[64,128]{1,0:T(8,128)S(1)} %broadcast_in_dim.4.wx_ref, f32[64,128]{1,0:T(8,128)S(1)} %broadcast_in_dim.5.wy_ref, f32[64,16,128]{2,1,0:T(8,128)S(1)} %copy-done.3, f32[4,16,128]{2,1,0:T(8,128)S(1)} %get-tuple-element.47.beside_ref.around_ref, ...), custom_call_target="tpu_custom_call" | custom-call | tf_op jit(solution)/shard_map/pallas_call | solution.py:27
  29.4 30.3 %all_to_all.5.refs_4_ = bf16[4,2,4,16,128]{4,3,2,1,0:T(8,128)(2,1)S(1)} all-to-all(bf16[4,2,4,16,128]{4,3,2,1,0:T(8,128)(2,1)S(1)} %shard_map.63), channel_id=1, replica_groups=mesh['tile'=8,'member'=4] {'member'}, dimensions={0} | all-to-all | bytes 262144 | tf_op jit(solution)/shard_map/all_to_all | solution.py:484
  59.7 0.6 shard_map.64
  60.4 3.0 %collective-permute-start.8 = (bf16[8,16,128]{2,1,0:T(8,128)(2,1)S(1)}, bf16[8,16,128]{2,1,0:T(8,128)(2,1)S(1)}, u32[]{:S(2)}, u32[]{:S(2)}) collective-permute-start(bf16[8,16,128]{2,1,0:T(8,128)(2,1)S(1)} %get-tuple-element.58), channel_id=1, source_target_pairs={{1,0},{2,1},{3,2},{5,4},{6,5},{7,6},{9,8},{10,9},{11,10},{13,12},{... | collective-permute-start | bytes 98312 | tf_op jit(solution)/shard_map/ppermute | solution.py:131
  63.3 2.9 %collective-permute-start.7 = (bf16[8,16,128]{2,1,0:T(8,128)(2,1)S(1)}, bf16[8,16,128]{2,1,0:T(8,128)(2,1)S(1)}, u32[]{:S(2)}, u32[]{:S(2)}) collective-permute-start(bf16[8,16,128]{2,1,0:T(8,128)(2,1)S(1)} %get-tuple-element.58), channel_id=1, source_target_pairs={{0,1},{1,2},{2,3},{4,5},{5,6},{6,7},{8,9},{9,10},{10,11},{12,13},{... | collective-permute-start | bytes 98312 | tf_op jit(solution)/shard_map/ppermute | solution.py:131
  66.2 3.0 %collective-permute-done.7.left_ref = bf16[8,16,128]{2,1,0:T(8,128)(2,1)S(1)} collective-permute-done((bf16[8,16,128]{2,1,0:T(8,128)(2,1)S(1)}, bf16[8,16,128]{2,1,0:T(8,128)(2,1)S(1)}, u32[]{:S(2)}, u32[]{:S(2)}) %collective-permute-start.7) | collective-permute-done | bytes 32800 | tf_op jit(solution)/shard_map/ppermute | solution.py:131
  69.2 0.4 shard_map.65
  69.6 1.9 %collective-permute-start.10 = (bf16[16,16,128]{2,1,0:T(8,128)(2,1)S(1)}, bf16[16,16,128]{2,1,0:T(8,128)(2,1)S(1)}, u32[]{:S(2)}, u32[]{:S(2)}) collective-permute-start(bf16[16,16,128]{2,1,0:T(8,128)(2,1)S(1)} %get-tuple-element.60), channel_id=1, source_target_pairs={{4,0},{8,4},{12,8},{16,12},{20,16},{24,20},{28,24},{5,1},{9,5},{13... | collective-permute-start | bytes 196616 | tf_op jit(solution)/shard_map/ppermute | solution.py:131
  71.5 2.4 %collective-permute-start.9 = (bf16[16,16,128]{2,1,0:T(8,128)(2,1)S(1)}, bf16[16,16,128]{2,1,0:T(8,128)(2,1)S(1)}, u32[]{:S(2)}, u32[]{:S(2)}) collective-permute-start(bf16[16,16,128]{2,1,0:T(8,128)(2,1)S(1)} %get-tuple-element.60), channel_id=1, source_target_pairs={{0,4},{4,8},{8,12},{12,16},{16,20},{20,24},{24,28},{1,5},{5,9},{9,... | collective-permute-start | bytes 196616 | tf_op jit(solution)/shard_map/ppermute | solution.py:131
  73.9 4.1 %collective-permute-done.9.above_ref = bf16[16,16,128]{2,1,0:T(8,128)(2,1)S(1)} collective-permute-done((bf16[16,16,128]{2,1,0:T(8,128)(2,1)S(1)}, bf16[16,16,128]{2,1,0:T(8,128)(2,1)S(1)}, u32[]{:S(2)}, u32[]{:S(2)}) %collective-permute-start.9) | collective-permute-done | bytes 65568 | tf_op jit(solution)/shard_map/ppermute | solution.py:131
  78.0 0.9 shard_map.66
  79.0 1.9 %collective-permute-start.11 = (bf16[17,16,128]{2,1,0:T(8,128)(2,1)S(1)}, bf16[17,16,128]{2,1,0:T(8,128)(2,1)S(1)}, u32[]{:S(2)}, u32[]{:S(2)}) collective-permute-start(bf16[17,16,128]{2,1,0:T(8,128)(2,1)S(1)} %get-tuple-element.66), channel_id=1, source_target_pairs={{0,4},{4,8},{8,12},{12,16},{16,20},{20,24},{24,28},{1,5},{5,9},{9,... | collective-permute-start | bytes 208904 | tf_op jit(solution)/shard_map/ppermute | solution.py:131
  80.9 4.5 %collective-permute-start.12 = (bf16[17,16,128]{2,1,0:T(8,128)(2,1)S(1)}, bf16[17,16,128]{2,1,0:T(8,128)(2,1)S(1)}, u32[]{:S(2)}, u32[]{:S(2)}) collective-permute-start(bf16[17,16,128]{2,1,0:T(8,128)(2,1)S(1)} %get-tuple-element.67), channel_id=1, source_target_pairs={{4,0},{8,4},{12,8},{16,12},{20,16},{24,20},{28,24},{5,1},{9,5},{13... | collective-permute-start | bytes 208904 | tf_op jit(solution)/shard_map/ppermute | solution.py:131
  85.4 2.5 %shard_map.67 = (f32[64,16,128]{2,1,0:T(8,128)S(1)}, f32[4,12,3,8,128]{4,3,2,1,0:T(8,128)S(1)}) custom-call(f32[64,128]{1,0:T(8,128)S(1)} %broadcast_in_dim.4.wx_ref, f32[64,128]{1,0:T(8,128)S(1)} %broadcast_in_dim.5.wy_ref, f32[64,16,128]{2,1,0:T(8,128)S(1)} %get-tuple-element.63.x_ref.residual_ref, f32[4,16,128]{2,1,0:T(8,128)S(1)} %get-tuple-element.65.beside_ref), custom_call_target="tpu_custom_call" | custom-call | tf_op jit(solution)/shard_map/pallas_call | solution.py:27
  88.0 2.8 %shard_map.68 = (f32[8,16,128]{2,1,0:T(8,128)S(1)}, bf16[8,16,128]{2,1,0:T(8,128)(2,1)S(1)}) custom-call(f32[64,128]{1,0:T(8,128)S(1)} %broadcast_in_dim.4.wx_ref, f32[64,128]{1,0:T(8,128)S(1)} %broadcast_in_dim.5.wy_ref, f32[64,16,128]{2,1,0:T(8,128)S(1)} %get-tuple-element.63.x_ref.residual_ref, f32[4,16,128]{2,1,0:T(8,128)S(1)} %get-tuple-element.65.beside_ref, ...), custom_call_target="tpu_custom_call" | custom-call | tf_op jit(solution)/shard_map/pallas_call | solution.py:27
  90.8 3.9 %collective-permute-start.14 = (bf16[8,16,128]{2,1,0:T(8,128)(2,1)S(1)}, bf16[8,16,128]{2,1,0:T(8,128)(2,1)S(1)}, u32[]{:S(2)}, u32[]{:S(2)}) collective-permute-start(bf16[8,16,128]{2,1,0:T(8,128)(2,1)S(1)} %get-tuple-element.70), channel_id=1, source_target_pairs={{1,0},{2,1},{3,2},{5,4},{6,5},{7,6},{9,8},{10,9},{11,10},{13,12},{... | collective-permute-start | bytes 98312 | tf_op jit(solution)/shard_map/ppermute | solution.py:131
  94.7 1.9 %collective-permute-start.13 = (bf16[8,16,128]{2,1,0:T(8,128)(2,1)S(1)}, bf16[8,16,128]{2,1,0:T(8,128)(2,1)S(1)}, u32[]{:S(2)}, u32[]{:S(2)}) collective-permute-start(bf16[8,16,128]{2,1,0:T(8,128)(2,1)S(1)} %get-tuple-element.70), channel_id=1, source_target_pairs={{0,1},{1,2},{2,3},{4,5},{5,6},{6,7},{8,9},{9,10},{10,11},{12,13},{... | collective-permute-start | bytes 98312 | tf_op jit(solution)/shard_map/ppermute | solution.py:131
  96.7 3.9 %collective-permute-done.13.left_ref = bf16[8,16,128]{2,1,0:T(8,128)(2,1)S(1)} collective-permute-done((bf16[8,16,128]{2,1,0:T(8,128)(2,1)S(1)}, bf16[8,16,128]{2,1,0:T(8,128)(2,1)S(1)}, u32[]{:S(2)}, u32[]{:S(2)}) %collective-permute-start.13) | collective-permute-done | bytes 32800 | tf_op jit(solution)/shard_map/ppermute | solution.py:131
  100.8 2.5 %collective-permute-start.16 = (bf16[8,16,128]{2,1,0:T(8,128)(2,1)S(1)}, bf16[8,16,128]{2,1,0:T(8,128)(2,1)S(1)}, u32[]{:S(2)}, u32[]{:S(2)}) collective-permute-start(bf16[8,16,128]{2,1,0:T(8,128)(2,1)S(1)} %get-tuple-element.72), channel_id=1, source_target_pairs={{4,0},{8,4},{12,8},{16,12},{20,16},{24,20},{28,24},{5,1},{9,5},{13... | collective-permute-start | bytes 98312 | tf_op jit(solution)/shard_map/ppermute | solution.py:131
  103.4 1.9 %collective-permute-start.15 = (bf16[8,16,128]{2,1,0:T(8,128)(2,1)S(1)}, bf16[8,16,128]{2,1,0:T(8,128)(2,1)S(1)}, u32[]{:S(2)}, u32[]{:S(2)}) collective-permute-start(bf16[8,16,128]{2,1,0:T(8,128)(2,1)S(1)} %get-tuple-element.72), channel_id=1, source_target_pairs={{0,4},{4,8},{8,12},{12,16},{16,20},{20,24},{24,28},{1,5},{5,9},{9,... | collective-permute-start | bytes 98312 | tf_op jit(solution)/shard_map/ppermute | solution.py:131
  105.3 4.2 %collective-permute-done.15.above_ref = bf16[8,16,128]{2,1,0:T(8,128)(2,1)S(1)} collective-permute-done((bf16[8,16,128]{2,1,0:T(8,128)(2,1)S(1)}, bf16[8,16,128]{2,1,0:T(8,128)(2,1)S(1)}, u32[]{:S(2)}, u32[]{:S(2)}) %collective-permute-start.15) | collective-permute-done | bytes 32800 | tf_op jit(solution)/shard_map/ppermute | solution.py:131
  109.5 1.8 %shard_map.70 = (f32[64,16,128]{2,1,0:T(8,128)}, f32[64,16,128]{2,1,0:T(8,128)}) custom-call(f32[64,16,128]{2,1,0:T(8,128)S(1)} %get-tuple-element.63.x_ref.residual_ref, f32[64,16,128]{2,1,0:T(8,128)S(1)} %get-tuple-element.64.before_ref, bf16[8,16,128]{2,1,0:T(8,128)(2,1)S(1)} %collective-permute-done.15.above_ref, ...), custom_call_target="tpu_custom_call" | custom-call | tf_op jit(solution)/shard_map/pallas_call | solution.py:27
  (29 shorter events, 1.4 us)
Async XLA Ops:
  0.6 1.0 copy-start.2
  1.7 12.9 %copy-start.3 = (f32[64,16,128]{2,1,0:T(8,128)S(1)}, f32[64,16,128]{2,1,0:T(8,128)}, u32[]{:S(2)}) copy-start(f32[64,16,128]{2,1,0:T(8,128)} %residual_ref.1) | copy-start | bytes 1572868
  2.0 7.8 %collective-permute-start = (f32[4,16,128]{2,1,0:T(8,128)S(1)}, f32[4,16,128]{2,1,0:T(8,128)S(1)}, u32[]{:S(2)}, u32[]{:S(2)}) collective-permute-start(f32[4,16,128]{2,1,0:T(8,128)S(1)} %get-tuple-element.42), channel_id=1, source_target_pairs={{0,1},{1,2},{2,3},{4,5},{5,6},{6,7},{8,9},{9,10},{10,11},{12,13},{... | collective-permute-start | bytes 98312 | tf_op jit(solution)/shard_map/ppermute | solution.py:131
  5.5 5.8 %collective-permute-start.1 = (f32[4,16,128]{2,1,0:T(8,128)S(1)}, f32[4,16,128]{2,1,0:T(8,128)S(1)}, u32[]{:S(2)}, u32[]{:S(2)}) collective-permute-start(f32[4,16,128]{2,1,0:T(8,128)S(1)} %get-tuple-element.43), channel_id=1, source_target_pairs={{1,0},{2,1},{3,2},{5,4},{6,5},{7,6},{9,8},{10,9},{11,10},{13,12},{... | collective-permute-start | bytes 98312 | tf_op jit(solution)/shard_map/ppermute | solution.py:131
  7.9 1.6 %copy-start = (bf16[2,64,16,512]{3,2,1,0:T(8,128)(2,1)S(1)}, bf16[2,64,16,512]{3,2,1,0:T(8,128)(2,1)}, u32[]{:S(2)}) copy-start(bf16[2,64,16,512]{3,2,1,0:T(8,128)(2,1)} %in_ref.2) | copy-start | bytes 6291460
  9.5 11.6 %copy-start.1 = (bf16[2,64,16,512]{3,2,1,0:T(8,128)(2,1)S(1)}, bf16[2,64,16,512]{3,2,1,0:T(8,128)(2,1)}, u32[]{:S(2)}) copy-start(bf16[2,64,16,512]{3,2,1,0:T(8,128)(2,1)} %in_ref.2) | copy-start | bytes 6291460
  9.5 15.1 %copy-start.4 = (f32[64]{0:T(128)S(1)}, f32[64]{0:T(128)}, u32[]{:S(2)}) copy-start(f32[64]{0:T(128)} %param.6) | copy-start | bytes 772
  9.5 15.1 %copy-start.5 = (f32[64]{0:T(128)S(1)}, f32[64]{0:T(128)}, u32[]{:S(2)}) copy-start(f32[64]{0:T(128)} %param.7) | copy-start | bytes 772
  11.3 48.4 %collective-permute-start.4 = (bf16[2,64,16,128]{3,2,1,0:T(8,128)(2,1)S(1)}, bf16[2,64,16,128]{3,2,1,0:T(8,128)(2,1)S(1)}, u32[]{:S(2)}, u32[]{:S(2)}) collective-permute-start(bf16[2,64,16,128]{3,2,1,0:T(8,128)(2,1)S(1)} %get-tuple-element.55), channel_id=1, source_target_pairs={{0,1},{1,2},{2,3},{3,0},{4,5},{5,6},{6,7},{7,4},{8,9},{9,10},{10,1... | collective-permute-start | bytes 1572872 | tf_op jit(solution)/shard_map/ppermute | solution.py:456
  11.5 48.2 %collective-permute-start.5 = (bf16[2,64,16,128]{3,2,1,0:T(8,128)(2,1)S(1)}, bf16[2,64,16,128]{3,2,1,0:T(8,128)(2,1)S(1)}, u32[]{:S(2)}, u32[]{:S(2)}) collective-permute-start(bf16[2,64,16,128]{3,2,1,0:T(8,128)(2,1)S(1)} %get-tuple-element.56), channel_id=1, source_target_pairs={{0,2},{1,3},{2,0},{3,1},{4,6},{5,7},{6,4},{7,5},{8,10},{9,11},{10,... | collective-permute-start | bytes 1572872 | tf_op jit(solution)/shard_map/ppermute | solution.py:456
  13.2 46.5 %collective-permute-start.6 = (bf16[2,64,16,128]{3,2,1,0:T(8,128)(2,1)S(1)}, bf16[2,64,16,128]{3,2,1,0:T(8,128)(2,1)S(1)}, u32[]{:S(2)}, u32[]{:S(2)}) collective-permute-start(bf16[2,64,16,128]{3,2,1,0:T(8,128)(2,1)S(1)} %get-tuple-element.57), channel_id=1, source_target_pairs={{0,3},{1,0},{2,1},{3,2},{4,7},{5,4},{6,5},{7,6},{8,11},{9,8},{10,9... | collective-permute-start | bytes 1572872 | tf_op jit(solution)/shard_map/ppermute | solution.py:456
  14.6 9.9 %collective-permute-start.2 = (f32[34,8,128]{2,1,0:T(8,128)S(1)}, f32[34,8,128]{2,1,0:T(8,128)S(1)}, u32[]{:S(2)}, u32[]{:S(2)}) collective-permute-start(f32[34,8,128]{2,1,0:T(8,128)S(1)} %get-tuple-element.48), channel_id=1, source_target_pairs={{0,4},{4,8},{8,12},{12,16},{16,20},{20,24},{24,28},{1,5},{5,9},{9,... | collective-permute-start | bytes 417800 | tf_op jit(solution)/shard_map/ppermute | solution.py:131
  16.5 8.0 %collective-permute-start.3 = (f32[34,8,128]{2,1,0:T(8,128)S(1)}, f32[34,8,128]{2,1,0:T(8,128)S(1)}, u32[]{:S(2)}, u32[]{:S(2)}) collective-permute-start(f32[34,8,128]{2,1,0:T(8,128)S(1)} %get-tuple-element.49), channel_id=1, source_target_pairs={{4,0},{8,4},{12,8},{16,12},{20,16},{24,20},{28,24},{5,1},{9,5},{13... | collective-permute-start | bytes 417800 | tf_op jit(solution)/shard_map/ppermute | solution.py:131
  60.4 5.9 %collective-permute-start.8 = (bf16[8,16,128]{2,1,0:T(8,128)(2,1)S(1)}, bf16[8,16,128]{2,1,0:T(8,128)(2,1)S(1)}, u32[]{:S(2)}, u32[]{:S(2)}) collective-permute-start(bf16[8,16,128]{2,1,0:T(8,128)(2,1)S(1)} %get-tuple-element.58), channel_id=1, source_target_pairs={{1,0},{2,1},{3,2},{5,4},{6,5},{7,6},{9,8},{10,9},{11,10},{13,12},{... | collective-permute-start | bytes 98312 | tf_op jit(solution)/shard_map/ppermute | solution.py:131
  63.3 5.9 %collective-permute-start.7 = (bf16[8,16,128]{2,1,0:T(8,128)(2,1)S(1)}, bf16[8,16,128]{2,1,0:T(8,128)(2,1)S(1)}, u32[]{:S(2)}, u32[]{:S(2)}) collective-permute-start(bf16[8,16,128]{2,1,0:T(8,128)(2,1)S(1)} %get-tuple-element.58), channel_id=1, source_target_pairs={{0,1},{1,2},{2,3},{4,5},{5,6},{6,7},{8,9},{9,10},{10,11},{12,13},{... | collective-permute-start | bytes 98312 | tf_op jit(solution)/shard_map/ppermute | solution.py:131
  69.6 4.3 %collective-permute-start.10 = (bf16[16,16,128]{2,1,0:T(8,128)(2,1)S(1)}, bf16[16,16,128]{2,1,0:T(8,128)(2,1)S(1)}, u32[]{:S(2)}, u32[]{:S(2)}) collective-permute-start(bf16[16,16,128]{2,1,0:T(8,128)(2,1)S(1)} %get-tuple-element.60), channel_id=1, source_target_pairs={{4,0},{8,4},{12,8},{16,12},{20,16},{24,20},{28,24},{5,1},{9,5},{13... | collective-permute-start | bytes 196616 | tf_op jit(solution)/shard_map/ppermute | solution.py:131
  71.5 6.5 %collective-permute-start.9 = (bf16[16,16,128]{2,1,0:T(8,128)(2,1)S(1)}, bf16[16,16,128]{2,1,0:T(8,128)(2,1)S(1)}, u32[]{:S(2)}, u32[]{:S(2)}) collective-permute-start(bf16[16,16,128]{2,1,0:T(8,128)(2,1)S(1)} %get-tuple-element.60), channel_id=1, source_target_pairs={{0,4},{4,8},{8,12},{12,16},{16,20},{20,24},{24,28},{1,5},{5,9},{9,... | collective-permute-start | bytes 196616 | tf_op jit(solution)/shard_map/ppermute | solution.py:131
  79.0 9.0 %collective-permute-start.11 = (bf16[17,16,128]{2,1,0:T(8,128)(2,1)S(1)}, bf16[17,16,128]{2,1,0:T(8,128)(2,1)S(1)}, u32[]{:S(2)}, u32[]{:S(2)}) collective-permute-start(bf16[17,16,128]{2,1,0:T(8,128)(2,1)S(1)} %get-tuple-element.66), channel_id=1, source_target_pairs={{0,4},{4,8},{8,12},{12,16},{16,20},{20,24},{24,28},{1,5},{5,9},{9,... | collective-permute-start | bytes 208904 | tf_op jit(solution)/shard_map/ppermute | solution.py:131
  80.9 7.1 %collective-permute-start.12 = (bf16[17,16,128]{2,1,0:T(8,128)(2,1)S(1)}, bf16[17,16,128]{2,1,0:T(8,128)(2,1)S(1)}, u32[]{:S(2)}, u32[]{:S(2)}) collective-permute-start(bf16[17,16,128]{2,1,0:T(8,128)(2,1)S(1)} %get-tuple-element.67), channel_id=1, source_target_pairs={{4,0},{8,4},{12,8},{16,12},{20,16},{24,20},{28,24},{5,1},{9,5},{13... | collective-permute-start | bytes 208904 | tf_op jit(solution)/shard_map/ppermute | solution.py:131
  90.8 5.9 %collective-permute-start.14 = (bf16[8,16,128]{2,1,0:T(8,128)(2,1)S(1)}, bf16[8,16,128]{2,1,0:T(8,128)(2,1)S(1)}, u32[]{:S(2)}, u32[]{:S(2)}) collective-permute-start(bf16[8,16,128]{2,1,0:T(8,128)(2,1)S(1)} %get-tuple-element.70), channel_id=1, source_target_pairs={{1,0},{2,1},{3,2},{5,4},{6,5},{7,6},{9,8},{10,9},{11,10},{13,12},{... | collective-permute-start | bytes 98312 | tf_op jit(solution)/shard_map/ppermute | solution.py:131
  94.7 5.8 %collective-permute-start.13 = (bf16[8,16,128]{2,1,0:T(8,128)(2,1)S(1)}, bf16[8,16,128]{2,1,0:T(8,128)(2,1)S(1)}, u32[]{:S(2)}, u32[]{:S(2)}) collective-permute-start(bf16[8,16,128]{2,1,0:T(8,128)(2,1)S(1)} %get-tuple-element.70), channel_id=1, source_target_pairs={{0,1},{1,2},{2,3},{4,5},{5,6},{6,7},{8,9},{9,10},{10,11},{12,13},{... | collective-permute-start | bytes 98312 | tf_op jit(solution)/shard_map/ppermute | solution.py:131
  100.8 4.5 %collective-permute-start.16 = (bf16[8,16,128]{2,1,0:T(8,128)(2,1)S(1)}, bf16[8,16,128]{2,1,0:T(8,128)(2,1)S(1)}, u32[]{:S(2)}, u32[]{:S(2)}) collective-permute-start(bf16[8,16,128]{2,1,0:T(8,128)(2,1)S(1)} %get-tuple-element.72), channel_id=1, source_target_pairs={{4,0},{8,4},{12,8},{16,12},{20,16},{24,20},{28,24},{5,1},{9,5},{13... | collective-permute-start | bytes 98312 | tf_op jit(solution)/shard_map/ppermute | solution.py:131
  103.4 6.1 %collective-permute-start.15 = (bf16[8,16,128]{2,1,0:T(8,128)(2,1)S(1)}, bf16[8,16,128]{2,1,0:T(8,128)(2,1)S(1)}, u32[]{:S(2)}, u32[]{:S(2)}) collective-permute-start(bf16[8,16,128]{2,1,0:T(8,128)(2,1)S(1)} %get-tuple-element.72), channel_id=1, source_target_pairs={{0,4},{4,8},{8,12},{12,16},{16,20},{20,24},{24,28},{1,5},{5,9},{9,... | collective-permute-start | bytes 98312 | tf_op jit(solution)/shard_map/ppermute | solution.py:131
where the time goes:
time: 112 us; the launch traced here: 111 us
  starting transfers between devices  42.5 us (38%)
  blocking collectives  30.3 us (27%)
  Pallas kernels  18.3 us (16%)
  waiting for transfers between devices  16.6 us (15%)
  local copies, waits for them, and re-layouts  2.78 us (2%)
    ppermute x14, starting transfers between devices, shift(): return lax.ppermute(x, axis, pairs)  39.2 us
    all_to_all x1, blocking collectives, per_device(): lax.all_to_all(sides, 'member', split_axis=0, concat_axis=0, tiled=True)  30.3 us
    pallas_call x12, Pallas kernels, call(): pl.pallas_call(body, out_shape=out_shape, in_specs=in_specs or [VMEM] * l...  18.3 us
    ppermute x14, waiting for transfers between devices, shift(): return lax.ppermute(x, axis, pairs)  16.6 us
    ppermute x3, starting transfers between devices, turned(): lax.ppermute(x, 'member', [(i, (i + step) % parts) for i in range(parts)])  3.26 us
    unnamed x12, local copies, waits for them, and re-layouts  2.64 us
  transfers between devices with their start and end apart: 17, of which 5 were waited for; matrix products, arithmetic and copies ran while one was open for 0% of the time, Pallas kernels for 10%

commit v1 on v0

--- a/solution.py
+++ b/solution.py
@@ -468,10 +468,13 @@
     packed = shape(groups, rows, LANES)
     wind_x, wind_y = (jnp.broadcast_to(w[:, None], (levels, LANES)) for w in (wind_x, wind_y))
 
+    blocks = list(split_columns(members, parts))
+    blocks[1], residual_in = lax.optimization_barrier((blocks[1], residual_in))
+    early = turned(blocks[1], 1)
     first, last = call(columns_edge_body, (packed, packed), residual_in)
     left, right = shift(last, "member", 1), shift(first, "member", -1)
-    blocks, left, right = lax.optimization_barrier((split_columns(members, parts), left, right))
-    blocks = [turned(x, r) if r else x for r, x in enumerate(blocks)]
+    blocks, early, left, right = lax.optimization_barrier((blocks, early, left, right))
+    blocks = [early if r == 1 else turned(x, r) if r else x for r, x in enumerate(blocks)]
     around, top, bottom = call(rows_body, (packed, halo, halo), residual_in, left, right)
     members, around = lax.optimization_barrier((members, around))
     sides = side_columns(members, parts)

time: 112 us -> 109 us (0.973)
  blocking collectives: 30.3 us -> 21 us
  waiting for transfers between devices: 16.6 us -> 21.5 us
  starting transfers between devices: 42.5 us -> 43.9 us
    all_to_all x1, blocking collectives: 30.3 us -> 21 us  [per_device(): lax.all_to_all(sides, 'member', split_axis=0, concat_axis=0, tiled=True)]
    ppermute x14, waiting for transfers between devices: 16.6 us -> 21.5 us  [shift(): return lax.ppermute(x, axis, pairs)]
    ppermute x3, starting transfers between devices: 3.26 us -> 4.67 us  [turned(): lax.ppermute(x, 'member', [(i, (i + step) % parts) for i in range(parts)])]
where the time goes in v1:
time: 109 us; the launch traced here: 108 us
  starting transfers between devices  43.9 us (40%)
  waiting for transfers between devices  21.5 us (20%)
  blocking collectives  21 us (19%)
  Pallas kernels  18.3 us (17%)
  local copies, waits for them, and re-layouts  2.79 us (3%)
    ppermute x14, starting transfers between devices, shift(): return lax.ppermute(x, axis, pairs)  39.2 us
    ppermute x14, waiting for transfers between devices, shift(): return lax.ppermute(x, axis, pairs)  21.5 us
    all_to_all x1, blocking collectives, per_device(): lax.all_to_all(sides, 'member', split_axis=0, concat_axis=0, tiled=True)  21 us
    pallas_call x12, Pallas kernels, call(): pl.pallas_call(body, out_shape=out_shape, in_specs=in_specs or [VMEM] * l...  18.3 us
    ppermute x3, starting transfers between devices, turned(): lax.ppermute(x, 'member', [(i, (i + step) % parts) for i in range(parts)])  4.67 us
    unnamed x12, local copies, waits for them, and re-layouts  2.65 us
  transfers between devices with their start and end apart: 17, of which 5 were waited for; matrix products, arithmetic and copies ran while one was open for 0% of the time, Pallas kernels for 10%

profile of v1, /device:TPU:20, one launch (start us, length us, event | category | flops | bytes accessed | tf_op | source)
XLA Modules:
  0.0 108.3 jit_solution(10334013308942792389)
XLA Ops:
  0.6 1.6 %copy-done = bf16[2,64,16,512]{3,2,1,0:T(8,128)(2,1)S(1)} copy-done((bf16[2,64,16,512]{3,2,1,0:T(8,128)(2,1)S(1)}, bf16[2,64,16,512]{3,2,1,0:T(8,128)(2,1)}, u32[]{:S(2)}) %copy-start) | copy-done | bytes 2097176
  2.6 1.6 %collective-permute-start = (bf16[2,64,16,128]{3,2,1,0:T(8,128)(2,1)S(1)}, bf16[2,64,16,128]{3,2,1,0:T(8,128)(2,1)S(1)}, u32[]{:S(2)}, u32[]{:S(2)}) collective-permute-start(bf16[2,64,16,128]{3,2,1,0:T(8,128)(2,1)S(1)} %get-tuple-element.43), channel_id=1, source_target_pairs={{0,1},{1,2},{2,3},{3,0},{4,5},{5,6},{6,7},{7,4},{8,9},{9,10},{10,1... | collective-permute-start | bytes 1572872 | tf_op jit(solution)/shard_map/ppermute | solution.py:456
  4.2 1.0 copy-done.2
  5.6 2.1 %collective-permute-start.1 = (f32[4,16,128]{2,1,0:T(8,128)S(1)}, f32[4,16,128]{2,1,0:T(8,128)S(1)}, u32[]{:S(2)}, u32[]{:S(2)}) collective-permute-start(f32[4,16,128]{2,1,0:T(8,128)S(1)} %get-tuple-element.46), channel_id=1, source_target_pairs={{0,1},{1,2},{2,3},{4,5},{5,6},{6,7},{8,9},{9,10},{10,11},{12,13},{... | collective-permute-start | bytes 98312 | tf_op jit(solution)/shard_map/ppermute | solution.py:131
  7.8 3.7 %collective-permute-start.2 = (f32[4,16,128]{2,1,0:T(8,128)S(1)}, f32[4,16,128]{2,1,0:T(8,128)S(1)}, u32[]{:S(2)}, u32[]{:S(2)}) collective-permute-start(f32[4,16,128]{2,1,0:T(8,128)S(1)} %get-tuple-element.47), channel_id=1, source_target_pairs={{1,0},{2,1},{3,2},{5,4},{6,5},{7,6},{9,8},{10,9},{11,10},{13,12},{... | collective-permute-start | bytes 98312 | tf_op jit(solution)/shard_map/ppermute | solution.py:131
  11.5 5.6 %collective-permute-done.1.left_ref = f32[4,16,128]{2,1,0:T(8,128)S(1)} collective-permute-done((f32[4,16,128]{2,1,0:T(8,128)S(1)}, f32[4,16,128]{2,1,0:T(8,128)S(1)}, u32[]{:S(2)}, u32[]{:S(2)}) %collective-permute-start.1) | collective-permute-done | bytes 32800 | tf_op jit(solution)/shard_map/ppermute | solution.py:131
  17.0 2.2 %collective-permute-start.5 = (bf16[2,64,16,128]{3,2,1,0:T(8,128)(2,1)S(1)}, bf16[2,64,16,128]{3,2,1,0:T(8,128)(2,1)S(1)}, u32[]{:S(2)}, u32[]{:S(2)}) collective-permute-start(bf16[2,64,16,128]{3,2,1,0:T(8,128)(2,1)S(1)} %get-tuple-element.60), channel_id=1, source_target_pairs={{0,2},{1,3},{2,0},{3,1},{4,6},{5,7},{6,4},{7,5},{8,10},{9,11},{10,... | collective-permute-start | bytes 1572872 | tf_op jit(solution)/shard_map/ppermute | solution.py:456
  19.2 0.8 collective-permute-start.6
  20.1 1.9 %collective-permute-start.3 = (f32[34,8,128]{2,1,0:T(8,128)S(1)}, f32[34,8,128]{2,1,0:T(8,128)S(1)}, u32[]{:S(2)}, u32[]{:S(2)}) collective-permute-start(f32[34,8,128]{2,1,0:T(8,128)S(1)} %get-tuple-element.52), channel_id=1, source_target_pairs={{0,4},{4,8},{8,12},{12,16},{16,20},{20,24},{24,28},{1,5},{5,9},{9,... | collective-permute-start | bytes 417800 | tf_op jit(solution)/shard_map/ppermute | solution.py:131
  22.0 4.5 %collective-permute-start.4 = (f32[34,8,128]{2,1,0:T(8,128)S(1)}, f32[34,8,128]{2,1,0:T(8,128)S(1)}, u32[]{:S(2)}, u32[]{:S(2)}) collective-permute-start(f32[34,8,128]{2,1,0:T(8,128)S(1)} %get-tuple-element.53), channel_id=1, source_target_pairs={{4,0},{8,4},{12,8},{16,12},{20,16},{24,20},{28,24},{5,1},{9,5},{13... | collective-permute-start | bytes 417800 | tf_op jit(solution)/shard_map/ppermute | solution.py:131
  26.6 3.4 %shard_map.63 = bf16[4,2,4,16,128]{4,3,2,1,0:T(8,128)(2,1)S(1)} custom-call(bf16[2,64,16,512]{3,2,1,0:T(8,128)(2,1)S(1)} %copy-done.1), custom_call_target="tpu_custom_call" | custom-call | tf_op jit(solution)/shard_map/pallas_call | solution.py:27
  30.2 4.8 %shard_map.62.grad_ref = f32[64,16,128]{2,1,0:T(8,128)S(1)} custom-call(f32[64,128]{1,0:T(8,128)S(1)} %broadcast_in_dim.4.wx_ref, f32[64,128]{1,0:T(8,128)S(1)} %broadcast_in_dim.5.wy_ref, f32[64,16,128]{2,1,0:T(8,128)S(1)} %copy-done.2, f32[4,16,128]{2,1,0:T(8,128)S(1)} %get-tuple-element.51.beside_ref.around_ref, ...), custom_call_target="tpu_custom_call" | custom-call | tf_op jit(solution)/shard_map/pallas_call | solution.py:27
  34.9 21.0 %all_to_all.5.refs_4_ = bf16[4,2,4,16,128]{4,3,2,1,0:T(8,128)(2,1)S(1)} all-to-all(bf16[4,2,4,16,128]{4,3,2,1,0:T(8,128)(2,1)S(1)} %shard_map.63), channel_id=1, replica_groups=mesh['tile'=8,'member'=4] {'member'}, dimensions={0} | all-to-all | bytes 262144 | tf_op jit(solution)/shard_map/all_to_all | solution.py:487
  55.9 0.6 shard_map.64
  56.6 3.8 %collective-permute-start.8 = (bf16[8,16,128]{2,1,0:T(8,128)(2,1)S(1)}, bf16[8,16,128]{2,1,0:T(8,128)(2,1)S(1)}, u32[]{:S(2)}, u32[]{:S(2)}) collective-permute-start(bf16[8,16,128]{2,1,0:T(8,128)(2,1)S(1)} %get-tuple-element.62), channel_id=1, source_target_pairs={{1,0},{2,1},{3,2},{5,4},{6,5},{7,6},{9,8},{10,9},{11,10},{13,12},{... | collective-permute-start | bytes 98312 | tf_op jit(solution)/shard_map/ppermute | solution.py:131
  60.4 2.0 %collective-permute-start.7 = (bf16[8,16,128]{2,1,0:T(8,128)(2,1)S(1)}, bf16[8,16,128]{2,1,0:T(8,128)(2,1)S(1)}, u32[]{:S(2)}, u32[]{:S(2)}) collective-permute-start(bf16[8,16,128]{2,1,0:T(8,128)(2,1)S(1)} %get-tuple-element.62), channel_id=1, source_target_pairs={{0,1},{1,2},{2,3},{4,5},{5,6},{6,7},{8,9},{9,10},{10,11},{12,13},{... | collective-permute-start | bytes 98312 | tf_op jit(solution)/shard_map/ppermute | solution.py:131
  62.4 3.8 %collective-permute-done.7.left_ref = bf16[8,16,128]{2,1,0:T(8,128)(2,1)S(1)} collective-permute-done((bf16[8,16,128]{2,1,0:T(8,128)(2,1)S(1)}, bf16[8,16,128]{2,1,0:T(8,128)(2,1)S(1)}, u32[]{:S(2)}, u32[]{:S(2)}) %collective-permute-start.7) | collective-permute-done | bytes 32800 | tf_op jit(solution)/shard_map/ppermute | solution.py:131
  66.6 1.9 %collective-permute-start.10 = (bf16[16,16,128]{2,1,0:T(8,128)(2,1)S(1)}, bf16[16,16,128]{2,1,0:T(8,128)(2,1)S(1)}, u32[]{:S(2)}, u32[]{:S(2)}) collective-permute-start(bf16[16,16,128]{2,1,0:T(8,128)(2,1)S(1)} %get-tuple-element.64), channel_id=1, source_target_pairs={{4,0},{8,4},{12,8},{16,12},{20,16},{24,20},{28,24},{5,1},{9,5},{13... | collective-permute-start | bytes 196616 | tf_op jit(solution)/shard_map/ppermute | solution.py:131
  68.5 2.4 %collective-permute-start.9 = (bf16[16,16,128]{2,1,0:T(8,128)(2,1)S(1)}, bf16[16,16,128]{2,1,0:T(8,128)(2,1)S(1)}, u32[]{:S(2)}, u32[]{:S(2)}) collective-permute-start(bf16[16,16,128]{2,1,0:T(8,128)(2,1)S(1)} %get-tuple-element.64), channel_id=1, source_target_pairs={{0,4},{4,8},{8,12},{12,16},{16,20},{20,24},{24,28},{1,5},{5,9},{9,... | collective-permute-start | bytes 196616 | tf_op jit(solution)/shard_map/ppermute | solution.py:131
  70.9 4.1 %collective-permute-done.9.above_ref = bf16[16,16,128]{2,1,0:T(8,128)(2,1)S(1)} collective-permute-done((bf16[16,16,128]{2,1,0:T(8,128)(2,1)S(1)}, bf16[16,16,128]{2,1,0:T(8,128)(2,1)S(1)}, u32[]{:S(2)}, u32[]{:S(2)}) %collective-permute-start.9) | collective-permute-done | bytes 65568 | tf_op jit(solution)/shard_map/ppermute | solution.py:131
  75.0 0.9 shard_map.66
  76.0 1.9 %collective-permute-start.11 = (bf16[17,16,128]{2,1,0:T(8,128)(2,1)S(1)}, bf16[17,16,128]{2,1,0:T(8,128)(2,1)S(1)}, u32[]{:S(2)}, u32[]{:S(2)}) collective-permute-start(bf16[17,16,128]{2,1,0:T(8,128)(2,1)S(1)} %get-tuple-element.70), channel_id=1, source_target_pairs={{0,4},{4,8},{8,12},{12,16},{16,20},{20,24},{24,28},{1,5},{5,9},{9,... | collective-permute-start | bytes 208904 | tf_op jit(solution)/shard_map/ppermute | solution.py:131
  77.9 4.5 %collective-permute-start.12 = (bf16[17,16,128]{2,1,0:T(8,128)(2,1)S(1)}, bf16[17,16,128]{2,1,0:T(8,128)(2,1)S(1)}, u32[]{:S(2)}, u32[]{:S(2)}) collective-permute-start(bf16[17,16,128]{2,1,0:T(8,128)(2,1)S(1)} %get-tuple-element.71), channel_id=1, source_target_pairs={{4,0},{8,4},{12,8},{16,12},{20,16},{24,20},{28,24},{5,1},{9,5},{13... | collective-permute-start | bytes 208904 | tf_op jit(solution)/shard_map/ppermute | solution.py:131
  82.4 2.5 %shard_map.67 = (f32[64,16,128]{2,1,0:T(8,128)S(1)}, f32[4,12,3,8,128]{4,3,2,1,0:T(8,128)S(1)}) custom-call(f32[64,128]{1,0:T(8,128)S(1)} %broadcast_in_dim.4.wx_ref, f32[64,128]{1,0:T(8,128)S(1)} %broadcast_in_dim.5.wy_ref, f32[64,16,128]{2,1,0:T(8,128)S(1)} %get-tuple-element.67.x_ref.residual_ref, f32[4,16,128]{2,1,0:T(8,128)S(1)} %get-tuple-element.69.beside_ref), custom_call_target="tpu_custom_call" | custom-call | tf_op jit(solution)/shard_map/pallas_call | solution.py:27
  85.0 2.8 %shard_map.68 = (f32[8,16,128]{2,1,0:T(8,128)S(1)}, bf16[8,16,128]{2,1,0:T(8,128)(2,1)S(1)}) custom-call(f32[64,128]{1,0:T(8,128)S(1)} %broadcast_in_dim.4.wx_ref, f32[64,128]{1,0:T(8,128)S(1)} %broadcast_in_dim.5.wy_ref, f32[64,16,128]{2,1,0:T(8,128)S(1)} %get-tuple-element.67.x_ref.residual_ref, f32[4,16,128]{2,1,0:T(8,128)S(1)} %get-tuple-element.69.beside_ref, ...), custom_call_target="tpu_custom_call" | custom-call | tf_op jit(solution)/shard_map/pallas_call | solution.py:27
  87.8 3.9 %collective-permute-start.14 = (bf16[8,16,128]{2,1,0:T(8,128)(2,1)S(1)}, bf16[8,16,128]{2,1,0:T(8,128)(2,1)S(1)}, u32[]{:S(2)}, u32[]{:S(2)}) collective-permute-start(bf16[8,16,128]{2,1,0:T(8,128)(2,1)S(1)} %get-tuple-element.74), channel_id=1, source_target_pairs={{1,0},{2,1},{3,2},{5,4},{6,5},{7,6},{9,8},{10,9},{11,10},{13,12},{... | collective-permute-start | bytes 98312 | tf_op jit(solution)/shard_map/ppermute | solution.py:131
  91.7 1.9 %collective-permute-start.13 = (bf16[8,16,128]{2,1,0:T(8,128)(2,1)S(1)}, bf16[8,16,128]{2,1,0:T(8,128)(2,1)S(1)}, u32[]{:S(2)}, u32[]{:S(2)}) collective-permute-start(bf16[8,16,128]{2,1,0:T(8,128)(2,1)S(1)} %get-tuple-element.74), channel_id=1, source_target_pairs={{0,1},{1,2},{2,3},{4,5},{5,6},{6,7},{8,9},{9,10},{10,11},{12,13},{... | collective-permute-start | bytes 98312 | tf_op jit(solution)/shard_map/ppermute | solution.py:131
  93.7 3.9 %collective-permute-done.13.left_ref = bf16[8,16,128]{2,1,0:T(8,128)(2,1)S(1)} collective-permute-done((bf16[8,16,128]{2,1,0:T(8,128)(2,1)S(1)}, bf16[8,16,128]{2,1,0:T(8,128)(2,1)S(1)}, u32[]{:S(2)}, u32[]{:S(2)}) %collective-permute-start.13) | collective-permute-done | bytes 32800 | tf_op jit(solution)/shard_map/ppermute | solution.py:131
  97.8 2.5 %collective-permute-start.16 = (bf16[8,16,128]{2,1,0:T(8,128)(2,1)S(1)}, bf16[8,16,128]{2,1,0:T(8,128)(2,1)S(1)}, u32[]{:S(2)}, u32[]{:S(2)}) collective-permute-start(bf16[8,16,128]{2,1,0:T(8,128)(2,1)S(1)} %get-tuple-element.76), channel_id=1, source_target_pairs={{4,0},{8,4},{12,8},{16,12},{20,16},{24,20},{28,24},{5,1},{9,5},{13... | collective-permute-start | bytes 98312 | tf_op jit(solution)/shard_map/ppermute | solution.py:131
  100.3 1.9 %collective-permute-start.15 = (bf16[8,16,128]{2,1,0:T(8,128)(2,1)S(1)}, bf16[8,16,128]{2,1,0:T(8,128)(2,1)S(1)}, u32[]{:S(2)}, u32[]{:S(2)}) collective-permute-start(bf16[8,16,128]{2,1,0:T(8,128)(2,1)S(1)} %get-tuple-element.76), channel_id=1, source_target_pairs={{0,4},{4,8},{8,12},{12,16},{16,20},{20,24},{24,28},{1,5},{5,9},{9,... | collective-permute-start | bytes 98312 | tf_op jit(solution)/shard_map/ppermute | solution.py:131
  102.3 4.2 %collective-permute-done.15.above_ref = bf16[8,16,128]{2,1,0:T(8,128)(2,1)S(1)} collective-permute-done((bf16[8,16,128]{2,1,0:T(8,128)(2,1)S(1)}, bf16[8,16,128]{2,1,0:T(8,128)(2,1)S(1)}, u32[]{:S(2)}, u32[]{:S(2)}) %collective-permute-start.15) | collective-permute-done | bytes 32800 | tf_op jit(solution)/shard_map/ppermute | solution.py:131
  106.5 1.8 %shard_map.70 = (f32[64,16,128]{2,1,0:T(8,128)}, f32[64,16,128]{2,1,0:T(8,128)}) custom-call(f32[64,16,128]{2,1,0:T(8,128)S(1)} %get-tuple-element.67.x_ref.residual_ref, f32[64,16,128]{2,1,0:T(8,128)S(1)} %get-tuple-element.68.before_ref, bf16[8,16,128]{2,1,0:T(8,128)(2,1)S(1)} %collective-permute-done.15.above_ref, ...), custom_call_target="tpu_custom_call" | custom-call | tf_op jit(solution)/shard_map/pallas_call | solution.py:27
  (29 shorter events, 1.6 us)
Async XLA Ops:
  0.6 1.6 %copy-start = (bf16[2,64,16,512]{3,2,1,0:T(8,128)(2,1)S(1)}, bf16[2,64,16,512]{3,2,1,0:T(8,128)(2,1)}, u32[]{:S(2)}) copy-start(bf16[2,64,16,512]{3,2,1,0:T(8,128)(2,1)} %in_ref.2) | copy-start | bytes 6291460
  2.2 24.4 %copy-start.1 = (bf16[2,64,16,512]{3,2,1,0:T(8,128)(2,1)S(1)}, bf16[2,64,16,512]{3,2,1,0:T(8,128)(2,1)}, u32[]{:S(2)}) copy-start(bf16[2,64,16,512]{3,2,1,0:T(8,128)(2,1)} %in_ref.2) | copy-start | bytes 6291460
  2.6 27.4 %copy-start.4 = (f32[64]{0:T(128)S(1)}, f32[64]{0:T(128)}, u32[]{:S(2)}) copy-start(f32[64]{0:T(128)} %param.6) | copy-start | bytes 772
  2.6 27.5 %copy-start.5 = (f32[64]{0:T(128)S(1)}, f32[64]{0:T(128)}, u32[]{:S(2)}) copy-start(f32[64]{0:T(128)} %param.7) | copy-start | bytes 772
  2.6 14.4 %collective-permute-start = (bf16[2,64,16,128]{3,2,1,0:T(8,128)(2,1)S(1)}, bf16[2,64,16,128]{3,2,1,0:T(8,128)(2,1)S(1)}, u32[]{:S(2)}, u32[]{:S(2)}) collective-permute-start(bf16[2,64,16,128]{3,2,1,0:T(8,128)(2,1)S(1)} %get-tuple-element.43), channel_id=1, source_target_pairs={{0,1},{1,2},{2,3},{3,0},{4,5},{5,6},{6,7},{7,4},{8,9},{9,10},{10,1... | collective-permute-start | bytes 1572872 | tf_op jit(solution)/shard_map/ppermute | solution.py:456
  4.2 1.0 copy-start.2
  5.6 11.4 %collective-permute-start.1 = (f32[4,16,128]{2,1,0:T(8,128)S(1)}, f32[4,16,128]{2,1,0:T(8,128)S(1)}, u32[]{:S(2)}, u32[]{:S(2)}) collective-permute-start(f32[4,16,128]{2,1,0:T(8,128)S(1)} %get-tuple-element.46), channel_id=1, source_target_pairs={{0,1},{1,2},{2,3},{4,5},{5,6},{6,7},{8,9},{9,10},{10,11},{12,13},{... | collective-permute-start | bytes 98312 | tf_op jit(solution)/shard_map/ppermute | solution.py:131
  7.8 9.3 %collective-permute-start.2 = (f32[4,16,128]{2,1,0:T(8,128)S(1)}, f32[4,16,128]{2,1,0:T(8,128)S(1)}, u32[]{:S(2)}, u32[]{:S(2)}) collective-permute-start(f32[4,16,128]{2,1,0:T(8,128)S(1)} %get-tuple-element.47), channel_id=1, source_target_pairs={{1,0},{2,1},{3,2},{5,4},{6,5},{7,6},{9,8},{10,9},{11,10},{13,12},{... | collective-permute-start | bytes 98312 | tf_op jit(solution)/shard_map/ppermute | solution.py:131
  17.0 38.9 %collective-permute-start.5 = (bf16[2,64,16,128]{3,2,1,0:T(8,128)(2,1)S(1)}, bf16[2,64,16,128]{3,2,1,0:T(8,128)(2,1)S(1)}, u32[]{:S(2)}, u32[]{:S(2)}) collective-permute-start(bf16[2,64,16,128]{3,2,1,0:T(8,128)(2,1)S(1)} %get-tuple-element.60), channel_id=1, source_target_pairs={{0,2},{1,3},{2,0},{3,1},{4,6},{5,7},{6,4},{7,5},{8,10},{9,11},{10,... | collective-permute-start | bytes 1572872 | tf_op jit(solution)/shard_map/ppermute | solution.py:456
  19.2 36.7 %collective-permute-start.6 = (bf16[2,64,16,128]{3,2,1,0:T(8,128)(2,1)S(1)}, bf16[2,64,16,128]{3,2,1,0:T(8,128)(2,1)S(1)}, u32[]{:S(2)}, u32[]{:S(2)}) collective-permute-start(bf16[2,64,16,128]{3,2,1,0:T(8,128)(2,1)S(1)} %get-tuple-element.61), channel_id=1, source_target_pairs={{0,3},{1,0},{2,1},{3,2},{4,7},{5,4},{6,5},{7,6},{8,11},{9,8},{10,9... | collective-permute-start | bytes 1572872 | tf_op jit(solution)/shard_map/ppermute | solution.py:456
  20.1 9.9 %collective-permute-start.3 = (f32[34,8,128]{2,1,0:T(8,128)S(1)}, f32[34,8,128]{2,1,0:T(8,128)S(1)}, u32[]{:S(2)}, u32[]{:S(2)}) collective-permute-start(f32[34,8,128]{2,1,0:T(8,128)S(1)} %get-tuple-element.52), channel_id=1, source_target_pairs={{0,4},{4,8},{8,12},{12,16},{16,20},{20,24},{24,28},{1,5},{5,9},{9,... | collective-permute-start | bytes 417800 | tf_op jit(solution)/shard_map/ppermute | solution.py:131
  22.0 8.0 %collective-permute-start.4 = (f32[34,8,128]{2,1,0:T(8,128)S(1)}, f32[34,8,128]{2,1,0:T(8,128)S(1)}, u32[]{:S(2)}, u32[]{:S(2)}) collective-permute-start(f32[34,8,128]{2,1,0:T(8,128)S(1)} %get-tuple-element.53), channel_id=1, source_target_pairs={{4,0},{8,4},{12,8},{16,12},{20,16},{24,20},{28,24},{5,1},{9,5},{13... | collective-permute-start | bytes 417800 | tf_op jit(solution)/shard_map/ppermute | solution.py:131
  30.2 44.8 %copy-start.3 = (f32[64,16,128]{2,1,0:T(8,128)S(1)}, f32[64,16,128]{2,1,0:T(8,128)}, u32[]{:S(2)}) copy-start(f32[64,16,128]{2,1,0:T(8,128)} %residual_ref) | copy-start | bytes 1572868
  56.6 5.9 %collective-permute-start.8 = (bf16[8,16,128]{2,1,0:T(8,128)(2,1)S(1)}, bf16[8,16,128]{2,1,0:T(8,128)(2,1)S(1)}, u32[]{:S(2)}, u32[]{:S(2)}) collective-permute-start(bf16[8,16,128]{2,1,0:T(8,128)(2,1)S(1)} %get-tuple-element.62), channel_id=1, source_target_pairs={{1,0},{2,1},{3,2},{5,4},{6,5},{7,6},{9,8},{10,9},{11,10},{13,12},{... | collective-permute-start | bytes 98312 | tf_op jit(solution)/shard_map/ppermute | solution.py:131
  60.4 5.8 %collective-permute-start.7 = (bf16[8,16,128]{2,1,0:T(8,128)(2,1)S(1)}, bf16[8,16,128]{2,1,0:T(8,128)(2,1)S(1)}, u32[]{:S(2)}, u32[]{:S(2)}) collective-permute-start(bf16[8,16,128]{2,1,0:T(8,128)(2,1)S(1)} %get-tuple-element.62), channel_id=1, source_target_pairs={{0,1},{1,2},{2,3},{4,5},{5,6},{6,7},{8,9},{9,10},{10,11},{12,13},{... | collective-permute-start | bytes 98312 | tf_op jit(solution)/shard_map/ppermute | solution.py:131
  66.6 4.3 %collective-permute-start.10 = (bf16[16,16,128]{2,1,0:T(8,128)(2,1)S(1)}, bf16[16,16,128]{2,1,0:T(8,128)(2,1)S(1)}, u32[]{:S(2)}, u32[]{:S(2)}) collective-permute-start(bf16[16,16,128]{2,1,0:T(8,128)(2,1)S(1)} %get-tuple-element.64), channel_id=1, source_target_pairs={{4,0},{8,4},{12,8},{16,12},{20,16},{24,20},{28,24},{5,1},{9,5},{13... | collective-permute-start | bytes 196616 | tf_op jit(solution)/shard_map/ppermute | solution.py:131
  68.5 6.5 %collective-permute-start.9 = (bf16[16,16,128]{2,1,0:T(8,128)(2,1)S(1)}, bf16[16,16,128]{2,1,0:T(8,128)(2,1)S(1)}, u32[]{:S(2)}, u32[]{:S(2)}) collective-permute-start(bf16[16,16,128]{2,1,0:T(8,128)(2,1)S(1)} %get-tuple-element.64), channel_id=1, source_target_pairs={{0,4},{4,8},{8,12},{12,16},{16,20},{20,24},{24,28},{1,5},{5,9},{9,... | collective-permute-start | bytes 196616 | tf_op jit(solution)/shard_map/ppermute | solution.py:131
  76.0 9.0 %collective-permute-start.11 = (bf16[17,16,128]{2,1,0:T(8,128)(2,1)S(1)}, bf16[17,16,128]{2,1,0:T(8,128)(2,1)S(1)}, u32[]{:S(2)}, u32[]{:S(2)}) collective-permute-start(bf16[17,16,128]{2,1,0:T(8,128)(2,1)S(1)} %get-tuple-element.70), channel_id=1, source_target_pairs={{0,4},{4,8},{8,12},{12,16},{16,20},{20,24},{24,28},{1,5},{5,9},{9,... | collective-permute-start | bytes 208904 | tf_op jit(solution)/shard_map/ppermute | solution.py:131
  77.9 7.1 %collective-permute-start.12 = (bf16[17,16,128]{2,1,0:T(8,128)(2,1)S(1)}, bf16[17,16,128]{2,1,0:T(8,128)(2,1)S(1)}, u32[]{:S(2)}, u32[]{:S(2)}) collective-permute-start(bf16[17,16,128]{2,1,0:T(8,128)(2,1)S(1)} %get-tuple-element.71), channel_id=1, source_target_pairs={{4,0},{8,4},{12,8},{16,12},{20,16},{24,20},{28,24},{5,1},{9,5},{13... | collective-permute-start | bytes 208904 | tf_op jit(solution)/shard_map/ppermute | solution.py:131
  87.8 5.9 %collective-permute-start.14 = (bf16[8,16,128]{2,1,0:T(8,128)(2,1)S(1)}, bf16[8,16,128]{2,1,0:T(8,128)(2,1)S(1)}, u32[]{:S(2)}, u32[]{:S(2)}) collective-permute-start(bf16[8,16,128]{2,1,0:T(8,128)(2,1)S(1)} %get-tuple-element.74), channel_id=1, source_target_pairs={{1,0},{2,1},{3,2},{5,4},{6,5},{7,6},{9,8},{10,9},{11,10},{13,12},{... | collective-permute-start | bytes 98312 | tf_op jit(solution)/shard_map/ppermute | solution.py:131
  91.7 5.8 %collective-permute-start.13 = (bf16[8,16,128]{2,1,0:T(8,128)(2,1)S(1)}, bf16[8,16,128]{2,1,0:T(8,128)(2,1)S(1)}, u32[]{:S(2)}, u32[]{:S(2)}) collective-permute-start(bf16[8,16,128]{2,1,0:T(8,128)(2,1)S(1)} %get-tuple-element.74), channel_id=1, source_target_pairs={{0,1},{1,2},{2,3},{4,5},{5,6},{6,7},{8,9},{9,10},{10,11},{12,13},{... | collective-permute-start | bytes 98312 | tf_op jit(solution)/shard_map/ppermute | solution.py:131
  97.8 4.5 %collective-permute-start.16 = (bf16[8,16,128]{2,1,0:T(8,128)(2,1)S(1)}, bf16[8,16,128]{2,1,0:T(8,128)(2,1)S(1)}, u32[]{:S(2)}, u32[]{:S(2)}) collective-permute-start(bf16[8,16,128]{2,1,0:T(8,128)(2,1)S(1)} %get-tuple-element.76), channel_id=1, source_target_pairs={{4,0},{8,4},{12,8},{16,12},{20,16},{24,20},{28,24},{5,1},{9,5},{13... | collective-permute-start | bytes 98312 | tf_op jit(solution)/shard_map/ppermute | solution.py:131
  100.3 6.1 %collective-permute-start.15 = (bf16[8,16,128]{2,1,0:T(8,128)(2,1)S(1)}, bf16[8,16,128]{2,1,0:T(8,128)(2,1)S(1)}, u32[]{:S(2)}, u32[]{:S(2)}) collective-permute-start(bf16[8,16,128]{2,1,0:T(8,128)(2,1)S(1)} %get-tuple-element.76), channel_id=1, source_target_pairs={{0,4},{4,8},{8,12},{12,16},{16,20},{20,24},{24,28},{1,5},{5,9},{9,... | collective-permute-start | bytes 98312 | tf_op jit(solution)/shard_map/ppermute | solution.py:131

commit v2 on v0

--- a/solution.py
+++ b/solution.py
@@ -48,18 +48,6 @@
     return jnp.where(at < 0, at + parts, jnp.where(at >= parts, at - parts, at))
 
 
-def columns_split_body(in_ref, *out_refs):
-    cols = out_refs[0].shape[-1]
-    for r, out_ref in enumerate(out_refs):
-        out_ref[...] = in_ref[:, :, :, pl.ds(pl.multiple_of(neighbor_of(r) * cols, cols), cols)]
-
-
-def split_columns(members, parts):
-    own, levels, rows, ny = members.shape
-    out = jax.ShapeDtypeStruct((own, levels, rows, ny // parts), members.dtype)
-    return call(columns_split_body, (out,) * parts, members, in_specs=[VMEM])
-
-
 def left_slot(k):
     return 3 * SUB - 1 - k % SUB - GROUP * (k // SUB)
 
@@ -107,13 +95,21 @@
         )
 
 
+def edge_plane(ref, levels, g):
+    per = ref.shape[1] - levels
+    return g // per, levels + g % per
+
+
 def rows_body(x_ref, left_ref, right_ref, beside_ref, top_ref, bottom_ref):
-    beside_ref[...] = left_ref[...] + right_ref[...]
+    levels = x_ref.shape[0]
+    for g in range(levels // GROUP):
+        left, right = (ref[edge_plane(ref, levels, g)].astype(F32) for ref in (left_ref, right_ref))
+        beside_ref[g] = left + right
     pack_rows(x_ref, 0, top_ref, bottom_ref)
-    pack_rows(beside_ref, x_ref.shape[0] // 2, top_ref, bottom_ref)
-
-
-def columns_edge_body(x_ref, first_ref, last_ref):
+    pack_rows(beside_ref, levels // 2, top_ref, bottom_ref)
+
+
+def opening_body(x_ref, members_ref, *block_refs):
     levels, rows, cols = x_ref.shape
     for g in range(levels // GROUP):
         first = jnp.zeros((rows, LANES), F32)
@@ -121,8 +117,11 @@
         for k in range(GROUP):
             last = put_left(x_ref[g * GROUP + k], k, last)
             first = put_right(x_ref[g * GROUP + k], k, first)
-        first_ref[g] = first
-        last_ref[g] = last
+        for ref, edge in ((block_refs[1], last), (block_refs[-1], first)):
+            ref[edge_plane(ref, levels, g)] = edge.astype(ref.dtype)
+    for r, block_ref in enumerate(block_refs):
+        at = pl.ds(pl.multiple_of(neighbor_of(r) * cols, cols), cols)
+        block_ref[:, :levels] = members_ref[:, :, :, at]
 
 
 def shift(x, axis, step):
@@ -468,13 +467,18 @@
     packed = shape(groups, rows, LANES)
     wind_x, wind_y = (jnp.broadcast_to(w[:, None], (levels, LANES)) for w in (wind_x, wind_y))
 
-    first, last = call(columns_edge_body, (packed, packed), residual_in)
-    left, right = shift(last, "member", 1), shift(first, "member", -1)
-    blocks, left, right = lax.optimization_barrier((split_columns(members, parts), left, right))
-    blocks = [turned(x, r) if r else x for r, x in enumerate(blocks)]
-    around, top, bottom = call(rows_body, (packed, halo, halo), residual_in, left, right)
-    members, around = lax.optimization_barrier((members, around))
+    own = members.shape[0]
+    near = (1, parts - 1)
+    extra = [groups // own if r in near else 0 for r in range(parts)]
+    blocks = [shape(own, levels + n, rows, cols, kind=members.dtype) for n in extra]
+    blocks = list(call(opening_body, tuple(blocks), residual_in, members))
+    for r in near:
+        blocks[r] = turned(blocks[r], r)
+    blocks[1], members, *rest = lax.optimization_barrier((blocks[1], members, *blocks[2:-1]))
+    blocks[2:-1] = [turned(x, r) for r, x in enumerate(rest, 2)]
     sides = side_columns(members, parts)
+    blocks[-1], sides = lax.optimization_barrier((blocks[-1], sides))
+    around, top, bottom = call(rows_body, (packed, halo, halo), residual_in, blocks[1], blocks[-1])
     above, below = shift(bottom, "tile", 1), shift(top, "tile", -1)
     grad = call(
         first_model_body, like,

time: 112 us -> 114 us (1.018)
  waiting for transfers between devices: 16.6 us -> 46.3 us
  blocking collectives: 30.3 us -> 9.74 us
  starting transfers between devices: 42.5 us -> 35.6 us
    ppermute x3, waiting for transfers between devices: 0.01 us -> 29.2 us  [turned(): lax.ppermute(x, 'member', [(i, (i + step) % parts) for i in range(parts)])]
    all_to_all x1, blocking collectives: 30.3 us -> 9.74 us  [per_device(): lax.all_to_all(sides, 'member', split_axis=0, concat_axis=0, tiled=True)]
    ppermute x14 -> x12, starting transfers between devices: 39.2 us -> 33.5 us  [shift(): return lax.ppermute(x, axis, pairs)]
    ppermute x3, starting transfers between devices: 3.26 us -> 2.08 us  [turned(): lax.ppermute(x, 'member', [(i, (i + step) % parts) for i in range(parts)])]
    ppermute x14 -> x12, waiting for transfers between devices: 16.6 us -> 17.1 us  [shift(): return lax.ppermute(x, axis, pairs)]
    pallas_call x12 -> x11, Pallas kernels: 18.3 us -> 17.9 us  [call(): pl.pallas_call(body, out_shape=out_shape, in_specs=in_specs or [VMEM] * l...]
  transfers between devices with their start and end apart: 17 -> 15, of which waited for: 5 -> 7; matrix products, arithmetic and copies ran while one was open for 0% -> 0% of each run, Pallas kernels for 10% -> 9%
where the time goes in v2:
time: 114 us; the launch traced here: 113 us
  waiting for transfers between devices  46.3 us (41%)
  starting transfers between devices  35.6 us (31%)
  Pallas kernels  17.9 us (16%)
  blocking collectives  9.74 us (9%)
  local copies, waits for them, and re-layouts  2.79 us (2%)
    ppermute x12, starting transfers between devices, shift(): return lax.ppermute(x, axis, pairs)  33.5 us
    ppermute x3, waiting for transfers between devices, turned(): lax.ppermute(x, 'member', [(i, (i + step) % parts) for i in range(parts)])  29.2 us
    pallas_call x11, Pallas kernels, call(): pl.pallas_call(body, out_shape=out_shape, in_specs=in_specs or [VMEM] * l...  17.9 us
    ppermute x12, waiting for transfers between devices, shift(): return lax.ppermute(x, axis, pairs)  17.1 us
    all_to_all x1, blocking collectives, per_device(): lax.all_to_all(sides, 'member', split_axis=0, concat_axis=0, tiled=True)  9.74 us
    unnamed x12, local copies, waits for them, and re-layouts  2.65 us
  transfers between devices with their start and end apart: 15, of which 7 were waited for; matrix products, arithmetic and copies ran while one was open for 0% of the time, Pallas kernels for 9%

profile of v2, /device:TPU:20, one launch (start us, length us, event | category | flops | bytes accessed | tf_op | source)
XLA Modules:
  0.0 113.3 jit_solution(14648121060868927996)
XLA Ops:
  0.6 1.6 %copy-done = bf16[2,64,16,512]{3,2,1,0:T(8,128)(2,1)S(1)} copy-done((bf16[2,64,16,512]{3,2,1,0:T(8,128)(2,1)S(1)}, bf16[2,64,16,512]{3,2,1,0:T(8,128)(2,1)}, u32[]{:S(2)}) %copy-start) | copy-done | bytes 2097176
  2.2 1.0 copy-done.2
  3.3 0.4 shard_map.59
  3.7 1.6 %collective-permute-start = (bf16[2,66,16,128]{3,2,1,0:T(8,128)(2,1)S(1)}, bf16[2,66,16,128]{3,2,1,0:T(8,128)(2,1)S(1)}, u32[]{:S(2)}, u32[]{:S(2)}) collective-permute-start(bf16[2,66,16,128]{3,2,1,0:T(8,128)(2,1)S(1)} %get-tuple-element.33), channel_id=1, source_target_pairs={{0,1},{1,2},{2,3},{3,0},{4,5},{5,6},{6,7},{7,4},{8,9},{9,10},{10,1... | collective-permute-start | bytes 1622024 | tf_op jit(solution)/shard_map/ppermute | solution.py:455
  5.4 0.4 collective-permute-start.1
  5.8 29.2 %collective-permute-done.left_ref.refs_1_ = bf16[2,66,16,128]{3,2,1,0:T(8,128)(2,1)S(1)} collective-permute-done((bf16[2,66,16,128]{3,2,1,0:T(8,128)(2,1)S(1)}, bf16[2,66,16,128]{3,2,1,0:T(8,128)(2,1)S(1)}, u32[]{:S(2)}, u32[]{:S(2)}) %collective-permute-start) | collective-permute-done | bytes 540704 | tf_op jit(solution)/shard_map/ppermute | solution.py:455
  35.0 3.4 %shard_map.60 = bf16[4,2,4,16,128]{4,3,2,1,0:T(8,128)(2,1)S(1)} custom-call(bf16[2,64,16,512]{3,2,1,0:T(8,128)(2,1)S(1)} %copy-done.1), custom_call_target="tpu_custom_call" | custom-call | tf_op jit(solution)/shard_map/pallas_call | solution.py:27
  38.5 1.9 %collective-permute-start.2 = (f32[34,8,128]{2,1,0:T(8,128)S(1)}, f32[34,8,128]{2,1,0:T(8,128)S(1)}, u32[]{:S(2)}, u32[]{:S(2)}) collective-permute-start(f32[34,8,128]{2,1,0:T(8,128)S(1)} %get-tuple-element.40), channel_id=1, source_target_pairs={{0,4},{4,8},{8,12},{12,16},{16,20},{20,24},{24,28},{1,5},{5,9},{9,... | collective-permute-start | bytes 417800 | tf_op jit(solution)/shard_map/ppermute | solution.py:130
  40.4 4.5 %collective-permute-start.3 = (f32[34,8,128]{2,1,0:T(8,128)S(1)}, f32[34,8,128]{2,1,0:T(8,128)S(1)}, u32[]{:S(2)}, u32[]{:S(2)}) collective-permute-start(f32[34,8,128]{2,1,0:T(8,128)S(1)} %get-tuple-element.41), channel_id=1, source_target_pairs={{4,0},{8,4},{12,8},{16,12},{20,16},{24,20},{28,24},{5,1},{9,5},{13... | collective-permute-start | bytes 417800 | tf_op jit(solution)/shard_map/ppermute | solution.py:130
  44.9 0.8 collective-permute-done.2.above_ref
  45.7 1.8 %collective-permute-done.3.below_ref = f32[34,8,128]{2,1,0:T(8,128)S(1)} collective-permute-done((f32[34,8,128]{2,1,0:T(8,128)S(1)}, f32[34,8,128]{2,1,0:T(8,128)S(1)}, u32[]{:S(2)}, u32[]{:S(2)}) %collective-permute-start.3) | collective-permute-done | bytes 139296 | tf_op jit(solution)/shard_map/ppermute | solution.py:130
  47.7 4.8 %shard_map.62.grad_ref = f32[64,16,128]{2,1,0:T(8,128)S(1)} custom-call(f32[64,128]{1,0:T(8,128)S(1)} %broadcast_in_dim.4.wx_ref, f32[64,128]{1,0:T(8,128)S(1)} %broadcast_in_dim.5.wy_ref, f32[64,16,128]{2,1,0:T(8,128)S(1)} %copy-done.2, f32[4,16,128]{2,1,0:T(8,128)S(1)} %get-tuple-element.39.beside_ref.around_ref, ...), custom_call_target="tpu_custom_call" | custom-call | tf_op jit(solution)/shard_map/pallas_call | solution.py:27
  52.4 9.7 %all_to_all.5.refs_4_ = bf16[4,2,4,16,128]{4,3,2,1,0:T(8,128)(2,1)S(1)} all-to-all(bf16[4,2,4,16,128]{4,3,2,1,0:T(8,128)(2,1)S(1)} %shard_map.60), channel_id=1, replica_groups=mesh['tile'=8,'member'=4] {'member'}, dimensions={0} | all-to-all | bytes 262144 | tf_op jit(solution)/shard_map/all_to_all | solution.py:488
  62.2 0.6 shard_map.63
  62.8 4.1 %collective-permute-start.6 = (bf16[8,16,128]{2,1,0:T(8,128)(2,1)S(1)}, bf16[8,16,128]{2,1,0:T(8,128)(2,1)S(1)}, u32[]{:S(2)}, u32[]{:S(2)}) collective-permute-start(bf16[8,16,128]{2,1,0:T(8,128)(2,1)S(1)} %get-tuple-element.48), channel_id=1, source_target_pairs={{1,0},{2,1},{3,2},{5,4},{6,5},{7,6},{9,8},{10,9},{11,10},{13,12},{... | collective-permute-start | bytes 98312 | tf_op jit(solution)/shard_map/ppermute | solution.py:130
  66.9 1.9 %collective-permute-start.5 = (bf16[8,16,128]{2,1,0:T(8,128)(2,1)S(1)}, bf16[8,16,128]{2,1,0:T(8,128)(2,1)S(1)}, u32[]{:S(2)}, u32[]{:S(2)}) collective-permute-start(bf16[8,16,128]{2,1,0:T(8,128)(2,1)S(1)} %get-tuple-element.48), channel_id=1, source_target_pairs={{0,1},{1,2},{2,3},{4,5},{5,6},{6,7},{8,9},{9,10},{10,11},{12,13},{... | collective-permute-start | bytes 98312 | tf_op jit(solution)/shard_map/ppermute | solution.py:130
  68.8 3.9 %collective-permute-done.5.left_ref = bf16[8,16,128]{2,1,0:T(8,128)(2,1)S(1)} collective-permute-done((bf16[8,16,128]{2,1,0:T(8,128)(2,1)S(1)}, bf16[8,16,128]{2,1,0:T(8,128)(2,1)S(1)}, u32[]{:S(2)}, u32[]{:S(2)}) %collective-permute-start.5) | collective-permute-done | bytes 32800 | tf_op jit(solution)/shard_map/ppermute | solution.py:130
  73.1 1.9 %collective-permute-start.8 = (bf16[16,16,128]{2,1,0:T(8,128)(2,1)S(1)}, bf16[16,16,128]{2,1,0:T(8,128)(2,1)S(1)}, u32[]{:S(2)}, u32[]{:S(2)}) collective-permute-start(bf16[16,16,128]{2,1,0:T(8,128)(2,1)S(1)} %get-tuple-element.50), channel_id=1, source_target_pairs={{4,0},{8,4},{12,8},{16,12},{20,16},{24,20},{28,24},{5,1},{9,5},{13... | collective-permute-start | bytes 196616 | tf_op jit(solution)/shard_map/ppermute | solution.py:130
  75.0 2.4 %collective-permute-start.7 = (bf16[16,16,128]{2,1,0:T(8,128)(2,1)S(1)}, bf16[16,16,128]{2,1,0:T(8,128)(2,1)S(1)}, u32[]{:S(2)}, u32[]{:S(2)}) collective-permute-start(bf16[16,16,128]{2,1,0:T(8,128)(2,1)S(1)} %get-tuple-element.50), channel_id=1, source_target_pairs={{0,4},{4,8},{8,12},{12,16},{16,20},{20,24},{24,28},{1,5},{5,9},{9,... | collective-permute-start | bytes 196616 | tf_op jit(solution)/shard_map/ppermute | solution.py:130
  77.4 4.1 %collective-permute-done.7.above_ref = bf16[16,16,128]{2,1,0:T(8,128)(2,1)S(1)} collective-permute-done((bf16[16,16,128]{2,1,0:T(8,128)(2,1)S(1)}, bf16[16,16,128]{2,1,0:T(8,128)(2,1)S(1)}, u32[]{:S(2)}, u32[]{:S(2)}) %collective-permute-start.7) | collective-permute-done | bytes 65568 | tf_op jit(solution)/shard_map/ppermute | solution.py:130
  81.5 1.0 shard_map.65
  82.4 1.9 %collective-permute-start.9 = (bf16[17,16,128]{2,1,0:T(8,128)(2,1)S(1)}, bf16[17,16,128]{2,1,0:T(8,128)(2,1)S(1)}, u32[]{:S(2)}, u32[]{:S(2)}) collective-permute-start(bf16[17,16,128]{2,1,0:T(8,128)(2,1)S(1)} %get-tuple-element.56), channel_id=1, source_target_pairs={{0,4},{4,8},{8,12},{12,16},{16,20},{20,24},{24,28},{1,5},{5,9},{9,... | collective-permute-start | bytes 208904 | tf_op jit(solution)/shard_map/ppermute | solution.py:130
  84.4 4.5 %collective-permute-start.10 = (bf16[17,16,128]{2,1,0:T(8,128)(2,1)S(1)}, bf16[17,16,128]{2,1,0:T(8,128)(2,1)S(1)}, u32[]{:S(2)}, u32[]{:S(2)}) collective-permute-start(bf16[17,16,128]{2,1,0:T(8,128)(2,1)S(1)} %get-tuple-element.57), channel_id=1, source_target_pairs={{4,0},{8,4},{12,8},{16,12},{20,16},{24,20},{28,24},{5,1},{9,5},{13... | collective-permute-start | bytes 208904 | tf_op jit(solution)/shard_map/ppermute | solution.py:130
  88.9 2.5 %shard_map.66 = (f32[64,16,128]{2,1,0:T(8,128)S(1)}, f32[4,12,3,8,128]{4,3,2,1,0:T(8,128)S(1)}) custom-call(f32[64,128]{1,0:T(8,128)S(1)} %broadcast_in_dim.4.wx_ref, f32[64,128]{1,0:T(8,128)S(1)} %broadcast_in_dim.5.wy_ref, f32[64,16,128]{2,1,0:T(8,128)S(1)} %get-tuple-element.53.x_ref.residual_ref, f32[4,16,128]{2,1,0:T(8,128)S(1)} %get-tuple-element.55.beside_ref), custom_call_target="tpu_custom_call" | custom-call | tf_op jit(solution)/shard_map/pallas_call | solution.py:27
  91.5 2.8 %shard_map.67 = (f32[8,16,128]{2,1,0:T(8,128)S(1)}, bf16[8,16,128]{2,1,0:T(8,128)(2,1)S(1)}) custom-call(f32[64,128]{1,0:T(8,128)S(1)} %broadcast_in_dim.4.wx_ref, f32[64,128]{1,0:T(8,128)S(1)} %broadcast_in_dim.5.wy_ref, f32[64,16,128]{2,1,0:T(8,128)S(1)} %get-tuple-element.53.x_ref.residual_ref, f32[4,16,128]{2,1,0:T(8,128)S(1)} %get-tuple-element.55.beside_ref, ...), custom_call_target="tpu_custom_call" | custom-call | tf_op jit(solution)/shard_map/pallas_call | solution.py:27
  94.3 2.5 %collective-permute-start.12 = (bf16[8,16,128]{2,1,0:T(8,128)(2,1)S(1)}, bf16[8,16,128]{2,1,0:T(8,128)(2,1)S(1)}, u32[]{:S(2)}, u32[]{:S(2)}) collective-permute-start(bf16[8,16,128]{2,1,0:T(8,128)(2,1)S(1)} %get-tuple-element.60), channel_id=1, source_target_pairs={{1,0},{2,1},{3,2},{5,4},{6,5},{7,6},{9,8},{10,9},{11,10},{13,12},{... | collective-permute-start | bytes 98312 | tf_op jit(solution)/shard_map/ppermute | solution.py:130
  96.7 3.4 %collective-permute-start.11 = (bf16[8,16,128]{2,1,0:T(8,128)(2,1)S(1)}, bf16[8,16,128]{2,1,0:T(8,128)(2,1)S(1)}, u32[]{:S(2)}, u32[]{:S(2)}) collective-permute-start(bf16[8,16,128]{2,1,0:T(8,128)(2,1)S(1)} %get-tuple-element.60), channel_id=1, source_target_pairs={{0,1},{1,2},{2,3},{4,5},{5,6},{6,7},{8,9},{9,10},{10,11},{12,13},{... | collective-permute-start | bytes 98312 | tf_op jit(solution)/shard_map/ppermute | solution.py:130
  100.1 2.4 %collective-permute-done.11.left_ref = bf16[8,16,128]{2,1,0:T(8,128)(2,1)S(1)} collective-permute-done((bf16[8,16,128]{2,1,0:T(8,128)(2,1)S(1)}, bf16[8,16,128]{2,1,0:T(8,128)(2,1)S(1)}, u32[]{:S(2)}, u32[]{:S(2)}) %collective-permute-start.11) | collective-permute-done | bytes 32800 | tf_op jit(solution)/shard_map/ppermute | solution.py:130
  102.8 2.5 %collective-permute-start.14 = (bf16[8,16,128]{2,1,0:T(8,128)(2,1)S(1)}, bf16[8,16,128]{2,1,0:T(8,128)(2,1)S(1)}, u32[]{:S(2)}, u32[]{:S(2)}) collective-permute-start(bf16[8,16,128]{2,1,0:T(8,128)(2,1)S(1)} %get-tuple-element.62), channel_id=1, source_target_pairs={{4,0},{8,4},{12,8},{16,12},{20,16},{24,20},{28,24},{5,1},{9,5},{13... | collective-permute-start | bytes 98312 | tf_op jit(solution)/shard_map/ppermute | solution.py:130
  105.4 1.9 %collective-permute-start.13 = (bf16[8,16,128]{2,1,0:T(8,128)(2,1)S(1)}, bf16[8,16,128]{2,1,0:T(8,128)(2,1)S(1)}, u32[]{:S(2)}, u32[]{:S(2)}) collective-permute-start(bf16[8,16,128]{2,1,0:T(8,128)(2,1)S(1)} %get-tuple-element.62), channel_id=1, source_target_pairs={{0,4},{4,8},{8,12},{12,16},{16,20},{20,24},{24,28},{1,5},{5,9},{9,... | collective-permute-start | bytes 98312 | tf_op jit(solution)/shard_map/ppermute | solution.py:130
  107.3 4.2 %collective-permute-done.13.above_ref = bf16[8,16,128]{2,1,0:T(8,128)(2,1)S(1)} collective-permute-done((bf16[8,16,128]{2,1,0:T(8,128)(2,1)S(1)}, bf16[8,16,128]{2,1,0:T(8,128)(2,1)S(1)}, u32[]{:S(2)}, u32[]{:S(2)}) %collective-permute-start.13) | collective-permute-done | bytes 32800 | tf_op jit(solution)/shard_map/ppermute | solution.py:130
  111.5 1.8 %shard_map.69 = (f32[64,16,128]{2,1,0:T(8,128)}, f32[64,16,128]{2,1,0:T(8,128)}) custom-call(f32[64,16,128]{2,1,0:T(8,128)S(1)} %get-tuple-element.53.x_ref.residual_ref, f32[64,16,128]{2,1,0:T(8,128)S(1)} %get-tuple-element.54.before_ref, bf16[8,16,128]{2,1,0:T(8,128)(2,1)S(1)} %collective-permute-done.13.above_ref, ...), custom_call_target="tpu_custom_call" | custom-call | tf_op jit(solution)/shard_map/pallas_call | solution.py:27
  (24 shorter events, 0.9 us)
Async XLA Ops:
  0.6 1.6 %copy-start = (bf16[2,64,16,512]{3,2,1,0:T(8,128)(2,1)S(1)}, bf16[2,64,16,512]{3,2,1,0:T(8,128)(2,1)}, u32[]{:S(2)}) copy-start(bf16[2,64,16,512]{3,2,1,0:T(8,128)(2,1)} %in_ref) | copy-start | bytes 6291460
  2.2 1.0 copy-start.2
  3.3 31.7 %copy-start.1 = (bf16[2,64,16,512]{3,2,1,0:T(8,128)(2,1)S(1)}, bf16[2,64,16,512]{3,2,1,0:T(8,128)(2,1)}, u32[]{:S(2)}) copy-start(bf16[2,64,16,512]{3,2,1,0:T(8,128)(2,1)} %in_ref) | copy-start | bytes 6291460
  3.7 43.8 %copy-start.4 = (f32[64]{0:T(128)S(1)}, f32[64]{0:T(128)}, u32[]{:S(2)}) copy-start(f32[64]{0:T(128)} %param.6) | copy-start | bytes 772
  3.7 43.9 %copy-start.5 = (f32[64]{0:T(128)S(1)}, f32[64]{0:T(128)}, u32[]{:S(2)}) copy-start(f32[64]{0:T(128)} %param.7) | copy-start | bytes 772
  3.7 31.3 %collective-permute-start = (bf16[2,66,16,128]{3,2,1,0:T(8,128)(2,1)S(1)}, bf16[2,66,16,128]{3,2,1,0:T(8,128)(2,1)S(1)}, u32[]{:S(2)}, u32[]{:S(2)}) collective-permute-start(bf16[2,66,16,128]{3,2,1,0:T(8,128)(2,1)S(1)} %get-tuple-element.33), channel_id=1, source_target_pairs={{0,1},{1,2},{2,3},{3,0},{4,5},{5,6},{6,7},{7,4},{8,9},{9,10},{10,1... | collective-permute-start | bytes 1622024 | tf_op jit(solution)/shard_map/ppermute | solution.py:455
  5.4 33.1 %collective-permute-start.1 = (bf16[2,66,16,128]{3,2,1,0:T(8,128)(2,1)S(1)}, bf16[2,66,16,128]{3,2,1,0:T(8,128)(2,1)S(1)}, u32[]{:S(2)}, u32[]{:S(2)}) collective-permute-start(bf16[2,66,16,128]{3,2,1,0:T(8,128)(2,1)S(1)} %get-tuple-element.36), channel_id=1, source_target_pairs={{0,3},{1,0},{2,1},{3,2},{4,7},{5,4},{6,5},{7,6},{8,11},{9,8},{10,9... | collective-permute-start | bytes 1622024 | tf_op jit(solution)/shard_map/ppermute | solution.py:455
  35.0 27.2 %collective-permute-start.4 = (bf16[2,64,16,128]{3,2,1,0:T(8,128)(2,1)S(1)}, bf16[2,64,16,128]{3,2,1,0:T(8,128)(2,1)S(1)}, u32[]{:S(2)}, u32[]{:S(2)}) collective-permute-start(bf16[2,64,16,128]{3,2,1,0:T(8,128)(2,1)S(1)} %get-tuple-element.47), channel_id=1, source_target_pairs={{0,2},{1,3},{2,0},{3,1},{4,6},{5,7},{6,4},{7,5},{8,10},{9,11},{10,... | collective-permute-start | bytes 1572872 | tf_op jit(solution)/shard_map/ppermute | solution.py:455
  38.5 7.3 %collective-permute-start.2 = (f32[34,8,128]{2,1,0:T(8,128)S(1)}, f32[34,8,128]{2,1,0:T(8,128)S(1)}, u32[]{:S(2)}, u32[]{:S(2)}) collective-permute-start(f32[34,8,128]{2,1,0:T(8,128)S(1)} %get-tuple-element.40), channel_id=1, source_target_pairs={{0,4},{4,8},{8,12},{12,16},{16,20},{20,24},{24,28},{1,5},{5,9},{9,... | collective-permute-start | bytes 417800 | tf_op jit(solution)/shard_map/ppermute | solution.py:130
  40.4 7.1 %collective-permute-start.3 = (f32[34,8,128]{2,1,0:T(8,128)S(1)}, f32[34,8,128]{2,1,0:T(8,128)S(1)}, u32[]{:S(2)}, u32[]{:S(2)}) collective-permute-start(f32[34,8,128]{2,1,0:T(8,128)S(1)} %get-tuple-element.41), channel_id=1, source_target_pairs={{4,0},{8,4},{12,8},{16,12},{20,16},{24,20},{28,24},{5,1},{9,5},{13... | collective-permute-start | bytes 417800 | tf_op jit(solution)/shard_map/ppermute | solution.py:130
  47.7 33.8 %copy-start.3 = (f32[64,16,128]{2,1,0:T(8,128)S(1)}, f32[64,16,128]{2,1,0:T(8,128)}, u32[]{:S(2)}) copy-start(f32[64,16,128]{2,1,0:T(8,128)} %residual_ref.1) | copy-start | bytes 1572868
  62.8 6.0 %collective-permute-start.6 = (bf16[8,16,128]{2,1,0:T(8,128)(2,1)S(1)}, bf16[8,16,128]{2,1,0:T(8,128)(2,1)S(1)}, u32[]{:S(2)}, u32[]{:S(2)}) collective-permute-start(bf16[8,16,128]{2,1,0:T(8,128)(2,1)S(1)} %get-tuple-element.48), channel_id=1, source_target_pairs={{1,0},{2,1},{3,2},{5,4},{6,5},{7,6},{9,8},{10,9},{11,10},{13,12},{... | collective-permute-start | bytes 98312 | tf_op jit(solution)/shard_map/ppermute | solution.py:130
  66.9 5.8 %collective-permute-start.5 = (bf16[8,16,128]{2,1,0:T(8,128)(2,1)S(1)}, bf16[8,16,128]{2,1,0:T(8,128)(2,1)S(1)}, u32[]{:S(2)}, u32[]{:S(2)}) collective-permute-start(bf16[8,16,128]{2,1,0:T(8,128)(2,1)S(1)} %get-tuple-element.48), channel_id=1, source_target_pairs={{0,1},{1,2},{2,3},{4,5},{5,6},{6,7},{8,9},{9,10},{10,11},{12,13},{... | collective-permute-start | bytes 98312 | tf_op jit(solution)/shard_map/ppermute | solution.py:130
  73.1 4.3 %collective-permute-start.8 = (bf16[16,16,128]{2,1,0:T(8,128)(2,1)S(1)}, bf16[16,16,128]{2,1,0:T(8,128)(2,1)S(1)}, u32[]{:S(2)}, u32[]{:S(2)}) collective-permute-start(bf16[16,16,128]{2,1,0:T(8,128)(2,1)S(1)} %get-tuple-element.50), channel_id=1, source_target_pairs={{4,0},{8,4},{12,8},{16,12},{20,16},{24,20},{28,24},{5,1},{9,5},{13... | collective-permute-start | bytes 196616 | tf_op jit(solution)/shard_map/ppermute | solution.py:130
  75.0 6.5 %collective-permute-start.7 = (bf16[16,16,128]{2,1,0:T(8,128)(2,1)S(1)}, bf16[16,16,128]{2,1,0:T(8,128)(2,1)S(1)}, u32[]{:S(2)}, u32[]{:S(2)}) collective-permute-start(bf16[16,16,128]{2,1,0:T(8,128)(2,1)S(1)} %get-tuple-element.50), channel_id=1, source_target_pairs={{0,4},{4,8},{8,12},{12,16},{16,20},{20,24},{24,28},{1,5},{5,9},{9,... | collective-permute-start | bytes 196616 | tf_op jit(solution)/shard_map/ppermute | solution.py:130
  82.4 9.0 %collective-permute-start.9 = (bf16[17,16,128]{2,1,0:T(8,128)(2,1)S(1)}, bf16[17,16,128]{2,1,0:T(8,128)(2,1)S(1)}, u32[]{:S(2)}, u32[]{:S(2)}) collective-permute-start(bf16[17,16,128]{2,1,0:T(8,128)(2,1)S(1)} %get-tuple-element.56), channel_id=1, source_target_pairs={{0,4},{4,8},{8,12},{12,16},{16,20},{20,24},{24,28},{1,5},{5,9},{9,... | collective-permute-start | bytes 208904 | tf_op jit(solution)/shard_map/ppermute | solution.py:130
  84.4 7.1 %collective-permute-start.10 = (bf16[17,16,128]{2,1,0:T(8,128)(2,1)S(1)}, bf16[17,16,128]{2,1,0:T(8,128)(2,1)S(1)}, u32[]{:S(2)}, u32[]{:S(2)}) collective-permute-start(bf16[17,16,128]{2,1,0:T(8,128)(2,1)S(1)} %get-tuple-element.57), channel_id=1, source_target_pairs={{4,0},{8,4},{12,8},{16,12},{20,16},{24,20},{28,24},{5,1},{9,5},{13... | collective-permute-start | bytes 208904 | tf_op jit(solution)/shard_map/ppermute | solution.py:130
  94.3 5.9 %collective-permute-start.12 = (bf16[8,16,128]{2,1,0:T(8,128)(2,1)S(1)}, bf16[8,16,128]{2,1,0:T(8,128)(2,1)S(1)}, u32[]{:S(2)}, u32[]{:S(2)}) collective-permute-start(bf16[8,16,128]{2,1,0:T(8,128)(2,1)S(1)} %get-tuple-element.60), channel_id=1, source_target_pairs={{1,0},{2,1},{3,2},{5,4},{6,5},{7,6},{9,8},{10,9},{11,10},{13,12},{... | collective-permute-start | bytes 98312 | tf_op jit(solution)/shard_map/ppermute | solution.py:130
  96.7 5.8 %collective-permute-start.11 = (bf16[8,16,128]{2,1,0:T(8,128)(2,1)S(1)}, bf16[8,16,128]{2,1,0:T(8,128)(2,1)S(1)}, u32[]{:S(2)}, u32[]{:S(2)}) collective-permute-start(bf16[8,16,128]{2,1,0:T(8,128)(2,1)S(1)} %get-tuple-element.60), channel_id=1, source_target_pairs={{0,1},{1,2},{2,3},{4,5},{5,6},{6,7},{8,9},{9,10},{10,11},{12,13},{... | collective-permute-start | bytes 98312 | tf_op jit(solution)/shard_map/ppermute | solution.py:130
  102.8 4.5 %collective-permute-start.14 = (bf16[8,16,128]{2,1,0:T(8,128)(2,1)S(1)}, bf16[8,16,128]{2,1,0:T(8,128)(2,1)S(1)}, u32[]{:S(2)}, u32[]{:S(2)}) collective-permute-start(bf16[8,16,128]{2,1,0:T(8,128)(2,1)S(1)} %get-tuple-element.62), channel_id=1, source_target_pairs={{4,0},{8,4},{12,8},{16,12},{20,16},{24,20},{28,24},{5,1},{9,5},{13... | collective-permute-start | bytes 98312 | tf_op jit(solution)/shard_map/ppermute | solution.py:130
  105.4 6.1 %collective-permute-start.13 = (bf16[8,16,128]{2,1,0:T(8,128)(2,1)S(1)}, bf16[8,16,128]{2,1,0:T(8,128)(2,1)S(1)}, u32[]{:S(2)}, u32[]{:S(2)}) collective-permute-start(bf16[8,16,128]{2,1,0:T(8,128)(2,1)S(1)} %get-tuple-element.62), channel_id=1, source_target_pairs={{0,4},{4,8},{8,12},{12,16},{16,20},{20,24},{24,28},{1,5},{5,9},{9,... | collective-permute-start | bytes 98312 | tf_op jit(solution)/shard_map/ppermute | solution.py:130

commit v3 on v0

--- a/solution.py
+++ b/solution.py
@@ -48,16 +48,20 @@
     return jnp.where(at < 0, at + parts, jnp.where(at >= parts, at - parts, at))
 
 
+def block_of(step, cols):
+    return pl.ds(pl.multiple_of(neighbor_of(step) * cols, cols), cols)
+
+
 def columns_split_body(in_ref, *out_refs):
     cols = out_refs[0].shape[-1]
     for r, out_ref in enumerate(out_refs):
-        out_ref[...] = in_ref[:, :, :, pl.ds(pl.multiple_of(neighbor_of(r) * cols, cols), cols)]
+        out_ref[...] = in_ref[:, :, :, block_of(r, cols)]
 
 
 def split_columns(members, parts):
     own, levels, rows, ny = members.shape
     out = jax.ShapeDtypeStruct((own, levels, rows, ny // parts), members.dtype)
-    return call(columns_split_body, (out,) * parts, members, in_specs=[VMEM])
+    return call(columns_split_body, (out,) * 2, members)
 
 
 def left_slot(k):
@@ -74,11 +78,15 @@
     return jnp.where(here, pltpu.roll(x, MODEL_STEPS * (left_slot(k) + SUB), 1), total)
 
 
-def sides_body(in_ref, out_ref):
-    parts, own, groups, rows, _ = out_ref.shape
-    cols = in_ref.shape[-1] // parts
-    for r in range(parts):
-        before, after = (pl.ds((r + parts + d) % parts * cols, cols) for d in (-1, 1))
+def sides_body(in_ref, *out_refs):
+    levels = in_ref.shape[1]
+    own, groups, rows, _ = out_refs[0].shape
+    cols = in_ref.shape[-1] // len(out_refs)
+    for r, out_ref in enumerate(out_refs):
+        start = out_ref.shape[1] - groups
+        if start:
+            out_ref[:, :start] = in_ref[:, :, :, block_of(r, cols)]
+        before, after = block_of(r - 1, cols), block_of(r + 1, cols)
         for m in range(own):
 
             def step(g, carry):
@@ -86,7 +94,7 @@
                 for k in range(GROUP):
                     total = put_left(in_ref[m, g * GROUP + k, :, before].astype(F32), k, total)
                     total = put_right(in_ref[m, g * GROUP + k, :, after].astype(F32), k, total)
-                out_ref[r, m, g] = total.astype(out_ref.dtype)
+                out_ref[m, start + g] = total.astype(out_ref.dtype)
                 return carry
 
             lax.fori_loop(0, groups, step, 0)
@@ -94,7 +102,10 @@
 
 def side_columns(members, parts):
     own, levels, rows, ny = members.shape
-    return call(sides_body, jax.ShapeDtypeStruct((parts, own, levels // GROUP, rows, LANES), members.dtype), members)
+    groups = levels // GROUP
+    thin = jax.ShapeDtypeStruct((own, groups, rows, LANES), members.dtype)
+    full = jax.ShapeDtypeStruct((own, levels + groups, rows, LANES), members.dtype)
+    return call(sides_body, (thin,) * 2 + (full,) * (parts - 2), members)
 
 
 def pack_rows(ref, at, top_ref, bottom_ref):
@@ -403,8 +414,8 @@
 
 
 def update_body(parts, residual_ref, around_ref, above_ref, mid_ref, below_ref, *refs):
-    member_refs, sides_ref = refs[:parts], refs[parts]
-    analysis_ref, out_ref, beside_ref, top_ref, bottom_ref, local_ref, top_wide_ref, bottom_wide_ref = refs[parts + 1 :]
+    member_refs, side_refs = refs[:parts], refs[parts : parts + 2] + refs[2:parts]
+    analysis_ref, out_ref, beside_ref, top_ref, bottom_ref, local_ref, top_wide_ref, bottom_wide_ref = refs[parts + 2 :]
     levels, rows, cols = residual_ref.shape
     own = member_refs[0].shape[0]
     count = parts * own
@@ -419,7 +430,10 @@
     for g in range(levels // GROUP):
         total = jnp.zeros((rows, LANES), F32)
         for m in range(count):
-            total = total + sides_ref[m // own, m % own, g].astype(F32) * local_ref[count + m]
+            ref = side_refs[m // own]
+            at = neighbor_of(-(m // own)) * own + m % own
+            member = ref[m % own, ref.shape[1] - levels // GROUP + g]
+            total = total + member.astype(F32) * local_ref[count + at]
         beside_ref[g] = around_ref[g] - RELAX * total
     pack_rows(out_ref, 0, top_wide_ref, bottom_wide_ref)
     pack_rows(beside_ref, levels // 2, top_wide_ref, bottom_wide_ref)
@@ -468,29 +482,30 @@
     packed = shape(groups, rows, LANES)
     wind_x, wind_y = (jnp.broadcast_to(w[:, None], (levels, LANES)) for w in (wind_x, wind_y))
 
+    mine, early = split_columns(members, parts)
+    early, residual_in = lax.optimization_barrier((early, residual_in))
+    early = turned(early, 1)
     first, last = call(columns_edge_body, (packed, packed), residual_in)
     left, right = shift(last, "member", 1), shift(first, "member", -1)
-    blocks, left, right = lax.optimization_barrier((split_columns(members, parts), left, right))
-    blocks = [turned(x, r) if r else x for r, x in enumerate(blocks)]
+    members, first = lax.optimization_barrier((members, first))
+    later, early, left, right = lax.optimization_barrier((side_columns(members, parts), early, left, right))
+    blocks = [mine, early] + [turned(x, r) for r, x in enumerate(later[2:], 2)]
+    sides = [later[0], turned(later[1], 1)]
     around, top, bottom = call(rows_body, (packed, halo, halo), residual_in, left, right)
-    members, around = lax.optimization_barrier((members, around))
-    sides = side_columns(members, parts)
     above, below = shift(bottom, "tile", 1), shift(top, "tile", -1)
     grad = call(
         first_model_body, like,
         wind_x, wind_y, residual_in, around, above, below, in_specs=[VMEM] * 6,
     )
     grad, sides = lax.optimization_barrier((grad, sides))
-    sides = lax.all_to_all(sides, "member", split_axis=0, concat_axis=0, tiled=True)
-    grad, sides = lax.optimization_barrier((grad, sides))
     wide, thin = call(
         project_body, both(count, rows, cols), grad, *blocks, in_specs=[VMEM] * (1 + parts)
     )
 
     analysis, residual, beside, top, bottom = call(
         functools.partial(update_body, parts), (like, like, packed, thin_halo, thin_halo),
-        residual_in, around, *smoothed(wide, thin, 2 * count), *blocks, sides,
-        in_specs=[VMEM] * (6 + parts),
+        residual_in, around, *smoothed(wide, thin, 2 * count), *blocks, *sides,
+        in_specs=[VMEM] * (7 + parts),
         scratch=[pltpu.VMEM((2 * count, rows, cols), F32)] + wide_halo,
     )
     above, below = shift(bottom, "tile", 1), shift(top, "tile", -1)

time: 112 us -> 108 us (0.964)
  blocking collectives: 30.3 us -> 0 us
  waiting for transfers between devices: 16.6 us -> 39.4 us
  starting transfers between devices: 42.5 us -> 45.6 us
    all_to_all x1 -> x0, blocking collectives: 30.3 us -> none  [per_device(): lax.all_to_all(sides, 'member', split_axis=0, concat_axis=0, tiled=True)]
    ppermute x3 -> x4, waiting for transfers between devices: 0.01 us -> 22.1 us  [turned(): lax.ppermute(x, 'member', [(i, (i + step) % parts) for i in range(parts)])]
    ppermute x3 -> x4, starting transfers between devices: 3.26 us -> 5.9 us  [turned(): lax.ppermute(x, 'member', [(i, (i + step) % parts) for i in range(parts)])]
  transfers between devices with their start and end apart: 17 -> 18, of which waited for: 5 -> 7; matrix products, arithmetic and copies ran while one was open for 0% -> 0% of each run, Pallas kernels for 10% -> 10%
where the time goes in v3:
time: 108 us; the launch traced here: 107 us
  starting transfers between devices  45.6 us (42%)
  waiting for transfers between devices  39.4 us (36%)
  Pallas kernels  18.3 us (17%)
  local copies, waits for them, and re-layouts  2.79 us (3%)
    ppermute x14, starting transfers between devices, shift(): return lax.ppermute(x, axis, pairs)  39.7 us
    ppermute x4, waiting for transfers between devices, turned(): lax.ppermute(x, 'member', [(i, (i + step) % parts) for i in range(parts)])  22.1 us
    pallas_call x12, Pallas kernels, call(): pl.pallas_call(body, out_shape=out_shape, in_specs=in_specs or [VMEM] * l...  18.3 us
    ppermute x14, waiting for transfers between devices, shift(): return lax.ppermute(x, axis, pairs)  17.3 us
    ppermute x4, starting transfers between devices, turned(): lax.ppermute(x, 'member', [(i, (i + step) % parts) for i in range(parts)])  5.9 us
    unnamed x12, local copies, waits for them, and re-layouts  2.65 us
  transfers between devices with their start and end apart: 18, of which 7 were waited for; matrix products, arithmetic and copies ran while one was open for 0% of the time, Pallas kernels for 10%

profile of v3, /device:TPU:20, one launch (start us, length us, event | category | flops | bytes accessed | tf_op | source)
XLA Modules:
  0.0 106.9 jit_solution(4763896373301700341)
XLA Ops:
  0.6 1.6 %copy-done = bf16[2,64,16,512]{3,2,1,0:T(8,128)(2,1)S(1)} copy-done((bf16[2,64,16,512]{3,2,1,0:T(8,128)(2,1)S(1)}, bf16[2,64,16,512]{3,2,1,0:T(8,128)(2,1)}, u32[]{:S(2)}) %copy-start) | copy-done | bytes 2097176
  2.4 1.6 %collective-permute-start = (bf16[2,64,16,128]{3,2,1,0:T(8,128)(2,1)S(1)}, bf16[2,64,16,128]{3,2,1,0:T(8,128)(2,1)S(1)}, u32[]{:S(2)}, u32[]{:S(2)}) collective-permute-start(bf16[2,64,16,128]{3,2,1,0:T(8,128)(2,1)S(1)} %get-tuple-element.49), channel_id=1, source_target_pairs={{0,1},{1,2},{2,3},{3,0},{4,5},{5,6},{6,7},{7,4},{8,9},{9,10},{10,1... | collective-permute-start | bytes 1572872 | tf_op jit(solution)/shard_map/ppermute | solution.py:470
  4.1 1.0 copy-done.2
  5.4 2.3 %collective-permute-start.1 = (f32[4,16,128]{2,1,0:T(8,128)S(1)}, f32[4,16,128]{2,1,0:T(8,128)S(1)}, u32[]{:S(2)}, u32[]{:S(2)}) collective-permute-start(f32[4,16,128]{2,1,0:T(8,128)S(1)} %get-tuple-element.50), channel_id=1, source_target_pairs={{0,1},{1,2},{2,3},{4,5},{5,6},{6,7},{8,9},{9,10},{10,11},{12,13},{... | collective-permute-start | bytes 98312 | tf_op jit(solution)/shard_map/ppermute | solution.py:142
  7.8 3.5 %collective-permute-start.2 = (f32[4,16,128]{2,1,0:T(8,128)S(1)}, f32[4,16,128]{2,1,0:T(8,128)S(1)}, u32[]{:S(2)}, u32[]{:S(2)}) collective-permute-start(f32[4,16,128]{2,1,0:T(8,128)S(1)} %get-tuple-element.43), channel_id=1, source_target_pairs={{1,0},{2,1},{3,2},{5,4},{6,5},{7,6},{9,8},{10,9},{11,10},{13,12},{... | collective-permute-start | bytes 98312 | tf_op jit(solution)/shard_map/ppermute | solution.py:142
  11.3 3.6 %shard_map.61 = (bf16[2,4,16,128]{3,2,1,0:T(8,128)(2,1)S(1)}, bf16[2,4,16,128]{3,2,1,0:T(8,128)(2,1)S(1)}, bf16[2,68,16,128]{3,2,1,0:T(8,128)(2,1)S(1)}, bf16[2,68,16,128]{3,2,1,0:T(8,128)(2,1)S(1)}) custom-call(bf16[2,64,16,512]{3,2,1,0:T(8,128)(2,1)S(1)} %copy-done.1), custom_call_target="tpu_custom_call" | custom-call | tf_op jit(solution)/shard_map/pallas_call | solution.py:27
  14.9 2.0 %collective-permute-done.1.left_ref = f32[4,16,128]{2,1,0:T(8,128)S(1)} collective-permute-done((f32[4,16,128]{2,1,0:T(8,128)S(1)}, f32[4,16,128]{2,1,0:T(8,128)S(1)}, u32[]{:S(2)}, u32[]{:S(2)}) %collective-permute-start.1) | collective-permute-done | bytes 32800 | tf_op jit(solution)/shard_map/ppermute | solution.py:142
  16.9 2.2 %collective-permute-start.6 = (bf16[2,68,16,128]{3,2,1,0:T(8,128)(2,1)S(1)}, bf16[2,68,16,128]{3,2,1,0:T(8,128)(2,1)S(1)}, u32[]{:S(2)}, u32[]{:S(2)}) collective-permute-start(bf16[2,68,16,128]{3,2,1,0:T(8,128)(2,1)S(1)} %get-tuple-element.61), channel_id=1, source_target_pairs={{0,2},{1,3},{2,0},{3,1},{4,6},{5,7},{6,4},{7,5},{8,10},{9,11},{10,... | collective-permute-start | bytes 1671176 | tf_op jit(solution)/shard_map/ppermute | solution.py:470
  19.9 1.9 %collective-permute-start.3 = (f32[34,8,128]{2,1,0:T(8,128)S(1)}, f32[34,8,128]{2,1,0:T(8,128)S(1)}, u32[]{:S(2)}, u32[]{:S(2)}) collective-permute-start(f32[34,8,128]{2,1,0:T(8,128)S(1)} %get-tuple-element.54), channel_id=1, source_target_pairs={{0,4},{4,8},{8,12},{12,16},{16,20},{20,24},{24,28},{1,5},{5,9},{9,... | collective-permute-start | bytes 417800 | tf_op jit(solution)/shard_map/ppermute | solution.py:142
  21.9 4.5 %collective-permute-start.4 = (f32[34,8,128]{2,1,0:T(8,128)S(1)}, f32[34,8,128]{2,1,0:T(8,128)S(1)}, u32[]{:S(2)}, u32[]{:S(2)}) collective-permute-start(f32[34,8,128]{2,1,0:T(8,128)S(1)} %get-tuple-element.55), channel_id=1, source_target_pairs={{4,0},{8,4},{12,8},{16,12},{20,16},{24,20},{28,24},{5,1},{9,5},{13... | collective-permute-start | bytes 417800 | tf_op jit(solution)/shard_map/ppermute | solution.py:142
  26.4 1.2 %collective-permute-start.5 = (bf16[2,4,16,128]{3,2,1,0:T(8,128)(2,1)S(1)}, bf16[2,4,16,128]{3,2,1,0:T(8,128)(2,1)S(1)}, u32[]{:S(2)}, u32[]{:S(2)}) collective-permute-start(bf16[2,4,16,128]{3,2,1,0:T(8,128)(2,1)S(1)} %get-tuple-element.57), channel_id=1, source_target_pairs={{0,1},{1,2},{2,3},{3,0},{4,5},{5,6},{6,7},{7,4},{8,9},{9,10},{10,1... | collective-permute-start | bytes 98312 | tf_op jit(solution)/shard_map/ppermute | solution.py:470
  27.6 1.3 %collective-permute-done.4.below_ref = f32[34,8,128]{2,1,0:T(8,128)S(1)} collective-permute-done((f32[34,8,128]{2,1,0:T(8,128)S(1)}, f32[34,8,128]{2,1,0:T(8,128)S(1)}, u32[]{:S(2)}, u32[]{:S(2)}) %collective-permute-start.4) | collective-permute-done | bytes 139296 | tf_op jit(solution)/shard_map/ppermute | solution.py:142
  29.1 4.8 %shard_map.63.grad_ref = f32[64,16,128]{2,1,0:T(8,128)S(1)} custom-call(f32[64,128]{1,0:T(8,128)S(1)} %broadcast_in_dim.4.wx_ref, f32[64,128]{1,0:T(8,128)S(1)} %broadcast_in_dim.5.wy_ref, f32[64,16,128]{2,1,0:T(8,128)S(1)} %copy-done.2, f32[4,16,128]{2,1,0:T(8,128)S(1)} %get-tuple-element.53.beside_ref.around_ref, ...), custom_call_target="tpu_custom_call" | custom-call | tf_op jit(solution)/shard_map/pallas_call | solution.py:27
  33.9 22.1 %collective-permute-done.5.refs_5_ = bf16[2,4,16,128]{3,2,1,0:T(8,128)(2,1)S(1)} collective-permute-done((bf16[2,4,16,128]{3,2,1,0:T(8,128)(2,1)S(1)}, bf16[2,4,16,128]{3,2,1,0:T(8,128)(2,1)S(1)}, u32[]{:S(2)}, u32[]{:S(2)}) %collective-permute-start.5) | collective-permute-done | bytes 32800 | tf_op jit(solution)/shard_map/ppermute | solution.py:470
  56.6 4.1 %collective-permute-start.9 = (bf16[8,16,128]{2,1,0:T(8,128)(2,1)S(1)}, bf16[8,16,128]{2,1,0:T(8,128)(2,1)S(1)}, u32[]{:S(2)}, u32[]{:S(2)}) collective-permute-start(bf16[8,16,128]{2,1,0:T(8,128)(2,1)S(1)} %get-tuple-element.63), channel_id=1, source_target_pairs={{1,0},{2,1},{3,2},{5,4},{6,5},{7,6},{9,8},{10,9},{11,10},{13,12},{... | collective-permute-start | bytes 98312 | tf_op jit(solution)/shard_map/ppermute | solution.py:142
  60.7 1.9 %collective-permute-start.8 = (bf16[8,16,128]{2,1,0:T(8,128)(2,1)S(1)}, bf16[8,16,128]{2,1,0:T(8,128)(2,1)S(1)}, u32[]{:S(2)}, u32[]{:S(2)}) collective-permute-start(bf16[8,16,128]{2,1,0:T(8,128)(2,1)S(1)} %get-tuple-element.63), channel_id=1, source_target_pairs={{0,1},{1,2},{2,3},{4,5},{5,6},{6,7},{8,9},{9,10},{10,11},{12,13},{... | collective-permute-start | bytes 98312 | tf_op jit(solution)/shard_map/ppermute | solution.py:142
  62.7 3.9 %collective-permute-done.8.left_ref = bf16[8,16,128]{2,1,0:T(8,128)(2,1)S(1)} collective-permute-done((bf16[8,16,128]{2,1,0:T(8,128)(2,1)S(1)}, bf16[8,16,128]{2,1,0:T(8,128)(2,1)S(1)}, u32[]{:S(2)}, u32[]{:S(2)}) %collective-permute-start.8) | collective-permute-done | bytes 32800 | tf_op jit(solution)/shard_map/ppermute | solution.py:142
  66.9 1.9 %collective-permute-start.11 = (bf16[16,16,128]{2,1,0:T(8,128)(2,1)S(1)}, bf16[16,16,128]{2,1,0:T(8,128)(2,1)S(1)}, u32[]{:S(2)}, u32[]{:S(2)}) collective-permute-start(bf16[16,16,128]{2,1,0:T(8,128)(2,1)S(1)} %get-tuple-element.65), channel_id=1, source_target_pairs={{4,0},{8,4},{12,8},{16,12},{20,16},{24,20},{28,24},{5,1},{9,5},{13... | collective-permute-start | bytes 196616 | tf_op jit(solution)/shard_map/ppermute | solution.py:142
  68.8 2.4 %collective-permute-start.10 = (bf16[16,16,128]{2,1,0:T(8,128)(2,1)S(1)}, bf16[16,16,128]{2,1,0:T(8,128)(2,1)S(1)}, u32[]{:S(2)}, u32[]{:S(2)}) collective-permute-start(bf16[16,16,128]{2,1,0:T(8,128)(2,1)S(1)} %get-tuple-element.65), channel_id=1, source_target_pairs={{0,4},{4,8},{8,12},{12,16},{16,20},{20,24},{24,28},{1,5},{5,9},{9,... | collective-permute-start | bytes 196616 | tf_op jit(solution)/shard_map/ppermute | solution.py:142
  71.3 4.1 %collective-permute-done.10.above_ref = bf16[16,16,128]{2,1,0:T(8,128)(2,1)S(1)} collective-permute-done((bf16[16,16,128]{2,1,0:T(8,128)(2,1)S(1)}, bf16[16,16,128]{2,1,0:T(8,128)(2,1)S(1)}, u32[]{:S(2)}, u32[]{:S(2)}) %collective-permute-start.10) | collective-permute-done | bytes 65568 | tf_op jit(solution)/shard_map/ppermute | solution.py:142
  75.3 0.9 shard_map.66
  76.3 1.9 %collective-permute-start.12 = (bf16[17,16,128]{2,1,0:T(8,128)(2,1)S(1)}, bf16[17,16,128]{2,1,0:T(8,128)(2,1)S(1)}, u32[]{:S(2)}, u32[]{:S(2)}) collective-permute-start(bf16[17,16,128]{2,1,0:T(8,128)(2,1)S(1)} %get-tuple-element.72), channel_id=1, source_target_pairs={{0,4},{4,8},{8,12},{12,16},{16,20},{20,24},{24,28},{1,5},{5,9},{9,... | collective-permute-start | bytes 208904 | tf_op jit(solution)/shard_map/ppermute | solution.py:142
  78.2 4.5 %collective-permute-start.13 = (bf16[17,16,128]{2,1,0:T(8,128)(2,1)S(1)}, bf16[17,16,128]{2,1,0:T(8,128)(2,1)S(1)}, u32[]{:S(2)}, u32[]{:S(2)}) collective-permute-start(bf16[17,16,128]{2,1,0:T(8,128)(2,1)S(1)} %get-tuple-element.73), channel_id=1, source_target_pairs={{4,0},{8,4},{12,8},{16,12},{20,16},{24,20},{28,24},{5,1},{9,5},{13... | collective-permute-start | bytes 208904 | tf_op jit(solution)/shard_map/ppermute | solution.py:142
  82.8 2.5 %shard_map.67 = (f32[64,16,128]{2,1,0:T(8,128)S(1)}, f32[4,12,3,8,128]{4,3,2,1,0:T(8,128)S(1)}) custom-call(f32[64,128]{1,0:T(8,128)S(1)} %broadcast_in_dim.4.wx_ref, f32[64,128]{1,0:T(8,128)S(1)} %broadcast_in_dim.5.wy_ref, f32[64,16,128]{2,1,0:T(8,128)S(1)} %get-tuple-element.69.x_ref.residual_ref, f32[4,16,128]{2,1,0:T(8,128)S(1)} %get-tuple-element.71.beside_ref), custom_call_target="tpu_custom_call" | custom-call | tf_op jit(solution)/shard_map/pallas_call | solution.py:27
  85.3 2.8 %shard_map.68 = (f32[8,16,128]{2,1,0:T(8,128)S(1)}, bf16[8,16,128]{2,1,0:T(8,128)(2,1)S(1)}) custom-call(f32[64,128]{1,0:T(8,128)S(1)} %broadcast_in_dim.4.wx_ref, f32[64,128]{1,0:T(8,128)S(1)} %broadcast_in_dim.5.wy_ref, f32[64,16,128]{2,1,0:T(8,128)S(1)} %get-tuple-element.69.x_ref.residual_ref, f32[4,16,128]{2,1,0:T(8,128)S(1)} %get-tuple-element.71.beside_ref, ...), custom_call_target="tpu_custom_call" | custom-call | tf_op jit(solution)/shard_map/pallas_call | solution.py:27
  88.1 1.9 %collective-permute-start.15 = (bf16[8,16,128]{2,1,0:T(8,128)(2,1)S(1)}, bf16[8,16,128]{2,1,0:T(8,128)(2,1)S(1)}, u32[]{:S(2)}, u32[]{:S(2)}) collective-permute-start(bf16[8,16,128]{2,1,0:T(8,128)(2,1)S(1)} %get-tuple-element.76), channel_id=1, source_target_pairs={{1,0},{2,1},{3,2},{5,4},{6,5},{7,6},{9,8},{10,9},{11,10},{13,12},{... | collective-permute-start | bytes 98312 | tf_op jit(solution)/shard_map/ppermute | solution.py:142
  90.0 3.9 %collective-permute-start.14 = (bf16[8,16,128]{2,1,0:T(8,128)(2,1)S(1)}, bf16[8,16,128]{2,1,0:T(8,128)(2,1)S(1)}, u32[]{:S(2)}, u32[]{:S(2)}) collective-permute-start(bf16[8,16,128]{2,1,0:T(8,128)(2,1)S(1)} %get-tuple-element.76), channel_id=1, source_target_pairs={{0,1},{1,2},{2,3},{4,5},{5,6},{6,7},{8,9},{9,10},{10,11},{12,13},{... | collective-permute-start | bytes 98312 | tf_op jit(solution)/shard_map/ppermute | solution.py:142
  94.0 1.9 %collective-permute-done.14.left_ref = bf16[8,16,128]{2,1,0:T(8,128)(2,1)S(1)} collective-permute-done((bf16[8,16,128]{2,1,0:T(8,128)(2,1)S(1)}, bf16[8,16,128]{2,1,0:T(8,128)(2,1)S(1)}, u32[]{:S(2)}, u32[]{:S(2)}) %collective-permute-start.14) | collective-permute-done | bytes 32800 | tf_op jit(solution)/shard_map/ppermute | solution.py:142
  96.1 2.8 %collective-permute-start.17 = (bf16[8,16,128]{2,1,0:T(8,128)(2,1)S(1)}, bf16[8,16,128]{2,1,0:T(8,128)(2,1)S(1)}, u32[]{:S(2)}, u32[]{:S(2)}) collective-permute-start(bf16[8,16,128]{2,1,0:T(8,128)(2,1)S(1)} %get-tuple-element.78), channel_id=1, source_target_pairs={{4,0},{8,4},{12,8},{16,12},{20,16},{24,20},{28,24},{5,1},{9,5},{13... | collective-permute-start | bytes 98312 | tf_op jit(solution)/shard_map/ppermute | solution.py:142
  98.9 1.9 %collective-permute-start.16 = (bf16[8,16,128]{2,1,0:T(8,128)(2,1)S(1)}, bf16[8,16,128]{2,1,0:T(8,128)(2,1)S(1)}, u32[]{:S(2)}, u32[]{:S(2)}) collective-permute-start(bf16[8,16,128]{2,1,0:T(8,128)(2,1)S(1)} %get-tuple-element.78), channel_id=1, source_target_pairs={{0,4},{4,8},{8,12},{12,16},{16,20},{20,24},{24,28},{1,5},{5,9},{9,... | collective-permute-start | bytes 98312 | tf_op jit(solution)/shard_map/ppermute | solution.py:142
  100.9 4.2 %collective-permute-done.16.above_ref = bf16[8,16,128]{2,1,0:T(8,128)(2,1)S(1)} collective-permute-done((bf16[8,16,128]{2,1,0:T(8,128)(2,1)S(1)}, bf16[8,16,128]{2,1,0:T(8,128)(2,1)S(1)}, u32[]{:S(2)}, u32[]{:S(2)}) %collective-permute-start.16) | collective-permute-done | bytes 32800 | tf_op jit(solution)/shard_map/ppermute | solution.py:142
  105.1 1.8 %shard_map.70 = (f32[64,16,128]{2,1,0:T(8,128)}, f32[64,16,128]{2,1,0:T(8,128)}) custom-call(f32[64,16,128]{2,1,0:T(8,128)S(1)} %get-tuple-element.69.x_ref.residual_ref, f32[64,16,128]{2,1,0:T(8,128)S(1)} %get-tuple-element.70.before_ref, bf16[8,16,128]{2,1,0:T(8,128)(2,1)S(1)} %collective-permute-done.16.above_ref, ...), custom_call_target="tpu_custom_call" | custom-call | tf_op jit(solution)/shard_map/pallas_call | solution.py:27
  (30 shorter events, 2.9 us)
Async XLA Ops:
  0.6 1.6 %copy-start = (bf16[2,64,16,512]{3,2,1,0:T(8,128)(2,1)S(1)}, bf16[2,64,16,512]{3,2,1,0:T(8,128)(2,1)}, u32[]{:S(2)}) copy-start(bf16[2,64,16,512]{3,2,1,0:T(8,128)(2,1)} %in_ref.2) | copy-start | bytes 6291460
  2.2 9.1 %copy-start.1 = (bf16[2,64,16,512]{3,2,1,0:T(8,128)(2,1)S(1)}, bf16[2,64,16,512]{3,2,1,0:T(8,128)(2,1)}, u32[]{:S(2)}) copy-start(bf16[2,64,16,512]{3,2,1,0:T(8,128)(2,1)} %in_ref.2) | copy-start | bytes 6291460
  2.4 26.6 %copy-start.4 = (f32[64]{0:T(128)S(1)}, f32[64]{0:T(128)}, u32[]{:S(2)}) copy-start(f32[64]{0:T(128)} %param.6) | copy-start | bytes 772
  2.4 26.6 %copy-start.5 = (f32[64]{0:T(128)S(1)}, f32[64]{0:T(128)}, u32[]{:S(2)}) copy-start(f32[64]{0:T(128)} %param.7) | copy-start | bytes 772
  2.4 14.4 %collective-permute-start = (bf16[2,64,16,128]{3,2,1,0:T(8,128)(2,1)S(1)}, bf16[2,64,16,128]{3,2,1,0:T(8,128)(2,1)S(1)}, u32[]{:S(2)}, u32[]{:S(2)}) collective-permute-start(bf16[2,64,16,128]{3,2,1,0:T(8,128)(2,1)S(1)} %get-tuple-element.49), channel_id=1, source_target_pairs={{0,1},{1,2},{2,3},{3,0},{4,5},{5,6},{6,7},{7,4},{8,9},{9,10},{10,1... | collective-permute-start | bytes 1572872 | tf_op jit(solution)/shard_map/ppermute | solution.py:470
  4.1 1.0 copy-start.2
  5.4 11.4 %collective-permute-start.1 = (f32[4,16,128]{2,1,0:T(8,128)S(1)}, f32[4,16,128]{2,1,0:T(8,128)S(1)}, u32[]{:S(2)}, u32[]{:S(2)}) collective-permute-start(f32[4,16,128]{2,1,0:T(8,128)S(1)} %get-tuple-element.50), channel_id=1, source_target_pairs={{0,1},{1,2},{2,3},{4,5},{5,6},{6,7},{8,9},{9,10},{10,11},{12,13},{... | collective-permute-start | bytes 98312 | tf_op jit(solution)/shard_map/ppermute | solution.py:142
  7.8 9.1 %collective-permute-start.2 = (f32[4,16,128]{2,1,0:T(8,128)S(1)}, f32[4,16,128]{2,1,0:T(8,128)S(1)}, u32[]{:S(2)}, u32[]{:S(2)}) collective-permute-start(f32[4,16,128]{2,1,0:T(8,128)S(1)} %get-tuple-element.43), channel_id=1, source_target_pairs={{1,0},{2,1},{3,2},{5,4},{6,5},{7,6},{9,8},{10,9},{11,10},{13,12},{... | collective-permute-start | bytes 98312 | tf_op jit(solution)/shard_map/ppermute | solution.py:142
  16.9 39.1 %collective-permute-start.6 = (bf16[2,68,16,128]{3,2,1,0:T(8,128)(2,1)S(1)}, bf16[2,68,16,128]{3,2,1,0:T(8,128)(2,1)S(1)}, u32[]{:S(2)}, u32[]{:S(2)}) collective-permute-start(bf16[2,68,16,128]{3,2,1,0:T(8,128)(2,1)S(1)} %get-tuple-element.61), channel_id=1, source_target_pairs={{0,2},{1,3},{2,0},{3,1},{4,6},{5,7},{6,4},{7,5},{8,10},{9,11},{10,... | collective-permute-start | bytes 1671176 | tf_op jit(solution)/shard_map/ppermute | solution.py:470
  19.1 36.9 %collective-permute-start.7 = (bf16[2,68,16,128]{3,2,1,0:T(8,128)(2,1)S(1)}, bf16[2,68,16,128]{3,2,1,0:T(8,128)(2,1)S(1)}, u32[]{:S(2)}, u32[]{:S(2)}) collective-permute-start(bf16[2,68,16,128]{3,2,1,0:T(8,128)(2,1)S(1)} %get-tuple-element.62), channel_id=1, source_target_pairs={{0,3},{1,0},{2,1},{3,2},{4,7},{5,4},{6,5},{7,6},{8,11},{9,8},{10,9... | collective-permute-start | bytes 1671176 | tf_op jit(solution)/shard_map/ppermute | solution.py:470
  19.9 7.7 %collective-permute-start.3 = (f32[34,8,128]{2,1,0:T(8,128)S(1)}, f32[34,8,128]{2,1,0:T(8,128)S(1)}, u32[]{:S(2)}, u32[]{:S(2)}) collective-permute-start(f32[34,8,128]{2,1,0:T(8,128)S(1)} %get-tuple-element.54), channel_id=1, source_target_pairs={{0,4},{4,8},{8,12},{12,16},{16,20},{20,24},{24,28},{1,5},{5,9},{9,... | collective-permute-start | bytes 417800 | tf_op jit(solution)/shard_map/ppermute | solution.py:142
  21.9 7.1 %collective-permute-start.4 = (f32[34,8,128]{2,1,0:T(8,128)S(1)}, f32[34,8,128]{2,1,0:T(8,128)S(1)}, u32[]{:S(2)}, u32[]{:S(2)}) collective-permute-start(f32[34,8,128]{2,1,0:T(8,128)S(1)} %get-tuple-element.55), channel_id=1, source_target_pairs={{4,0},{8,4},{12,8},{16,12},{20,16},{24,20},{28,24},{5,1},{9,5},{13... | collective-permute-start | bytes 417800 | tf_op jit(solution)/shard_map/ppermute | solution.py:142
  26.4 29.5 %collective-permute-start.5 = (bf16[2,4,16,128]{3,2,1,0:T(8,128)(2,1)S(1)}, bf16[2,4,16,128]{3,2,1,0:T(8,128)(2,1)S(1)}, u32[]{:S(2)}, u32[]{:S(2)}) collective-permute-start(bf16[2,4,16,128]{3,2,1,0:T(8,128)(2,1)S(1)} %get-tuple-element.57), channel_id=1, source_target_pairs={{0,1},{1,2},{2,3},{3,0},{4,5},{5,6},{6,7},{7,4},{8,9},{9,10},{10,1... | collective-permute-start | bytes 98312 | tf_op jit(solution)/shard_map/ppermute | solution.py:470
  29.1 46.2 %copy-start.3 = (f32[64,16,128]{2,1,0:T(8,128)S(1)}, f32[64,16,128]{2,1,0:T(8,128)}, u32[]{:S(2)}) copy-start(f32[64,16,128]{2,1,0:T(8,128)} %residual_ref) | copy-start | bytes 1572868
  56.6 6.1 %collective-permute-start.9 = (bf16[8,16,128]{2,1,0:T(8,128)(2,1)S(1)}, bf16[8,16,128]{2,1,0:T(8,128)(2,1)S(1)}, u32[]{:S(2)}, u32[]{:S(2)}) collective-permute-start(bf16[8,16,128]{2,1,0:T(8,128)(2,1)S(1)} %get-tuple-element.63), channel_id=1, source_target_pairs={{1,0},{2,1},{3,2},{5,4},{6,5},{7,6},{9,8},{10,9},{11,10},{13,12},{... | collective-permute-start | bytes 98312 | tf_op jit(solution)/shard_map/ppermute | solution.py:142
  60.7 5.8 %collective-permute-start.8 = (bf16[8,16,128]{2,1,0:T(8,128)(2,1)S(1)}, bf16[8,16,128]{2,1,0:T(8,128)(2,1)S(1)}, u32[]{:S(2)}, u32[]{:S(2)}) collective-permute-start(bf16[8,16,128]{2,1,0:T(8,128)(2,1)S(1)} %get-tuple-element.63), channel_id=1, source_target_pairs={{0,1},{1,2},{2,3},{4,5},{5,6},{6,7},{8,9},{9,10},{10,11},{12,13},{... | collective-permute-start | bytes 98312 | tf_op jit(solution)/shard_map/ppermute | solution.py:142
  66.9 4.3 %collective-permute-start.11 = (bf16[16,16,128]{2,1,0:T(8,128)(2,1)S(1)}, bf16[16,16,128]{2,1,0:T(8,128)(2,1)S(1)}, u32[]{:S(2)}, u32[]{:S(2)}) collective-permute-start(bf16[16,16,128]{2,1,0:T(8,128)(2,1)S(1)} %get-tuple-element.65), channel_id=1, source_target_pairs={{4,0},{8,4},{12,8},{16,12},{20,16},{24,20},{28,24},{5,1},{9,5},{13... | collective-permute-start | bytes 196616 | tf_op jit(solution)/shard_map/ppermute | solution.py:142
  68.8 6.5 %collective-permute-start.10 = (bf16[16,16,128]{2,1,0:T(8,128)(2,1)S(1)}, bf16[16,16,128]{2,1,0:T(8,128)(2,1)S(1)}, u32[]{:S(2)}, u32[]{:S(2)}) collective-permute-start(bf16[16,16,128]{2,1,0:T(8,128)(2,1)S(1)} %get-tuple-element.65), channel_id=1, source_target_pairs={{0,4},{4,8},{8,12},{12,16},{16,20},{20,24},{24,28},{1,5},{5,9},{9,... | collective-permute-start | bytes 196616 | tf_op jit(solution)/shard_map/ppermute | solution.py:142
  76.3 9.0 %collective-permute-start.12 = (bf16[17,16,128]{2,1,0:T(8,128)(2,1)S(1)}, bf16[17,16,128]{2,1,0:T(8,128)(2,1)S(1)}, u32[]{:S(2)}, u32[]{:S(2)}) collective-permute-start(bf16[17,16,128]{2,1,0:T(8,128)(2,1)S(1)} %get-tuple-element.72), channel_id=1, source_target_pairs={{0,4},{4,8},{8,12},{12,16},{16,20},{20,24},{24,28},{1,5},{5,9},{9,... | collective-permute-start | bytes 208904 | tf_op jit(solution)/shard_map/ppermute | solution.py:142
  78.2 7.1 %collective-permute-start.13 = (bf16[17,16,128]{2,1,0:T(8,128)(2,1)S(1)}, bf16[17,16,128]{2,1,0:T(8,128)(2,1)S(1)}, u32[]{:S(2)}, u32[]{:S(2)}) collective-permute-start(bf16[17,16,128]{2,1,0:T(8,128)(2,1)S(1)} %get-tuple-element.73), channel_id=1, source_target_pairs={{4,0},{8,4},{12,8},{16,12},{20,16},{24,20},{28,24},{5,1},{9,5},{13... | collective-permute-start | bytes 208904 | tf_op jit(solution)/shard_map/ppermute | solution.py:142
  88.1 5.9 %collective-permute-start.15 = (bf16[8,16,128]{2,1,0:T(8,128)(2,1)S(1)}, bf16[8,16,128]{2,1,0:T(8,128)(2,1)S(1)}, u32[]{:S(2)}, u32[]{:S(2)}) collective-permute-start(bf16[8,16,128]{2,1,0:T(8,128)(2,1)S(1)} %get-tuple-element.76), channel_id=1, source_target_pairs={{1,0},{2,1},{3,2},{5,4},{6,5},{7,6},{9,8},{10,9},{11,10},{13,12},{... | collective-permute-start | bytes 98312 | tf_op jit(solution)/shard_map/ppermute | solution.py:142
  90.0 5.8 %collective-permute-start.14 = (bf16[8,16,128]{2,1,0:T(8,128)(2,1)S(1)}, bf16[8,16,128]{2,1,0:T(8,128)(2,1)S(1)}, u32[]{:S(2)}, u32[]{:S(2)}) collective-permute-start(bf16[8,16,128]{2,1,0:T(8,128)(2,1)S(1)} %get-tuple-element.76), channel_id=1, source_target_pairs={{0,1},{1,2},{2,3},{4,5},{5,6},{6,7},{8,9},{9,10},{10,11},{12,13},{... | collective-permute-start | bytes 98312 | tf_op jit(solution)/shard_map/ppermute | solution.py:142
  96.1 4.8 %collective-permute-start.17 = (bf16[8,16,128]{2,1,0:T(8,128)(2,1)S(1)}, bf16[8,16,128]{2,1,0:T(8,128)(2,1)S(1)}, u32[]{:S(2)}, u32[]{:S(2)}) collective-permute-start(bf16[8,16,128]{2,1,0:T(8,128)(2,1)S(1)} %get-tuple-element.78), channel_id=1, source_target_pairs={{4,0},{8,4},{12,8},{16,12},{20,16},{24,20},{28,24},{5,1},{9,5},{13... | collective-permute-start | bytes 98312 | tf_op jit(solution)/shard_map/ppermute | solution.py:142
  98.9 6.1 %collective-permute-start.16 = (bf16[8,16,128]{2,1,0:T(8,128)(2,1)S(1)}, bf16[8,16,128]{2,1,0:T(8,128)(2,1)S(1)}, u32[]{:S(2)}, u32[]{:S(2)}) collective-permute-start(bf16[8,16,128]{2,1,0:T(8,128)(2,1)S(1)} %get-tuple-element.78), channel_id=1, source_target_pairs={{0,4},{4,8},{8,12},{12,16},{16,20},{20,24},{24,28},{1,5},{5,9},{9,... | collective-permute-start | bytes 98312 | tf_op jit(solution)/shard_map/ppermute | solution.py:142

commit v4 on v3

--- a/solution.py
+++ b/solution.py
@@ -488,8 +488,10 @@
     first, last = call(columns_edge_body, (packed, packed), residual_in)
     left, right = shift(last, "member", 1), shift(first, "member", -1)
     members, first = lax.optimization_barrier((members, first))
-    later, early, left, right = lax.optimization_barrier((side_columns(members, parts), early, left, right))
-    blocks = [mine, early] + [turned(x, r) for r, x in enumerate(later[2:], 2)]
+    *later, final = side_columns(members, parts)
+    final = turned(final, parts - 1)
+    later, early, left, right = lax.optimization_barrier((later, early, left, right))
+    blocks = [mine, early] + [turned(x, r) for r, x in enumerate(later[2:], 2)] + [final]
     sides = [later[0], turned(later[1], 1)]
     around, top, bottom = call(rows_body, (packed, halo, halo), residual_in, left, right)
     above, below = shift(bottom, "tile", 1), shift(top, "tile", -1)

time: 108 us -> 105 us (0.972)
  starting transfers between devices: 45.6 us -> 44.3 us
    ppermute x4, waiting for transfers between devices: 22.1 us -> 20.7 us  [turned(): lax.ppermute(x, 'member', [(i, (i + step) % parts) for i in range(parts)])]
  transfers between devices with their start and end apart: 18 -> 18, of which waited for: 7 -> 8; matrix products, arithmetic and copies ran while one was open for 0% -> 0% of each run, Pallas kernels for 10% -> 11%
where the time goes in v4:
time: 105 us
  starting transfers between devices  44.3 us (42%)
  waiting for transfers between devices  38.4 us (37%)
  Pallas kernels  18.3 us (17%)
  local copies, waits for them, and re-layouts  2.79 us (3%)
    ppermute x14, starting transfers between devices, shift(): return lax.ppermute(x, axis, pairs)  39.2 us
    ppermute x4, waiting for transfers between devices, turned(): lax.ppermute(x, 'member', [(i, (i + step) % parts) for i in range(parts)])  20.7 us
    pallas_call x12, Pallas kernels, call(): pl.pallas_call(body, out_shape=out_shape, in_specs=in_specs or [VMEM] * l...  18.3 us
    ppermute x14, waiting for transfers between devices, shift(): return lax.ppermute(x, axis, pairs)  17.7 us
    ppermute x4, starting transfers between devices, turned(): lax.ppermute(x, 'member', [(i, (i + step) % parts) for i in range(parts)])  5.03 us
    unnamed x12, local copies, waits for them, and re-layouts  2.65 us
  transfers between devices with their start and end apart: 18, of which 8 were waited for; matrix products, arithmetic and copies ran while one was open for 0% of the time, Pallas kernels for 11%

profile of v4, /device:TPU:20, one launch (start us, length us, event | category | flops | bytes accessed | tf_op | source)
XLA Modules:
  0.0 104.6 jit_solution(15990443494896857704)
XLA Ops:
  0.6 1.6 %copy-done = bf16[2,64,16,512]{3,2,1,0:T(8,128)(2,1)S(1)} copy-done((bf16[2,64,16,512]{3,2,1,0:T(8,128)(2,1)S(1)}, bf16[2,64,16,512]{3,2,1,0:T(8,128)(2,1)}, u32[]{:S(2)}) %copy-start) | copy-done | bytes 2097176
  2.4 1.6 %collective-permute-start = (bf16[2,64,16,128]{3,2,1,0:T(8,128)(2,1)S(1)}, bf16[2,64,16,128]{3,2,1,0:T(8,128)(2,1)S(1)}, u32[]{:S(2)}, u32[]{:S(2)}) collective-permute-start(bf16[2,64,16,128]{3,2,1,0:T(8,128)(2,1)S(1)} %get-tuple-element.47), channel_id=1, source_target_pairs={{0,1},{1,2},{2,3},{3,0},{4,5},{5,6},{6,7},{7,4},{8,9},{9,10},{10,1... | collective-permute-start | bytes 1572872 | tf_op jit(solution)/shard_map/ppermute | solution.py:470
  4.1 1.0 copy-done.2
  5.4 2.3 %collective-permute-start.1 = (f32[4,16,128]{2,1,0:T(8,128)S(1)}, f32[4,16,128]{2,1,0:T(8,128)S(1)}, u32[]{:S(2)}, u32[]{:S(2)}) collective-permute-start(f32[4,16,128]{2,1,0:T(8,128)S(1)} %get-tuple-element.48), channel_id=1, source_target_pairs={{0,1},{1,2},{2,3},{4,5},{5,6},{6,7},{8,9},{9,10},{10,11},{12,13},{... | collective-permute-start | bytes 98312 | tf_op jit(solution)/shard_map/ppermute | solution.py:142
  7.8 3.5 %collective-permute-start.2 = (f32[4,16,128]{2,1,0:T(8,128)S(1)}, f32[4,16,128]{2,1,0:T(8,128)S(1)}, u32[]{:S(2)}, u32[]{:S(2)}) collective-permute-start(f32[4,16,128]{2,1,0:T(8,128)S(1)} %get-tuple-element.42), channel_id=1, source_target_pairs={{1,0},{2,1},{3,2},{5,4},{6,5},{7,6},{9,8},{10,9},{11,10},{13,12},{... | collective-permute-start | bytes 98312 | tf_op jit(solution)/shard_map/ppermute | solution.py:142
  11.3 3.6 %shard_map.61 = (bf16[2,4,16,128]{3,2,1,0:T(8,128)(2,1)S(1)}, bf16[2,4,16,128]{3,2,1,0:T(8,128)(2,1)S(1)}, bf16[2,68,16,128]{3,2,1,0:T(8,128)(2,1)S(1)}, bf16[2,68,16,128]{3,2,1,0:T(8,128)(2,1)S(1)}) custom-call(bf16[2,64,16,512]{3,2,1,0:T(8,128)(2,1)S(1)} %copy-done.1), custom_call_target="tpu_custom_call" | custom-call | tf_op jit(solution)/shard_map/pallas_call | solution.py:27
  15.4 1.5 %collective-permute-done.1.left_ref = f32[4,16,128]{2,1,0:T(8,128)S(1)} collective-permute-done((f32[4,16,128]{2,1,0:T(8,128)S(1)}, f32[4,16,128]{2,1,0:T(8,128)S(1)}, u32[]{:S(2)}, u32[]{:S(2)}) %collective-permute-start.1) | collective-permute-done | bytes 32800 | tf_op jit(solution)/shard_map/ppermute | solution.py:142
  16.9 2.3 %collective-permute-start.6 = (bf16[2,68,16,128]{3,2,1,0:T(8,128)(2,1)S(1)}, bf16[2,68,16,128]{3,2,1,0:T(8,128)(2,1)S(1)}, u32[]{:S(2)}, u32[]{:S(2)}) collective-permute-start(bf16[2,68,16,128]{3,2,1,0:T(8,128)(2,1)S(1)} %get-tuple-element.59), channel_id=1, source_target_pairs={{0,2},{1,3},{2,0},{3,1},{4,6},{5,7},{6,4},{7,5},{8,10},{9,11},{10,... | collective-permute-start | bytes 1671176 | tf_op jit(solution)/shard_map/ppermute | solution.py:470
  19.2 1.9 %collective-permute-start.3 = (f32[34,8,128]{2,1,0:T(8,128)S(1)}, f32[34,8,128]{2,1,0:T(8,128)S(1)}, u32[]{:S(2)}, u32[]{:S(2)}) collective-permute-start(f32[34,8,128]{2,1,0:T(8,128)S(1)} %get-tuple-element.52), channel_id=1, source_target_pairs={{0,4},{4,8},{8,12},{12,16},{16,20},{20,24},{24,28},{1,5},{5,9},{9,... | collective-permute-start | bytes 417800 | tf_op jit(solution)/shard_map/ppermute | solution.py:142
  21.1 4.5 %collective-permute-start.4 = (f32[34,8,128]{2,1,0:T(8,128)S(1)}, f32[34,8,128]{2,1,0:T(8,128)S(1)}, u32[]{:S(2)}, u32[]{:S(2)}) collective-permute-start(f32[34,8,128]{2,1,0:T(8,128)S(1)} %get-tuple-element.53), channel_id=1, source_target_pairs={{4,0},{8,4},{12,8},{16,12},{20,16},{24,20},{28,24},{5,1},{9,5},{13... | collective-permute-start | bytes 417800 | tf_op jit(solution)/shard_map/ppermute | solution.py:142
  26.5 1.8 %collective-permute-done.4.below_ref = f32[34,8,128]{2,1,0:T(8,128)S(1)} collective-permute-done((f32[34,8,128]{2,1,0:T(8,128)S(1)}, f32[34,8,128]{2,1,0:T(8,128)S(1)}, u32[]{:S(2)}, u32[]{:S(2)}) %collective-permute-start.4) | collective-permute-done | bytes 139296 | tf_op jit(solution)/shard_map/ppermute | solution.py:142
  28.4 4.8 %shard_map.63.grad_ref = f32[64,16,128]{2,1,0:T(8,128)S(1)} custom-call(f32[64,128]{1,0:T(8,128)S(1)} %broadcast_in_dim.4.wx_ref, f32[64,128]{1,0:T(8,128)S(1)} %broadcast_in_dim.5.wy_ref, f32[64,16,128]{2,1,0:T(8,128)S(1)} %copy-done.2, f32[4,16,128]{2,1,0:T(8,128)S(1)} %get-tuple-element.51.beside_ref.around_ref, ...), custom_call_target="tpu_custom_call" | custom-call | tf_op jit(solution)/shard_map/pallas_call | solution.py:27
  33.2 20.7 %collective-permute-done.5.refs_5_ = bf16[2,4,16,128]{3,2,1,0:T(8,128)(2,1)S(1)} collective-permute-done((bf16[2,4,16,128]{3,2,1,0:T(8,128)(2,1)S(1)}, bf16[2,4,16,128]{3,2,1,0:T(8,128)(2,1)S(1)}, u32[]{:S(2)}, u32[]{:S(2)}) %collective-permute-start.5) | collective-permute-done | bytes 32800 | tf_op jit(solution)/shard_map/ppermute | solution.py:470
  53.8 0.6 shard_map.64
  54.5 1.9 %collective-permute-start.9 = (bf16[8,16,128]{2,1,0:T(8,128)(2,1)S(1)}, bf16[8,16,128]{2,1,0:T(8,128)(2,1)S(1)}, u32[]{:S(2)}, u32[]{:S(2)}) collective-permute-start(bf16[8,16,128]{2,1,0:T(8,128)(2,1)S(1)} %get-tuple-element.61), channel_id=1, source_target_pairs={{1,0},{2,1},{3,2},{5,4},{6,5},{7,6},{9,8},{10,9},{11,10},{13,12},{... | collective-permute-start | bytes 98312 | tf_op jit(solution)/shard_map/ppermute | solution.py:142
  56.4 3.9 %collective-permute-start.8 = (bf16[8,16,128]{2,1,0:T(8,128)(2,1)S(1)}, bf16[8,16,128]{2,1,0:T(8,128)(2,1)S(1)}, u32[]{:S(2)}, u32[]{:S(2)}) collective-permute-start(bf16[8,16,128]{2,1,0:T(8,128)(2,1)S(1)} %get-tuple-element.61), channel_id=1, source_target_pairs={{0,1},{1,2},{2,3},{4,5},{5,6},{6,7},{8,9},{9,10},{10,11},{12,13},{... | collective-permute-start | bytes 98312 | tf_op jit(solution)/shard_map/ppermute | solution.py:142
  60.3 2.1 %collective-permute-done.8.left_ref = bf16[8,16,128]{2,1,0:T(8,128)(2,1)S(1)} collective-permute-done((bf16[8,16,128]{2,1,0:T(8,128)(2,1)S(1)}, bf16[8,16,128]{2,1,0:T(8,128)(2,1)S(1)}, u32[]{:S(2)}, u32[]{:S(2)}) %collective-permute-start.8) | collective-permute-done | bytes 32800 | tf_op jit(solution)/shard_map/ppermute | solution.py:142
  62.9 1.9 %collective-permute-start.11 = (bf16[16,16,128]{2,1,0:T(8,128)(2,1)S(1)}, bf16[16,16,128]{2,1,0:T(8,128)(2,1)S(1)}, u32[]{:S(2)}, u32[]{:S(2)}) collective-permute-start(bf16[16,16,128]{2,1,0:T(8,128)(2,1)S(1)} %get-tuple-element.63), channel_id=1, source_target_pairs={{4,0},{8,4},{12,8},{16,12},{20,16},{24,20},{28,24},{5,1},{9,5},{13... | collective-permute-start | bytes 196616 | tf_op jit(solution)/shard_map/ppermute | solution.py:142
  64.8 2.4 %collective-permute-start.10 = (bf16[16,16,128]{2,1,0:T(8,128)(2,1)S(1)}, bf16[16,16,128]{2,1,0:T(8,128)(2,1)S(1)}, u32[]{:S(2)}, u32[]{:S(2)}) collective-permute-start(bf16[16,16,128]{2,1,0:T(8,128)(2,1)S(1)} %get-tuple-element.63), channel_id=1, source_target_pairs={{0,4},{4,8},{8,12},{12,16},{16,20},{20,24},{24,28},{1,5},{5,9},{9,... | collective-permute-start | bytes 196616 | tf_op jit(solution)/shard_map/ppermute | solution.py:142
  67.2 4.1 %collective-permute-done.10.above_ref = bf16[16,16,128]{2,1,0:T(8,128)(2,1)S(1)} collective-permute-done((bf16[16,16,128]{2,1,0:T(8,128)(2,1)S(1)}, bf16[16,16,128]{2,1,0:T(8,128)(2,1)S(1)}, u32[]{:S(2)}, u32[]{:S(2)}) %collective-permute-start.10) | collective-permute-done | bytes 65568 | tf_op jit(solution)/shard_map/ppermute | solution.py:142
  71.3 1.0 shard_map.66
  72.2 1.9 %collective-permute-start.12 = (bf16[17,16,128]{2,1,0:T(8,128)(2,1)S(1)}, bf16[17,16,128]{2,1,0:T(8,128)(2,1)S(1)}, u32[]{:S(2)}, u32[]{:S(2)}) collective-permute-start(bf16[17,16,128]{2,1,0:T(8,128)(2,1)S(1)} %get-tuple-element.70), channel_id=1, source_target_pairs={{0,4},{4,8},{8,12},{12,16},{16,20},{20,24},{24,28},{1,5},{5,9},{9,... | collective-permute-start | bytes 208904 | tf_op jit(solution)/shard_map/ppermute | solution.py:142
  74.2 4.5 %collective-permute-start.13 = (bf16[17,16,128]{2,1,0:T(8,128)(2,1)S(1)}, bf16[17,16,128]{2,1,0:T(8,128)(2,1)S(1)}, u32[]{:S(2)}, u32[]{:S(2)}) collective-permute-start(bf16[17,16,128]{2,1,0:T(8,128)(2,1)S(1)} %get-tuple-element.71), channel_id=1, source_target_pairs={{4,0},{8,4},{12,8},{16,12},{20,16},{24,20},{28,24},{5,1},{9,5},{13... | collective-permute-start | bytes 208904 | tf_op jit(solution)/shard_map/ppermute | solution.py:142
  78.7 2.5 %shard_map.67 = (f32[64,16,128]{2,1,0:T(8,128)S(1)}, f32[4,12,3,8,128]{4,3,2,1,0:T(8,128)S(1)}) custom-call(f32[64,128]{1,0:T(8,128)S(1)} %broadcast_in_dim.4.wx_ref, f32[64,128]{1,0:T(8,128)S(1)} %broadcast_in_dim.5.wy_ref, f32[64,16,128]{2,1,0:T(8,128)S(1)} %get-tuple-element.67.x_ref.residual_ref, f32[4,16,128]{2,1,0:T(8,128)S(1)} %get-tuple-element.69.beside_ref), custom_call_target="tpu_custom_call" | custom-call | tf_op jit(solution)/shard_map/pallas_call | solution.py:27
  81.3 2.8 %shard_map.68 = (f32[8,16,128]{2,1,0:T(8,128)S(1)}, bf16[8,16,128]{2,1,0:T(8,128)(2,1)S(1)}) custom-call(f32[64,128]{1,0:T(8,128)S(1)} %broadcast_in_dim.4.wx_ref, f32[64,128]{1,0:T(8,128)S(1)} %broadcast_in_dim.5.wy_ref, f32[64,16,128]{2,1,0:T(8,128)S(1)} %get-tuple-element.67.x_ref.residual_ref, f32[4,16,128]{2,1,0:T(8,128)S(1)} %get-tuple-element.69.beside_ref, ...), custom_call_target="tpu_custom_call" | custom-call | tf_op jit(solution)/shard_map/pallas_call | solution.py:27
  84.1 3.9 %collective-permute-start.15 = (bf16[8,16,128]{2,1,0:T(8,128)(2,1)S(1)}, bf16[8,16,128]{2,1,0:T(8,128)(2,1)S(1)}, u32[]{:S(2)}, u32[]{:S(2)}) collective-permute-start(bf16[8,16,128]{2,1,0:T(8,128)(2,1)S(1)} %get-tuple-element.74), channel_id=1, source_target_pairs={{1,0},{2,1},{3,2},{5,4},{6,5},{7,6},{9,8},{10,9},{11,10},{13,12},{... | collective-permute-start | bytes 98312 | tf_op jit(solution)/shard_map/ppermute | solution.py:142
  88.0 1.9 %collective-permute-start.14 = (bf16[8,16,128]{2,1,0:T(8,128)(2,1)S(1)}, bf16[8,16,128]{2,1,0:T(8,128)(2,1)S(1)}, u32[]{:S(2)}, u32[]{:S(2)}) collective-permute-start(bf16[8,16,128]{2,1,0:T(8,128)(2,1)S(1)} %get-tuple-element.74), channel_id=1, source_target_pairs={{0,1},{1,2},{2,3},{4,5},{5,6},{6,7},{8,9},{9,10},{10,11},{12,13},{... | collective-permute-start | bytes 98312 | tf_op jit(solution)/shard_map/ppermute | solution.py:142
  89.9 3.9 %collective-permute-done.14.left_ref = bf16[8,16,128]{2,1,0:T(8,128)(2,1)S(1)} collective-permute-done((bf16[8,16,128]{2,1,0:T(8,128)(2,1)S(1)}, bf16[8,16,128]{2,1,0:T(8,128)(2,1)S(1)}, u32[]{:S(2)}, u32[]{:S(2)}) %collective-permute-start.14) | collective-permute-done | bytes 32800 | tf_op jit(solution)/shard_map/ppermute | solution.py:142
  94.1 2.5 %collective-permute-start.17 = (bf16[8,16,128]{2,1,0:T(8,128)(2,1)S(1)}, bf16[8,16,128]{2,1,0:T(8,128)(2,1)S(1)}, u32[]{:S(2)}, u32[]{:S(2)}) collective-permute-start(bf16[8,16,128]{2,1,0:T(8,128)(2,1)S(1)} %get-tuple-element.76), channel_id=1, source_target_pairs={{4,0},{8,4},{12,8},{16,12},{20,16},{24,20},{28,24},{5,1},{9,5},{13... | collective-permute-start | bytes 98312 | tf_op jit(solution)/shard_map/ppermute | solution.py:142
  96.6 1.9 %collective-permute-start.16 = (bf16[8,16,128]{2,1,0:T(8,128)(2,1)S(1)}, bf16[8,16,128]{2,1,0:T(8,128)(2,1)S(1)}, u32[]{:S(2)}, u32[]{:S(2)}) collective-permute-start(bf16[8,16,128]{2,1,0:T(8,128)(2,1)S(1)} %get-tuple-element.76), channel_id=1, source_target_pairs={{0,4},{4,8},{8,12},{12,16},{16,20},{20,24},{24,28},{1,5},{5,9},{9,... | collective-permute-start | bytes 98312 | tf_op jit(solution)/shard_map/ppermute | solution.py:142
  98.6 4.2 %collective-permute-done.16.above_ref = bf16[8,16,128]{2,1,0:T(8,128)(2,1)S(1)} collective-permute-done((bf16[8,16,128]{2,1,0:T(8,128)(2,1)S(1)}, bf16[8,16,128]{2,1,0:T(8,128)(2,1)S(1)}, u32[]{:S(2)}, u32[]{:S(2)}) %collective-permute-start.16) | collective-permute-done | bytes 32800 | tf_op jit(solution)/shard_map/ppermute | solution.py:142
  102.8 1.8 %shard_map.70 = (f32[64,16,128]{2,1,0:T(8,128)}, f32[64,16,128]{2,1,0:T(8,128)}) custom-call(f32[64,16,128]{2,1,0:T(8,128)S(1)} %get-tuple-element.67.x_ref.residual_ref, f32[64,16,128]{2,1,0:T(8,128)S(1)} %get-tuple-element.68.before_ref, bf16[8,16,128]{2,1,0:T(8,128)(2,1)S(1)} %collective-permute-done.16.above_ref, ...), custom_call_target="tpu_custom_call" | custom-call | tf_op jit(solution)/shard_map/pallas_call | solution.py:27
  (30 shorter events, 2.7 us)
Async XLA Ops:
  0.6 1.6 %copy-start = (bf16[2,64,16,512]{3,2,1,0:T(8,128)(2,1)S(1)}, bf16[2,64,16,512]{3,2,1,0:T(8,128)(2,1)}, u32[]{:S(2)}) copy-start(bf16[2,64,16,512]{3,2,1,0:T(8,128)(2,1)} %in_ref.2) | copy-start | bytes 6291460
  2.2 9.1 %copy-start.1 = (bf16[2,64,16,512]{3,2,1,0:T(8,128)(2,1)S(1)}, bf16[2,64,16,512]{3,2,1,0:T(8,128)(2,1)}, u32[]{:S(2)}) copy-start(bf16[2,64,16,512]{3,2,1,0:T(8,128)(2,1)} %in_ref.2) | copy-start | bytes 6291460
  2.4 25.8 %copy-start.4 = (f32[64]{0:T(128)S(1)}, f32[64]{0:T(128)}, u32[]{:S(2)}) copy-start(f32[64]{0:T(128)} %param.6) | copy-start | bytes 772
  2.4 25.9 %copy-start.5 = (f32[64]{0:T(128)S(1)}, f32[64]{0:T(128)}, u32[]{:S(2)}) copy-start(f32[64]{0:T(128)} %param.7) | copy-start | bytes 772
  2.4 14.4 %collective-permute-start = (bf16[2,64,16,128]{3,2,1,0:T(8,128)(2,1)S(1)}, bf16[2,64,16,128]{3,2,1,0:T(8,128)(2,1)S(1)}, u32[]{:S(2)}, u32[]{:S(2)}) collective-permute-start(bf16[2,64,16,128]{3,2,1,0:T(8,128)(2,1)S(1)} %get-tuple-element.47), channel_id=1, source_target_pairs={{0,1},{1,2},{2,3},{3,0},{4,5},{5,6},{6,7},{7,4},{8,9},{9,10},{10,1... | collective-permute-start | bytes 1572872 | tf_op jit(solution)/shard_map/ppermute | solution.py:470
  4.1 1.0 copy-start.2
  5.4 11.4 %collective-permute-start.1 = (f32[4,16,128]{2,1,0:T(8,128)S(1)}, f32[4,16,128]{2,1,0:T(8,128)S(1)}, u32[]{:S(2)}, u32[]{:S(2)}) collective-permute-start(f32[4,16,128]{2,1,0:T(8,128)S(1)} %get-tuple-element.48), channel_id=1, source_target_pairs={{0,1},{1,2},{2,3},{4,5},{5,6},{6,7},{8,9},{9,10},{10,11},{12,13},{... | collective-permute-start | bytes 98312 | tf_op jit(solution)/shard_map/ppermute | solution.py:142
  7.8 9.1 %collective-permute-start.2 = (f32[4,16,128]{2,1,0:T(8,128)S(1)}, f32[4,16,128]{2,1,0:T(8,128)S(1)}, u32[]{:S(2)}, u32[]{:S(2)}) collective-permute-start(f32[4,16,128]{2,1,0:T(8,128)S(1)} %get-tuple-element.42), channel_id=1, source_target_pairs={{1,0},{2,1},{3,2},{5,4},{6,5},{7,6},{9,8},{10,9},{11,10},{13,12},{... | collective-permute-start | bytes 98312 | tf_op jit(solution)/shard_map/ppermute | solution.py:142
  14.9 38.9 %collective-permute-start.7 = (bf16[2,68,16,128]{3,2,1,0:T(8,128)(2,1)S(1)}, bf16[2,68,16,128]{3,2,1,0:T(8,128)(2,1)S(1)}, u32[]{:S(2)}, u32[]{:S(2)}) collective-permute-start(bf16[2,68,16,128]{3,2,1,0:T(8,128)(2,1)S(1)} %get-tuple-element.60), channel_id=1, source_target_pairs={{0,3},{1,0},{2,1},{3,2},{4,7},{5,4},{6,5},{7,6},{8,11},{9,8},{10,9... | collective-permute-start | bytes 1671176 | tf_op jit(solution)/shard_map/ppermute | solution.py:470
  16.9 37.0 %collective-permute-start.6 = (bf16[2,68,16,128]{3,2,1,0:T(8,128)(2,1)S(1)}, bf16[2,68,16,128]{3,2,1,0:T(8,128)(2,1)S(1)}, u32[]{:S(2)}, u32[]{:S(2)}) collective-permute-start(bf16[2,68,16,128]{3,2,1,0:T(8,128)(2,1)S(1)} %get-tuple-element.59), channel_id=1, source_target_pairs={{0,2},{1,3},{2,0},{3,1},{4,6},{5,7},{6,4},{7,5},{8,10},{9,11},{10,... | collective-permute-start | bytes 1671176 | tf_op jit(solution)/shard_map/ppermute | solution.py:470
  19.2 7.3 %collective-permute-start.3 = (f32[34,8,128]{2,1,0:T(8,128)S(1)}, f32[34,8,128]{2,1,0:T(8,128)S(1)}, u32[]{:S(2)}, u32[]{:S(2)}) collective-permute-start(f32[34,8,128]{2,1,0:T(8,128)S(1)} %get-tuple-element.52), channel_id=1, source_target_pairs={{0,4},{4,8},{8,12},{12,16},{16,20},{20,24},{24,28},{1,5},{5,9},{9,... | collective-permute-start | bytes 417800 | tf_op jit(solution)/shard_map/ppermute | solution.py:142
  21.1 7.1 %collective-permute-start.4 = (f32[34,8,128]{2,1,0:T(8,128)S(1)}, f32[34,8,128]{2,1,0:T(8,128)S(1)}, u32[]{:S(2)}, u32[]{:S(2)}) collective-permute-start(f32[34,8,128]{2,1,0:T(8,128)S(1)} %get-tuple-element.53), channel_id=1, source_target_pairs={{4,0},{8,4},{12,8},{16,12},{20,16},{24,20},{28,24},{5,1},{9,5},{13... | collective-permute-start | bytes 417800 | tf_op jit(solution)/shard_map/ppermute | solution.py:142
  25.7 28.1 %collective-permute-start.5 = (bf16[2,4,16,128]{3,2,1,0:T(8,128)(2,1)S(1)}, bf16[2,4,16,128]{3,2,1,0:T(8,128)(2,1)S(1)}, u32[]{:S(2)}, u32[]{:S(2)}) collective-permute-start(bf16[2,4,16,128]{3,2,1,0:T(8,128)(2,1)S(1)} %get-tuple-element.55), channel_id=1, source_target_pairs={{0,1},{1,2},{2,3},{3,0},{4,5},{5,6},{6,7},{7,4},{8,9},{9,10},{10,1... | collective-permute-start | bytes 98312 | tf_op jit(solution)/shard_map/ppermute | solution.py:470
  28.4 42.9 %copy-start.3 = (f32[64,16,128]{2,1,0:T(8,128)S(1)}, f32[64,16,128]{2,1,0:T(8,128)}, u32[]{:S(2)}) copy-start(f32[64,16,128]{2,1,0:T(8,128)} %residual_ref) | copy-start | bytes 1572868
  54.5 5.9 %collective-permute-start.9 = (bf16[8,16,128]{2,1,0:T(8,128)(2,1)S(1)}, bf16[8,16,128]{2,1,0:T(8,128)(2,1)S(1)}, u32[]{:S(2)}, u32[]{:S(2)}) collective-permute-start(bf16[8,16,128]{2,1,0:T(8,128)(2,1)S(1)} %get-tuple-element.61), channel_id=1, source_target_pairs={{1,0},{2,1},{3,2},{5,4},{6,5},{7,6},{9,8},{10,9},{11,10},{13,12},{... | collective-permute-start | bytes 98312 | tf_op jit(solution)/shard_map/ppermute | solution.py:142
  56.4 6.1 %collective-permute-start.8 = (bf16[8,16,128]{2,1,0:T(8,128)(2,1)S(1)}, bf16[8,16,128]{2,1,0:T(8,128)(2,1)S(1)}, u32[]{:S(2)}, u32[]{:S(2)}) collective-permute-start(bf16[8,16,128]{2,1,0:T(8,128)(2,1)S(1)} %get-tuple-element.61), channel_id=1, source_target_pairs={{0,1},{1,2},{2,3},{4,5},{5,6},{6,7},{8,9},{9,10},{10,11},{12,13},{... | collective-permute-start | bytes 98312 | tf_op jit(solution)/shard_map/ppermute | solution.py:142
  62.9 4.3 %collective-permute-start.11 = (bf16[16,16,128]{2,1,0:T(8,128)(2,1)S(1)}, bf16[16,16,128]{2,1,0:T(8,128)(2,1)S(1)}, u32[]{:S(2)}, u32[]{:S(2)}) collective-permute-start(bf16[16,16,128]{2,1,0:T(8,128)(2,1)S(1)} %get-tuple-element.63), channel_id=1, source_target_pairs={{4,0},{8,4},{12,8},{16,12},{20,16},{24,20},{28,24},{5,1},{9,5},{13... | collective-permute-start | bytes 196616 | tf_op jit(solution)/shard_map/ppermute | solution.py:142
  64.8 6.5 %collective-permute-start.10 = (bf16[16,16,128]{2,1,0:T(8,128)(2,1)S(1)}, bf16[16,16,128]{2,1,0:T(8,128)(2,1)S(1)}, u32[]{:S(2)}, u32[]{:S(2)}) collective-permute-start(bf16[16,16,128]{2,1,0:T(8,128)(2,1)S(1)} %get-tuple-element.63), channel_id=1, source_target_pairs={{0,4},{4,8},{8,12},{12,16},{16,20},{20,24},{24,28},{1,5},{5,9},{9,... | collective-permute-start | bytes 196616 | tf_op jit(solution)/shard_map/ppermute | solution.py:142
  72.2 9.0 %collective-permute-start.12 = (bf16[17,16,128]{2,1,0:T(8,128)(2,1)S(1)}, bf16[17,16,128]{2,1,0:T(8,128)(2,1)S(1)}, u32[]{:S(2)}, u32[]{:S(2)}) collective-permute-start(bf16[17,16,128]{2,1,0:T(8,128)(2,1)S(1)} %get-tuple-element.70), channel_id=1, source_target_pairs={{0,4},{4,8},{8,12},{12,16},{16,20},{20,24},{24,28},{1,5},{5,9},{9,... | collective-permute-start | bytes 208904 | tf_op jit(solution)/shard_map/ppermute | solution.py:142
  74.2 7.1 %collective-permute-start.13 = (bf16[17,16,128]{2,1,0:T(8,128)(2,1)S(1)}, bf16[17,16,128]{2,1,0:T(8,128)(2,1)S(1)}, u32[]{:S(2)}, u32[]{:S(2)}) collective-permute-start(bf16[17,16,128]{2,1,0:T(8,128)(2,1)S(1)} %get-tuple-element.71), channel_id=1, source_target_pairs={{4,0},{8,4},{12,8},{16,12},{20,16},{24,20},{28,24},{5,1},{9,5},{13... | collective-permute-start | bytes 208904 | tf_op jit(solution)/shard_map/ppermute | solution.py:142
  84.1 5.9 %collective-permute-start.15 = (bf16[8,16,128]{2,1,0:T(8,128)(2,1)S(1)}, bf16[8,16,128]{2,1,0:T(8,128)(2,1)S(1)}, u32[]{:S(2)}, u32[]{:S(2)}) collective-permute-start(bf16[8,16,128]{2,1,0:T(8,128)(2,1)S(1)} %get-tuple-element.74), channel_id=1, source_target_pairs={{1,0},{2,1},{3,2},{5,4},{6,5},{7,6},{9,8},{10,9},{11,10},{13,12},{... | collective-permute-start | bytes 98312 | tf_op jit(solution)/shard_map/ppermute | solution.py:142
  88.0 5.8 %collective-permute-start.14 = (bf16[8,16,128]{2,1,0:T(8,128)(2,1)S(1)}, bf16[8,16,128]{2,1,0:T(8,128)(2,1)S(1)}, u32[]{:S(2)}, u32[]{:S(2)}) collective-permute-start(bf16[8,16,128]{2,1,0:T(8,128)(2,1)S(1)} %get-tuple-element.74), channel_id=1, source_target_pairs={{0,1},{1,2},{2,3},{4,5},{5,6},{6,7},{8,9},{9,10},{10,11},{12,13},{... | collective-permute-start | bytes 98312 | tf_op jit(solution)/shard_map/ppermute | solution.py:142
  94.1 4.5 %collective-permute-start.17 = (bf16[8,16,128]{2,1,0:T(8,128)(2,1)S(1)}, bf16[8,16,128]{2,1,0:T(8,128)(2,1)S(1)}, u32[]{:S(2)}, u32[]{:S(2)}) collective-permute-start(bf16[8,16,128]{2,1,0:T(8,128)(2,1)S(1)} %get-tuple-element.76), channel_id=1, source_target_pairs={{4,0},{8,4},{12,8},{16,12},{20,16},{24,20},{28,24},{5,1},{9,5},{13... | collective-permute-start | bytes 98312 | tf_op jit(solution)/shard_map/ppermute | solution.py:142
  96.6 6.1 %collective-permute-start.16 = (bf16[8,16,128]{2,1,0:T(8,128)(2,1)S(1)}, bf16[8,16,128]{2,1,0:T(8,128)(2,1)S(1)}, u32[]{:S(2)}, u32[]{:S(2)}) collective-permute-start(bf16[8,16,128]{2,1,0:T(8,128)(2,1)S(1)} %get-tuple-element.76), channel_id=1, source_target_pairs={{0,4},{4,8},{8,12},{12,16},{16,20},{20,24},{24,28},{1,5},{5,9},{9,... | collective-permute-start | bytes 98312 | tf_op jit(solution)/shard_map/ppermute | solution.py:142

commit v5 on v4

--- a/solution.py
+++ b/solution.py
@@ -321,14 +321,29 @@
     outer_sweep(x_ref, model_parts(wx_ref, wy_ref, x_ref, above_ref, below_ref, side_row, grad_ref), kept_ref)
     row = sub_iota((rows, cols))
     inside = (row >= MODEL_STEPS) & (row < rows - MODEL_STEPS)
-    project_levels(lambda level: jnp.where(inside, inner_ref[level], grad_ref[level]), levels, *others)
-
-
-def project_body(grad_ref, *refs):
-    project_levels(lambda level: grad_ref[level], grad_ref.shape[0], *refs)
-
-
-def project_levels(grad, levels, *refs):
+    project_levels(lambda level: jnp.where(inside, inner_ref[level], grad_ref[level]), levels, list(range(len(others) - 2)), *others)
+
+
+def near_turns(parts):
+    return [0, 1, parts - 1]
+
+
+def first_project_body(parts, grad_ref, *refs):
+    project_levels(lambda level: grad_ref[level], grad_ref.shape[0], near_turns(parts), *refs)
+
+
+def last_project_body(parts, grad_ref, wide_in_ref, thin_in_ref, *refs):
+    *member_refs, wide_ref, thin_ref = refs
+    own = member_refs[0].shape[0]
+    for r in near_turns(parts):
+        for m in range(own):
+            at = neighbor_of(-r) * own + m
+            wide_ref[at] = wide_in_ref[at]
+            thin_ref[at] = thin_in_ref[at]
+    project_levels(lambda level: grad_ref[level], grad_ref.shape[0], list(range(2, parts - 1)), *refs)
+
+
+def project_levels(grad, levels, turns, *refs):
     *member_refs, wide_ref, thin_ref = refs
     own, _, rows, cols = member_refs[0].shape
     count = len(member_refs) * own
@@ -343,7 +358,7 @@
 
     total = lax.fori_loop(0, levels // 2, step, (jnp.zeros((rows, cols), F32),) * count)
     for m in range(count):
-        at = neighbor_of(-(m // own)) * own + m % own
+        at = neighbor_of(-turns[m // own]) * own + m % own
         wide_ref[at] = total[m]
         thin_ref[at] = total[m].astype(BF16)
 
@@ -396,7 +411,7 @@
     return [out[:, m * cols : (m + 1) * cols] for m in range(count)]
 
 
-def increments(member_refs, local_ref, levels, emit):
+def increments(member_refs, local_ref, start, levels, emit):
     own = member_refs[0].shape[0]
     count = len(member_refs) * own
     local = [local_ref[neighbor_of(-(m // own)) * own + m % own] for m in range(count)]
@@ -410,7 +425,7 @@
             emit(level, total)
         return carry
 
-    lax.fori_loop(0, levels // 2, step, 0)
+    lax.fori_loop(start // 2, (start + levels) // 2, step, 0)
 
 
 def update_body(parts, residual_ref, around_ref, above_ref, mid_ref, below_ref, *refs):
@@ -426,7 +441,7 @@
         analysis_ref[level] = value
         out_ref[level] = residual_ref[level] - RELAX * value
 
-    increments(member_refs, local_ref, levels, emit)
+    increments(member_refs, local_ref, 0, levels, emit)
     for g in range(levels // GROUP):
         total = jnp.zeros((rows, LANES), F32)
         for m in range(count):
@@ -443,7 +458,8 @@
 
 def final_body(parts, residual_ref, before_ref, above_ref, mid_ref, below_ref, *refs):
     member_refs = refs[:parts]
-    analysis_ref, out_ref, local_ref = refs[parts:]
+    analysis_out_ref, residual_out_ref, local_ref, analysis_ref, out_ref, sems = refs[parts:]
+    levels = residual_ref.shape[0]
     for m, value in enumerate(smooth_rows(above_ref, mid_ref, below_ref)):
         local_ref[m] = value
 
@@ -451,7 +467,17 @@
         analysis_ref[level] = before_ref[level] + value
         out_ref[level] = residual_ref[level] - RELAX * value
 
-    increments(member_refs, local_ref, residual_ref.shape[0], emit)
+    pieces = sems.shape[1]
+    count = levels // pieces
+    copies = []
+    for i in range(pieces):
+        increments(member_refs, local_ref, i * count, count, emit)
+        at = pl.ds(i * count, count)
+        for j, (source, target) in enumerate(((analysis_ref, analysis_out_ref), (out_ref, residual_out_ref))):
+            copies.append(pltpu.make_async_copy(source.at[at], target.at[at], sems.at[j, i]))
+            copies[-1].start()
+    for copy in copies:
+        copy.wait()
 
 
 def per_device(residual_in, members, wind_x, wind_y):
@@ -500,8 +526,10 @@
         wind_x, wind_y, residual_in, around, above, below, in_specs=[VMEM] * 6,
     )
     grad, sides = lax.optimization_barrier((grad, sides))
+    near = [blocks[r] for r in near_turns(parts)]
+    wide, thin = call(functools.partial(first_project_body, parts), both(count, rows, cols), grad, *near)
     wide, thin = call(
-        project_body, both(count, rows, cols), grad, *blocks, in_specs=[VMEM] * (1 + parts)
+        functools.partial(last_project_body, parts), both(count, rows, cols), grad, wide, thin, *blocks[2:-1]
     )
 
     analysis, residual, beside, top, bottom = call(
@@ -518,11 +546,19 @@
         wind_x, wind_y, residual, beside, above, below, inner, kept, *blocks,
         scratch=[pltpu.VMEM((levels, rows, cols), F32)] + wide_halo,
     )
-    return call(
-        functools.partial(final_body, parts), (like, like),
-        residual, analysis, *smoothed(wide, thin, count), *blocks,
-        in_specs=[VMEM] * (5 + parts), scratch=[pltpu.VMEM((count, rows, cols), F32)],
-    )
+    return pl.pallas_call(
+        functools.partial(final_body, parts),
+        out_shape=(like, like),
+        in_specs=[VMEM] * (5 + parts),
+        out_specs=(pl.BlockSpec(memory_space=pl.ANY),) * 2,
+        scratch_shapes=[
+            pltpu.VMEM((count, rows, cols), F32),
+            pltpu.VMEM(like.shape, F32),
+            pltpu.VMEM(like.shape, F32),
+            pltpu.SemaphoreType.DMA((2, 4)),
+        ],
+        compiler_params=PARAMS,
+    )(residual, analysis, *smoothed(wide, thin, count), *blocks)
 
 
 def solution(mesh):

time: 105 us -> 105 us (level)
    pallas_call x12, Pallas kernels: 18.3 us -> 16.6 us  [call(): pl.pallas_call(body, out_shape=out_shape, in_specs=in_specs or [VMEM] * l...]
    pallas_call x0 -> x1, Pallas kernels: none -> 1.63 us  [per_device(): pl.pallas_call(functools.partial(final_body, parts), out_shape=(like, lik...]
where the time goes in v5:
time: 105 us; the launch traced here: 104 us
  starting transfers between devices  44.3 us (42%)
  waiting for transfers between devices  37.9 us (36%)
  Pallas kernels  18.2 us (17%)
  local copies, waits for them, and re-layouts  2.79 us (3%)
    ppermute x14, starting transfers between devices, shift(): return lax.ppermute(x, axis, pairs)  39.2 us
    ppermute x4, waiting for transfers between devices, turned(): lax.ppermute(x, 'member', [(i, (i + step) % parts) for i in range(parts)])  20.7 us
    ppermute x14, waiting for transfers between devices, shift(): return lax.ppermute(x, axis, pairs)  17.2 us
    pallas_call x12, Pallas kernels, call(): pl.pallas_call(body, out_shape=out_shape, in_specs=in_specs or [VMEM] * l...  16.6 us
    ppermute x4, starting transfers between devices, turned(): lax.ppermute(x, 'member', [(i, (i + step) % parts) for i in range(parts)])  5.03 us
    unnamed x12, local copies, waits for them, and re-layouts  2.65 us
  transfers between devices with their start and end apart: 18, of which 8 were waited for; matrix products, arithmetic and copies ran while one was open for 0% of the time, Pallas kernels for 11%

profile of v5, /device:TPU:20, one launch (start us, length us, event | category | flops | bytes accessed | tf_op | source)
XLA Modules:
  0.0 104.0 jit_solution(30250135911176929)
XLA Ops:
  0.6 1.6 %copy-done = bf16[2,64,16,512]{3,2,1,0:T(8,128)(2,1)S(1)} copy-done((bf16[2,64,16,512]{3,2,1,0:T(8,128)(2,1)S(1)}, bf16[2,64,16,512]{3,2,1,0:T(8,128)(2,1)}, u32[]{:S(2)}) %copy-start) | copy-done | bytes 2097176
  2.4 1.6 %collective-permute-start = (bf16[2,64,16,128]{3,2,1,0:T(8,128)(2,1)S(1)}, bf16[2,64,16,128]{3,2,1,0:T(8,128)(2,1)S(1)}, u32[]{:S(2)}, u32[]{:S(2)}) collective-permute-start(bf16[2,64,16,128]{3,2,1,0:T(8,128)(2,1)S(1)} %get-tuple-element.49), channel_id=1, source_target_pairs={{0,1},{1,2},{2,3},{3,0},{4,5},{5,6},{6,7},{7,4},{8,9},{9,10},{10,1... | collective-permute-start | bytes 1572872 | tf_op jit(solution)/shard_map/ppermute | solution.py:496
  4.1 1.0 copy-done.2
  5.4 2.3 %collective-permute-start.1 = (f32[4,16,128]{2,1,0:T(8,128)S(1)}, f32[4,16,128]{2,1,0:T(8,128)S(1)}, u32[]{:S(2)}, u32[]{:S(2)}) collective-permute-start(f32[4,16,128]{2,1,0:T(8,128)S(1)} %get-tuple-element.50), channel_id=1, source_target_pairs={{0,1},{1,2},{2,3},{4,5},{5,6},{6,7},{8,9},{9,10},{10,11},{12,13},{... | collective-permute-start | bytes 98312 | tf_op jit(solution)/shard_map/ppermute | solution.py:142
  7.8 3.5 %collective-permute-start.2 = (f32[4,16,128]{2,1,0:T(8,128)S(1)}, f32[4,16,128]{2,1,0:T(8,128)S(1)}, u32[]{:S(2)}, u32[]{:S(2)}) collective-permute-start(f32[4,16,128]{2,1,0:T(8,128)S(1)} %get-tuple-element.44), channel_id=1, source_target_pairs={{1,0},{2,1},{3,2},{5,4},{6,5},{7,6},{9,8},{10,9},{11,10},{13,12},{... | collective-permute-start | bytes 98312 | tf_op jit(solution)/shard_map/ppermute | solution.py:142
  11.3 3.6 %shard_map.61 = (bf16[2,4,16,128]{3,2,1,0:T(8,128)(2,1)S(1)}, bf16[2,4,16,128]{3,2,1,0:T(8,128)(2,1)S(1)}, bf16[2,68,16,128]{3,2,1,0:T(8,128)(2,1)S(1)}, bf16[2,68,16,128]{3,2,1,0:T(8,128)(2,1)S(1)}) custom-call(bf16[2,64,16,512]{3,2,1,0:T(8,128)(2,1)S(1)} %copy-done.1), custom_call_target="tpu_custom_call" | custom-call | tf_op jit(solution)/shard_map/pallas_call | solution.py:27
  15.4 1.5 %collective-permute-done.1.left_ref = f32[4,16,128]{2,1,0:T(8,128)S(1)} collective-permute-done((f32[4,16,128]{2,1,0:T(8,128)S(1)}, f32[4,16,128]{2,1,0:T(8,128)S(1)}, u32[]{:S(2)}, u32[]{:S(2)}) %collective-permute-start.1) | collective-permute-done | bytes 32800 | tf_op jit(solution)/shard_map/ppermute | solution.py:142
  16.9 2.3 %collective-permute-start.7 = (bf16[2,68,16,128]{3,2,1,0:T(8,128)(2,1)S(1)}, bf16[2,68,16,128]{3,2,1,0:T(8,128)(2,1)S(1)}, u32[]{:S(2)}, u32[]{:S(2)}) collective-permute-start(bf16[2,68,16,128]{3,2,1,0:T(8,128)(2,1)S(1)} %get-tuple-element.64), channel_id=1, source_target_pairs={{0,2},{1,3},{2,0},{3,1},{4,6},{5,7},{6,4},{7,5},{8,10},{9,11},{10,... | collective-permute-start | bytes 1671176 | tf_op jit(solution)/shard_map/ppermute | solution.py:496
  19.2 1.9 %collective-permute-start.3 = (f32[34,8,128]{2,1,0:T(8,128)S(1)}, f32[34,8,128]{2,1,0:T(8,128)S(1)}, u32[]{:S(2)}, u32[]{:S(2)}) collective-permute-start(f32[34,8,128]{2,1,0:T(8,128)S(1)} %get-tuple-element.54), channel_id=1, source_target_pairs={{0,4},{4,8},{8,12},{12,16},{16,20},{20,24},{24,28},{1,5},{5,9},{9,... | collective-permute-start | bytes 417800 | tf_op jit(solution)/shard_map/ppermute | solution.py:142
  21.1 4.5 %collective-permute-start.4 = (f32[34,8,128]{2,1,0:T(8,128)S(1)}, f32[34,8,128]{2,1,0:T(8,128)S(1)}, u32[]{:S(2)}, u32[]{:S(2)}) collective-permute-start(f32[34,8,128]{2,1,0:T(8,128)S(1)} %get-tuple-element.55), channel_id=1, source_target_pairs={{4,0},{8,4},{12,8},{16,12},{20,16},{24,20},{28,24},{5,1},{9,5},{13... | collective-permute-start | bytes 417800 | tf_op jit(solution)/shard_map/ppermute | solution.py:142
  25.7 0.6 collective-permute-start.5
  26.5 1.8 %collective-permute-done.4.below_ref = f32[34,8,128]{2,1,0:T(8,128)S(1)} collective-permute-done((f32[34,8,128]{2,1,0:T(8,128)S(1)}, f32[34,8,128]{2,1,0:T(8,128)S(1)}, u32[]{:S(2)}, u32[]{:S(2)}) %collective-permute-start.4) | collective-permute-done | bytes 139296 | tf_op jit(solution)/shard_map/ppermute | solution.py:142
  28.4 4.8 %shard_map.63.grad_ref = f32[64,16,128]{2,1,0:T(8,128)S(1)} custom-call(f32[64,128]{1,0:T(8,128)S(1)} %broadcast_in_dim.4.wx_ref, f32[64,128]{1,0:T(8,128)S(1)} %broadcast_in_dim.5.wy_ref, f32[64,16,128]{2,1,0:T(8,128)S(1)} %copy-done.2, f32[4,16,128]{2,1,0:T(8,128)S(1)} %get-tuple-element.53.beside_ref.around_ref, ...), custom_call_target="tpu_custom_call" | custom-call | tf_op jit(solution)/shard_map/pallas_call | solution.py:27
  33.2 20.7 %collective-permute-done.5.refs_5_ = bf16[2,4,16,128]{3,2,1,0:T(8,128)(2,1)S(1)} collective-permute-done((bf16[2,4,16,128]{3,2,1,0:T(8,128)(2,1)S(1)}, bf16[2,4,16,128]{3,2,1,0:T(8,128)(2,1)S(1)}, u32[]{:S(2)}, u32[]{:S(2)}) %collective-permute-start.5) | collective-permute-done | bytes 32800 | tf_op jit(solution)/shard_map/ppermute | solution.py:496
  54.6 1.9 %collective-permute-start.9 = (bf16[8,16,128]{2,1,0:T(8,128)(2,1)S(1)}, bf16[8,16,128]{2,1,0:T(8,128)(2,1)S(1)}, u32[]{:S(2)}, u32[]{:S(2)}) collective-permute-start(bf16[8,16,128]{2,1,0:T(8,128)(2,1)S(1)} %get-tuple-element.65), channel_id=1, source_target_pairs={{1,0},{2,1},{3,2},{5,4},{6,5},{7,6},{9,8},{10,9},{11,10},{13,12},{... | collective-permute-start | bytes 98312 | tf_op jit(solution)/shard_map/ppermute | solution.py:142
  56.5 3.9 %collective-permute-start.8 = (bf16[8,16,128]{2,1,0:T(8,128)(2,1)S(1)}, bf16[8,16,128]{2,1,0:T(8,128)(2,1)S(1)}, u32[]{:S(2)}, u32[]{:S(2)}) collective-permute-start(bf16[8,16,128]{2,1,0:T(8,128)(2,1)S(1)} %get-tuple-element.65), channel_id=1, source_target_pairs={{0,1},{1,2},{2,3},{4,5},{5,6},{6,7},{8,9},{9,10},{10,11},{12,13},{... | collective-permute-start | bytes 98312 | tf_op jit(solution)/shard_map/ppermute | solution.py:142
  60.5 1.9 %collective-permute-done.8.left_ref = bf16[8,16,128]{2,1,0:T(8,128)(2,1)S(1)} collective-permute-done((bf16[8,16,128]{2,1,0:T(8,128)(2,1)S(1)}, bf16[8,16,128]{2,1,0:T(8,128)(2,1)S(1)}, u32[]{:S(2)}, u32[]{:S(2)}) %collective-permute-start.8) | collective-permute-done | bytes 32800 | tf_op jit(solution)/shard_map/ppermute | solution.py:142
  62.7 1.9 %collective-permute-start.11 = (bf16[16,16,128]{2,1,0:T(8,128)(2,1)S(1)}, bf16[16,16,128]{2,1,0:T(8,128)(2,1)S(1)}, u32[]{:S(2)}, u32[]{:S(2)}) collective-permute-start(bf16[16,16,128]{2,1,0:T(8,128)(2,1)S(1)} %get-tuple-element.67), channel_id=1, source_target_pairs={{4,0},{8,4},{12,8},{16,12},{20,16},{24,20},{28,24},{5,1},{9,5},{13... | collective-permute-start | bytes 196616 | tf_op jit(solution)/shard_map/ppermute | solution.py:142
  64.7 2.4 %collective-permute-start.10 = (bf16[16,16,128]{2,1,0:T(8,128)(2,1)S(1)}, bf16[16,16,128]{2,1,0:T(8,128)(2,1)S(1)}, u32[]{:S(2)}, u32[]{:S(2)}) collective-permute-start(bf16[16,16,128]{2,1,0:T(8,128)(2,1)S(1)} %get-tuple-element.67), channel_id=1, source_target_pairs={{0,4},{4,8},{8,12},{12,16},{16,20},{20,24},{24,28},{1,5},{5,9},{9,... | collective-permute-start | bytes 196616 | tf_op jit(solution)/shard_map/ppermute | solution.py:142
  67.1 4.1 %collective-permute-done.10.above_ref = bf16[16,16,128]{2,1,0:T(8,128)(2,1)S(1)} collective-permute-done((bf16[16,16,128]{2,1,0:T(8,128)(2,1)S(1)}, bf16[16,16,128]{2,1,0:T(8,128)(2,1)S(1)}, u32[]{:S(2)}, u32[]{:S(2)}) %collective-permute-start.10) | collective-permute-done | bytes 65568 | tf_op jit(solution)/shard_map/ppermute | solution.py:142
  71.1 0.9 shard_map.67
  72.1 1.9 %collective-permute-start.12 = (bf16[17,16,128]{2,1,0:T(8,128)(2,1)S(1)}, bf16[17,16,128]{2,1,0:T(8,128)(2,1)S(1)}, u32[]{:S(2)}, u32[]{:S(2)}) collective-permute-start(bf16[17,16,128]{2,1,0:T(8,128)(2,1)S(1)} %get-tuple-element.74), channel_id=1, source_target_pairs={{0,4},{4,8},{8,12},{12,16},{16,20},{20,24},{24,28},{1,5},{5,9},{9,... | collective-permute-start | bytes 208904 | tf_op jit(solution)/shard_map/ppermute | solution.py:142
  74.0 4.5 %collective-permute-start.13 = (bf16[17,16,128]{2,1,0:T(8,128)(2,1)S(1)}, bf16[17,16,128]{2,1,0:T(8,128)(2,1)S(1)}, u32[]{:S(2)}, u32[]{:S(2)}) collective-permute-start(bf16[17,16,128]{2,1,0:T(8,128)(2,1)S(1)} %get-tuple-element.75), channel_id=1, source_target_pairs={{4,0},{8,4},{12,8},{16,12},{20,16},{24,20},{28,24},{5,1},{9,5},{13... | collective-permute-start | bytes 208904 | tf_op jit(solution)/shard_map/ppermute | solution.py:142
  78.6 2.5 %shard_map.68 = (f32[64,16,128]{2,1,0:T(8,128)S(1)}, f32[4,12,3,8,128]{4,3,2,1,0:T(8,128)S(1)}) custom-call(f32[64,128]{1,0:T(8,128)S(1)} %broadcast_in_dim.4.wx_ref, f32[64,128]{1,0:T(8,128)S(1)} %broadcast_in_dim.5.wy_ref, f32[64,16,128]{2,1,0:T(8,128)S(1)} %get-tuple-element.71.x_ref.residual_ref, f32[4,16,128]{2,1,0:T(8,128)S(1)} %get-tuple-element.73.beside_ref), custom_call_target="tpu_custom_call" | custom-call | tf_op jit(solution)/shard_map/pallas_call | solution.py:27
  81.1 2.8 %shard_map.69 = (f32[8,16,128]{2,1,0:T(8,128)S(1)}, bf16[8,16,128]{2,1,0:T(8,128)(2,1)S(1)}) custom-call(f32[64,128]{1,0:T(8,128)S(1)} %broadcast_in_dim.4.wx_ref, f32[64,128]{1,0:T(8,128)S(1)} %broadcast_in_dim.5.wy_ref, f32[64,16,128]{2,1,0:T(8,128)S(1)} %get-tuple-element.71.x_ref.residual_ref, f32[4,16,128]{2,1,0:T(8,128)S(1)} %get-tuple-element.73.beside_ref, ...), custom_call_target="tpu_custom_call" | custom-call | tf_op jit(solution)/shard_map/pallas_call | solution.py:27
  83.9 3.7 %collective-permute-start.15 = (bf16[8,16,128]{2,1,0:T(8,128)(2,1)S(1)}, bf16[8,16,128]{2,1,0:T(8,128)(2,1)S(1)}, u32[]{:S(2)}, u32[]{:S(2)}) collective-permute-start(bf16[8,16,128]{2,1,0:T(8,128)(2,1)S(1)} %get-tuple-element.78), channel_id=1, source_target_pairs={{1,0},{2,1},{3,2},{5,4},{6,5},{7,6},{9,8},{10,9},{11,10},{13,12},{... | collective-permute-start | bytes 98312 | tf_op jit(solution)/shard_map/ppermute | solution.py:142
  87.6 2.1 %collective-permute-start.14 = (bf16[8,16,128]{2,1,0:T(8,128)(2,1)S(1)}, bf16[8,16,128]{2,1,0:T(8,128)(2,1)S(1)}, u32[]{:S(2)}, u32[]{:S(2)}) collective-permute-start(bf16[8,16,128]{2,1,0:T(8,128)(2,1)S(1)} %get-tuple-element.78), channel_id=1, source_target_pairs={{0,1},{1,2},{2,3},{4,5},{5,6},{6,7},{8,9},{9,10},{10,11},{12,13},{... | collective-permute-start | bytes 98312 | tf_op jit(solution)/shard_map/ppermute | solution.py:142
  89.8 3.6 %collective-permute-done.14.left_ref = bf16[8,16,128]{2,1,0:T(8,128)(2,1)S(1)} collective-permute-done((bf16[8,16,128]{2,1,0:T(8,128)(2,1)S(1)}, bf16[8,16,128]{2,1,0:T(8,128)(2,1)S(1)}, u32[]{:S(2)}, u32[]{:S(2)}) %collective-permute-start.14) | collective-permute-done | bytes 32800 | tf_op jit(solution)/shard_map/ppermute | solution.py:142
  93.7 2.5 %collective-permute-start.17 = (bf16[8,16,128]{2,1,0:T(8,128)(2,1)S(1)}, bf16[8,16,128]{2,1,0:T(8,128)(2,1)S(1)}, u32[]{:S(2)}, u32[]{:S(2)}) collective-permute-start(bf16[8,16,128]{2,1,0:T(8,128)(2,1)S(1)} %get-tuple-element.80), channel_id=1, source_target_pairs={{4,0},{8,4},{12,8},{16,12},{20,16},{24,20},{28,24},{5,1},{9,5},{13... | collective-permute-start | bytes 98312 | tf_op jit(solution)/shard_map/ppermute | solution.py:142
  96.3 1.9 %collective-permute-start.16 = (bf16[8,16,128]{2,1,0:T(8,128)(2,1)S(1)}, bf16[8,16,128]{2,1,0:T(8,128)(2,1)S(1)}, u32[]{:S(2)}, u32[]{:S(2)}) collective-permute-start(bf16[8,16,128]{2,1,0:T(8,128)(2,1)S(1)} %get-tuple-element.80), channel_id=1, source_target_pairs={{0,4},{4,8},{8,12},{12,16},{16,20},{20,24},{24,28},{1,5},{5,9},{9,... | collective-permute-start | bytes 98312 | tf_op jit(solution)/shard_map/ppermute | solution.py:142
  98.2 4.2 %collective-permute-done.16.above_ref = bf16[8,16,128]{2,1,0:T(8,128)(2,1)S(1)} collective-permute-done((bf16[8,16,128]{2,1,0:T(8,128)(2,1)S(1)}, bf16[8,16,128]{2,1,0:T(8,128)(2,1)S(1)}, u32[]{:S(2)}, u32[]{:S(2)}) %collective-permute-start.16) | collective-permute-done | bytes 32800 | tf_op jit(solution)/shard_map/ppermute | solution.py:142
  102.4 1.6 %shard_map.71 = (f32[64,16,128]{2,1,0:T(8,128)}, f32[64,16,128]{2,1,0:T(8,128)}) custom-call(f32[64,16,128]{2,1,0:T(8,128)S(1)} %get-tuple-element.71.x_ref.residual_ref, f32[64,16,128]{2,1,0:T(8,128)S(1)} %get-tuple-element.72.before_ref, bf16[8,16,128]{2,1,0:T(8,128)(2,1)S(1)} %collective-permute-done.16.above_ref, ...), custom_call_target="tpu_custom_call" | custom-call | tf_op jit(solution)/shard_map/pallas_call | solution.py:549
  (31 shorter events, 2.8 us)
Async XLA Ops:
  0.6 1.6 %copy-start = (bf16[2,64,16,512]{3,2,1,0:T(8,128)(2,1)S(1)}, bf16[2,64,16,512]{3,2,1,0:T(8,128)(2,1)}, u32[]{:S(2)}) copy-start(bf16[2,64,16,512]{3,2,1,0:T(8,128)(2,1)} %in_ref.2) | copy-start | bytes 6291460
  2.2 9.1 %copy-start.1 = (bf16[2,64,16,512]{3,2,1,0:T(8,128)(2,1)S(1)}, bf16[2,64,16,512]{3,2,1,0:T(8,128)(2,1)}, u32[]{:S(2)}) copy-start(bf16[2,64,16,512]{3,2,1,0:T(8,128)(2,1)} %in_ref.2) | copy-start | bytes 6291460
  2.4 25.8 %copy-start.4 = (f32[64]{0:T(128)S(1)}, f32[64]{0:T(128)}, u32[]{:S(2)}) copy-start(f32[64]{0:T(128)} %param.6) | copy-start | bytes 772
  2.4 25.9 %copy-start.5 = (f32[64]{0:T(128)S(1)}, f32[64]{0:T(128)}, u32[]{:S(2)}) copy-start(f32[64]{0:T(128)} %param.7) | copy-start | bytes 772
  2.4 14.4 %collective-permute-start = (bf16[2,64,16,128]{3,2,1,0:T(8,128)(2,1)S(1)}, bf16[2,64,16,128]{3,2,1,0:T(8,128)(2,1)S(1)}, u32[]{:S(2)}, u32[]{:S(2)}) collective-permute-start(bf16[2,64,16,128]{3,2,1,0:T(8,128)(2,1)S(1)} %get-tuple-element.49), channel_id=1, source_target_pairs={{0,1},{1,2},{2,3},{3,0},{4,5},{5,6},{6,7},{7,4},{8,9},{9,10},{10,1... | collective-permute-start | bytes 1572872 | tf_op jit(solution)/shard_map/ppermute | solution.py:496
  4.1 1.0 %copy-start.2 = (f32[64,16,128]{2,1,0:T(8,128)S(1)}, f32[64,16,128]{2,1,0:T(8,128)}, u32[]{:S(2)}) copy-start(f32[64,16,128]{2,1,0:T(8,128)} %residual_ref) | copy-start | bytes 1572868
  5.4 11.4 %collective-permute-start.1 = (f32[4,16,128]{2,1,0:T(8,128)S(1)}, f32[4,16,128]{2,1,0:T(8,128)S(1)}, u32[]{:S(2)}, u32[]{:S(2)}) collective-permute-start(f32[4,16,128]{2,1,0:T(8,128)S(1)} %get-tuple-element.50), channel_id=1, source_target_pairs={{0,1},{1,2},{2,3},{4,5},{5,6},{6,7},{8,9},{9,10},{10,11},{12,13},{... | collective-permute-start | bytes 98312 | tf_op jit(solution)/shard_map/ppermute | solution.py:142
  7.8 9.1 %collective-permute-start.2 = (f32[4,16,128]{2,1,0:T(8,128)S(1)}, f32[4,16,128]{2,1,0:T(8,128)S(1)}, u32[]{:S(2)}, u32[]{:S(2)}) collective-permute-start(f32[4,16,128]{2,1,0:T(8,128)S(1)} %get-tuple-element.44), channel_id=1, source_target_pairs={{1,0},{2,1},{3,2},{5,4},{6,5},{7,6},{9,8},{10,9},{11,10},{13,12},{... | collective-permute-start | bytes 98312 | tf_op jit(solution)/shard_map/ppermute | solution.py:142
  14.9 38.9 %collective-permute-start.6 = (bf16[2,68,16,128]{3,2,1,0:T(8,128)(2,1)S(1)}, bf16[2,68,16,128]{3,2,1,0:T(8,128)(2,1)S(1)}, u32[]{:S(2)}, u32[]{:S(2)}) collective-permute-start(bf16[2,68,16,128]{3,2,1,0:T(8,128)(2,1)S(1)} %get-tuple-element.61), channel_id=1, source_target_pairs={{0,3},{1,0},{2,1},{3,2},{4,7},{5,4},{6,5},{7,6},{8,11},{9,8},{10,9... | collective-permute-start | bytes 1671176 | tf_op jit(solution)/shard_map/ppermute | solution.py:496
  16.9 37.4 %collective-permute-start.7 = (bf16[2,68,16,128]{3,2,1,0:T(8,128)(2,1)S(1)}, bf16[2,68,16,128]{3,2,1,0:T(8,128)(2,1)S(1)}, u32[]{:S(2)}, u32[]{:S(2)}) collective-permute-start(bf16[2,68,16,128]{3,2,1,0:T(8,128)(2,1)S(1)} %get-tuple-element.64), channel_id=1, source_target_pairs={{0,2},{1,3},{2,0},{3,1},{4,6},{5,7},{6,4},{7,5},{8,10},{9,11},{10,... | collective-permute-start | bytes 1671176 | tf_op jit(solution)/shard_map/ppermute | solution.py:496
  19.2 7.3 %collective-permute-start.3 = (f32[34,8,128]{2,1,0:T(8,128)S(1)}, f32[34,8,128]{2,1,0:T(8,128)S(1)}, u32[]{:S(2)}, u32[]{:S(2)}) collective-permute-start(f32[34,8,128]{2,1,0:T(8,128)S(1)} %get-tuple-element.54), channel_id=1, source_target_pairs={{0,4},{4,8},{8,12},{12,16},{16,20},{20,24},{24,28},{1,5},{5,9},{9,... | collective-permute-start | bytes 417800 | tf_op jit(solution)/shard_map/ppermute | solution.py:142
  21.1 7.1 %collective-permute-start.4 = (f32[34,8,128]{2,1,0:T(8,128)S(1)}, f32[34,8,128]{2,1,0:T(8,128)S(1)}, u32[]{:S(2)}, u32[]{:S(2)}) collective-permute-start(f32[34,8,128]{2,1,0:T(8,128)S(1)} %get-tuple-element.55), channel_id=1, source_target_pairs={{4,0},{8,4},{12,8},{16,12},{20,16},{24,20},{28,24},{5,1},{9,5},{13... | collective-permute-start | bytes 417800 | tf_op jit(solution)/shard_map/ppermute | solution.py:142
  25.7 28.1 %collective-permute-start.5 = (bf16[2,4,16,128]{3,2,1,0:T(8,128)(2,1)S(1)}, bf16[2,4,16,128]{3,2,1,0:T(8,128)(2,1)S(1)}, u32[]{:S(2)}, u32[]{:S(2)}) collective-permute-start(bf16[2,4,16,128]{3,2,1,0:T(8,128)(2,1)S(1)} %get-tuple-element.57), channel_id=1, source_target_pairs={{0,1},{1,2},{2,3},{3,0},{4,5},{5,6},{6,7},{7,4},{8,9},{9,10},{10,1... | collective-permute-start | bytes 98312 | tf_op jit(solution)/shard_map/ppermute | solution.py:496
  28.4 42.7 %copy-start.3 = (f32[64,16,128]{2,1,0:T(8,128)S(1)}, f32[64,16,128]{2,1,0:T(8,128)}, u32[]{:S(2)}) copy-start(f32[64,16,128]{2,1,0:T(8,128)} %residual_ref) | copy-start | bytes 1572868
  54.6 5.9 %collective-permute-start.9 = (bf16[8,16,128]{2,1,0:T(8,128)(2,1)S(1)}, bf16[8,16,128]{2,1,0:T(8,128)(2,1)S(1)}, u32[]{:S(2)}, u32[]{:S(2)}) collective-permute-start(bf16[8,16,128]{2,1,0:T(8,128)(2,1)S(1)} %get-tuple-element.65), channel_id=1, source_target_pairs={{1,0},{2,1},{3,2},{5,4},{6,5},{7,6},{9,8},{10,9},{11,10},{13,12},{... | collective-permute-start | bytes 98312 | tf_op jit(solution)/shard_map/ppermute | solution.py:142
  56.5 5.8 %collective-permute-start.8 = (bf16[8,16,128]{2,1,0:T(8,128)(2,1)S(1)}, bf16[8,16,128]{2,1,0:T(8,128)(2,1)S(1)}, u32[]{:S(2)}, u32[]{:S(2)}) collective-permute-start(bf16[8,16,128]{2,1,0:T(8,128)(2,1)S(1)} %get-tuple-element.65), channel_id=1, source_target_pairs={{0,1},{1,2},{2,3},{4,5},{5,6},{6,7},{8,9},{9,10},{10,11},{12,13},{... | collective-permute-start | bytes 98312 | tf_op jit(solution)/shard_map/ppermute | solution.py:142
  62.7 4.3 %collective-permute-start.11 = (bf16[16,16,128]{2,1,0:T(8,128)(2,1)S(1)}, bf16[16,16,128]{2,1,0:T(8,128)(2,1)S(1)}, u32[]{:S(2)}, u32[]{:S(2)}) collective-permute-start(bf16[16,16,128]{2,1,0:T(8,128)(2,1)S(1)} %get-tuple-element.67), channel_id=1, source_target_pairs={{4,0},{8,4},{12,8},{16,12},{20,16},{24,20},{28,24},{5,1},{9,5},{13... | collective-permute-start | bytes 196616 | tf_op jit(solution)/shard_map/ppermute | solution.py:142
  64.7 6.5 %collective-permute-start.10 = (bf16[16,16,128]{2,1,0:T(8,128)(2,1)S(1)}, bf16[16,16,128]{2,1,0:T(8,128)(2,1)S(1)}, u32[]{:S(2)}, u32[]{:S(2)}) collective-permute-start(bf16[16,16,128]{2,1,0:T(8,128)(2,1)S(1)} %get-tuple-element.67), channel_id=1, source_target_pairs={{0,4},{4,8},{8,12},{12,16},{16,20},{20,24},{24,28},{1,5},{5,9},{9,... | collective-permute-start | bytes 196616 | tf_op jit(solution)/shard_map/ppermute | solution.py:142
  72.1 9.0 %collective-permute-start.12 = (bf16[17,16,128]{2,1,0:T(8,128)(2,1)S(1)}, bf16[17,16,128]{2,1,0:T(8,128)(2,1)S(1)}, u32[]{:S(2)}, u32[]{:S(2)}) collective-permute-start(bf16[17,16,128]{2,1,0:T(8,128)(2,1)S(1)} %get-tuple-element.74), channel_id=1, source_target_pairs={{0,4},{4,8},{8,12},{12,16},{16,20},{20,24},{24,28},{1,5},{5,9},{9,... | collective-permute-start | bytes 208904 | tf_op jit(solution)/shard_map/ppermute | solution.py:142
  74.0 7.1 %collective-permute-start.13 = (bf16[17,16,128]{2,1,0:T(8,128)(2,1)S(1)}, bf16[17,16,128]{2,1,0:T(8,128)(2,1)S(1)}, u32[]{:S(2)}, u32[]{:S(2)}) collective-permute-start(bf16[17,16,128]{2,1,0:T(8,128)(2,1)S(1)} %get-tuple-element.75), channel_id=1, source_target_pairs={{4,0},{8,4},{12,8},{16,12},{20,16},{24,20},{28,24},{5,1},{9,5},{13... | collective-permute-start | bytes 208904 | tf_op jit(solution)/shard_map/ppermute | solution.py:142
  83.9 5.9 %collective-permute-start.15 = (bf16[8,16,128]{2,1,0:T(8,128)(2,1)S(1)}, bf16[8,16,128]{2,1,0:T(8,128)(2,1)S(1)}, u32[]{:S(2)}, u32[]{:S(2)}) collective-permute-start(bf16[8,16,128]{2,1,0:T(8,128)(2,1)S(1)} %get-tuple-element.78), channel_id=1, source_target_pairs={{1,0},{2,1},{3,2},{5,4},{6,5},{7,6},{9,8},{10,9},{11,10},{13,12},{... | collective-permute-start | bytes 98312 | tf_op jit(solution)/shard_map/ppermute | solution.py:142
  87.6 5.8 %collective-permute-start.14 = (bf16[8,16,128]{2,1,0:T(8,128)(2,1)S(1)}, bf16[8,16,128]{2,1,0:T(8,128)(2,1)S(1)}, u32[]{:S(2)}, u32[]{:S(2)}) collective-permute-start(bf16[8,16,128]{2,1,0:T(8,128)(2,1)S(1)} %get-tuple-element.78), channel_id=1, source_target_pairs={{0,1},{1,2},{2,3},{4,5},{5,6},{6,7},{8,9},{9,10},{10,11},{12,13},{... | collective-permute-start | bytes 98312 | tf_op jit(solution)/shard_map/ppermute | solution.py:142
  93.7 4.5 %collective-permute-start.17 = (bf16[8,16,128]{2,1,0:T(8,128)(2,1)S(1)}, bf16[8,16,128]{2,1,0:T(8,128)(2,1)S(1)}, u32[]{:S(2)}, u32[]{:S(2)}) collective-permute-start(bf16[8,16,128]{2,1,0:T(8,128)(2,1)S(1)} %get-tuple-element.80), channel_id=1, source_target_pairs={{4,0},{8,4},{12,8},{16,12},{20,16},{24,20},{28,24},{5,1},{9,5},{13... | collective-permute-start | bytes 98312 | tf_op jit(solution)/shard_map/ppermute | solution.py:142
  96.3 6.1 %collective-permute-start.16 = (bf16[8,16,128]{2,1,0:T(8,128)(2,1)S(1)}, bf16[8,16,128]{2,1,0:T(8,128)(2,1)S(1)}, u32[]{:S(2)}, u32[]{:S(2)}) collective-permute-start(bf16[8,16,128]{2,1,0:T(8,128)(2,1)S(1)} %get-tuple-element.80), channel_id=1, source_target_pairs={{0,4},{4,8},{8,12},{12,16},{16,20},{20,24},{24,28},{1,5},{5,9},{9,... | collective-permute-start | bytes 98312 | tf_op jit(solution)/shard_map/ppermute | solution.py:142

commit v6 on v5

--- a/solution.py
+++ b/solution.py
@@ -78,11 +78,11 @@
     return jnp.where(here, pltpu.roll(x, MODEL_STEPS * (left_slot(k) + SUB), 1), total)
 
 
-def sides_body(in_ref, *out_refs):
-    levels = in_ref.shape[1]
-    own, groups, rows, _ = out_refs[0].shape
-    cols = in_ref.shape[-1] // len(out_refs)
-    for r, out_ref in enumerate(out_refs):
+def sides_body(turns, parts, in_ref, *out_refs):
+    own, levels, rows, ny = in_ref.shape
+    groups = levels // GROUP
+    cols = ny // parts
+    for r, out_ref in zip(turns, out_refs):
         start = out_ref.shape[1] - groups
         if start:
             out_ref[:, :start] = in_ref[:, :, :, block_of(r, cols)]
@@ -100,12 +100,13 @@
             lax.fori_loop(0, groups, step, 0)
 
 
-def side_columns(members, parts):
+def side_columns(members, parts, turns):
     own, levels, rows, ny = members.shape
     groups = levels // GROUP
-    thin = jax.ShapeDtypeStruct((own, groups, rows, LANES), members.dtype)
-    full = jax.ShapeDtypeStruct((own, levels + groups, rows, LANES), members.dtype)
-    return call(sides_body, (thin,) * 2 + (full,) * (parts - 2), members)
+    out = [
+        jax.ShapeDtypeStruct((own, (levels if r > 1 else 0) + groups, rows, LANES), members.dtype) for r in turns
+    ]
+    return call(functools.partial(sides_body, turns, parts), tuple(out), members)
 
 
 def pack_rows(ref, at, top_ref, bottom_ref):
@@ -514,8 +515,10 @@
     first, last = call(columns_edge_body, (packed, packed), residual_in)
     left, right = shift(last, "member", 1), shift(first, "member", -1)
     members, first = lax.optimization_barrier((members, first))
-    *later, final = side_columns(members, parts)
+    (final,) = side_columns(members, parts, [parts - 1])
+    final, members = lax.optimization_barrier((final, members))
     final = turned(final, parts - 1)
+    later = side_columns(members, parts, list(range(parts - 1)))
     later, early, left, right = lax.optimization_barrier((later, early, left, right))
     blocks = [mine, early] + [turned(x, r) for r, x in enumerate(later[2:], 2)] + [final]
     sides = [later[0], turned(later[1], 1)]

time: 105 us -> 105 us (level)
  starting transfers between devices: 44.3 us -> 41.4 us
  waiting for transfers between devices: 37.9 us -> 40.7 us
    ppermute x14, waiting for transfers between devices: 17.2 us -> 36.1 us  [shift(): return lax.ppermute(x, axis, pairs)]
    ppermute x4, waiting for transfers between devices: 20.7 us -> 4.54 us  [turned(): lax.ppermute(x, 'member', [(i, (i + step) % parts) for i in range(parts)])]
    ppermute x4, starting transfers between devices: 5.03 us -> 2.19 us  [turned(): lax.ppermute(x, 'member', [(i, (i + step) % parts) for i in range(parts)])]
    pallas_call x12 -> x13, Pallas kernels: 16.6 us -> 16.6 us  [call(): pl.pallas_call(body, out_shape=out_shape, in_specs=in_specs or [VMEM] * l...]
where the time goes in v6:
time: 105 us; the launch traced here: 104 us
  starting transfers between devices  41.4 us (39%)
  waiting for transfers between devices  40.7 us (39%)
  Pallas kernels  18.2 us (17%)
  local copies, waits for them, and re-layouts  2.79 us (3%)
    ppermute x14, starting transfers between devices, shift(): return lax.ppermute(x, axis, pairs)  39.2 us
    ppermute x14, waiting for transfers between devices, shift(): return lax.ppermute(x, axis, pairs)  36.1 us
    pallas_call x13, Pallas kernels, call(): pl.pallas_call(body, out_shape=out_shape, in_specs=in_specs or [VMEM] * l...  16.6 us
    ppermute x4, waiting for transfers between devices, turned(): lax.ppermute(x, 'member', [(i, (i + step) % parts) for i in range(parts)])  4.54 us
    unnamed x12, local copies, waits for them, and re-layouts  2.65 us
    ppermute x4, starting transfers between devices, turned(): lax.ppermute(x, 'member', [(i, (i + step) % parts) for i in range(parts)])  2.19 us
  transfers between devices with their start and end apart: 18, of which 8 were waited for; matrix products, arithmetic and copies ran while one was open for 0% of the time, Pallas kernels for 11%

profile of v6, /device:TPU:20, one launch (start us, length us, event | category | flops | bytes accessed | tf_op | source)
XLA Modules:
  0.0 104.0 jit_solution(18358958726599308828)
XLA Ops:
  0.6 1.6 %copy-done = bf16[2,64,16,512]{3,2,1,0:T(8,128)(2,1)S(1)} copy-done((bf16[2,64,16,512]{3,2,1,0:T(8,128)(2,1)S(1)}, bf16[2,64,16,512]{3,2,1,0:T(8,128)(2,1)}, u32[]{:S(2)}) %copy-start) | copy-done | bytes 2097176
  2.4 1.6 %collective-permute-start = (bf16[2,64,16,128]{3,2,1,0:T(8,128)(2,1)S(1)}, bf16[2,64,16,128]{3,2,1,0:T(8,128)(2,1)S(1)}, u32[]{:S(2)}, u32[]{:S(2)}) collective-permute-start(bf16[2,64,16,128]{3,2,1,0:T(8,128)(2,1)S(1)} %get-tuple-element.51), channel_id=1, source_target_pairs={{0,1},{1,2},{2,3},{3,0},{4,5},{5,6},{6,7},{7,4},{8,9},{9,10},{10,1... | collective-permute-start | bytes 1572872 | tf_op jit(solution)/shard_map/ppermute | solution.py:497
  4.0 1.0 copy-done.2
  5.4 2.3 %collective-permute-start.1 = (f32[4,16,128]{2,1,0:T(8,128)S(1)}, f32[4,16,128]{2,1,0:T(8,128)S(1)}, u32[]{:S(2)}, u32[]{:S(2)}) collective-permute-start(f32[4,16,128]{2,1,0:T(8,128)S(1)} %get-tuple-element.52), channel_id=1, source_target_pairs={{0,1},{1,2},{2,3},{4,5},{5,6},{6,7},{8,9},{9,10},{10,11},{12,13},{... | collective-permute-start | bytes 98312 | tf_op jit(solution)/shard_map/ppermute | solution.py:143
  7.7 3.5 %collective-permute-start.2 = (f32[4,16,128]{2,1,0:T(8,128)S(1)}, f32[4,16,128]{2,1,0:T(8,128)S(1)}, u32[]{:S(2)}, u32[]{:S(2)}) collective-permute-start(f32[4,16,128]{2,1,0:T(8,128)S(1)} %get-tuple-element.45), channel_id=1, source_target_pairs={{1,0},{2,1},{3,2},{5,4},{6,5},{7,6},{9,8},{10,9},{11,10},{13,12},{... | collective-permute-start | bytes 98312 | tf_op jit(solution)/shard_map/ppermute | solution.py:143
  11.3 0.9 shard_map.61
  12.8 2.6 %shard_map.62 = (bf16[2,4,16,128]{3,2,1,0:T(8,128)(2,1)S(1)}, bf16[2,4,16,128]{3,2,1,0:T(8,128)(2,1)S(1)}, bf16[2,68,16,128]{3,2,1,0:T(8,128)(2,1)S(1)}) custom-call(bf16[2,64,16,512]{3,2,1,0:T(8,128)(2,1)S(1)} %copy-done.1), custom_call_target="tpu_custom_call" | custom-call | tf_op jit(solution)/shard_map/pallas_call | solution.py:27
  15.4 19.3 %collective-permute-done.1.left_ref = f32[4,16,128]{2,1,0:T(8,128)S(1)} collective-permute-done((f32[4,16,128]{2,1,0:T(8,128)S(1)}, f32[4,16,128]{2,1,0:T(8,128)S(1)}, u32[]{:S(2)}, u32[]{:S(2)}) %collective-permute-start.1) | collective-permute-done | bytes 32800 | tf_op jit(solution)/shard_map/ppermute | solution.py:143
  34.8 1.9 %collective-permute-start.3 = (f32[34,8,128]{2,1,0:T(8,128)S(1)}, f32[34,8,128]{2,1,0:T(8,128)S(1)}, u32[]{:S(2)}, u32[]{:S(2)}) collective-permute-start(f32[34,8,128]{2,1,0:T(8,128)S(1)} %get-tuple-element.56), channel_id=1, source_target_pairs={{0,4},{4,8},{8,12},{12,16},{16,20},{20,24},{24,28},{1,5},{5,9},{9,... | collective-permute-start | bytes 417800 | tf_op jit(solution)/shard_map/ppermute | solution.py:143
  36.7 4.5 %collective-permute-start.4 = (f32[34,8,128]{2,1,0:T(8,128)S(1)}, f32[34,8,128]{2,1,0:T(8,128)S(1)}, u32[]{:S(2)}, u32[]{:S(2)}) collective-permute-start(f32[34,8,128]{2,1,0:T(8,128)S(1)} %get-tuple-element.57), channel_id=1, source_target_pairs={{4,0},{8,4},{12,8},{16,12},{20,16},{24,20},{28,24},{5,1},{9,5},{13... | collective-permute-start | bytes 417800 | tf_op jit(solution)/shard_map/ppermute | solution.py:143
  41.3 0.7 collective-permute-done.3.above_ref
  42.1 1.8 %collective-permute-done.4.below_ref = f32[34,8,128]{2,1,0:T(8,128)S(1)} collective-permute-done((f32[34,8,128]{2,1,0:T(8,128)S(1)}, f32[34,8,128]{2,1,0:T(8,128)S(1)}, u32[]{:S(2)}, u32[]{:S(2)}) %collective-permute-start.4) | collective-permute-done | bytes 139296 | tf_op jit(solution)/shard_map/ppermute | solution.py:143
  44.0 4.8 %shard_map.64.grad_ref = f32[64,16,128]{2,1,0:T(8,128)S(1)} custom-call(f32[64,128]{1,0:T(8,128)S(1)} %broadcast_in_dim.4.wx_ref, f32[64,128]{1,0:T(8,128)S(1)} %broadcast_in_dim.5.wy_ref, f32[64,16,128]{2,1,0:T(8,128)S(1)} %copy-done.2, f32[4,16,128]{2,1,0:T(8,128)S(1)} %get-tuple-element.55.beside_ref.around_ref, ...), custom_call_target="tpu_custom_call" | custom-call | tf_op jit(solution)/shard_map/pallas_call | solution.py:27
  48.8 4.5 %collective-permute-done.5.refs_5_ = bf16[2,4,16,128]{3,2,1,0:T(8,128)(2,1)S(1)} collective-permute-done((bf16[2,4,16,128]{3,2,1,0:T(8,128)(2,1)S(1)}, bf16[2,4,16,128]{3,2,1,0:T(8,128)(2,1)S(1)}, u32[]{:S(2)}, u32[]{:S(2)}) %collective-permute-start.5) | collective-permute-done | bytes 32800 | tf_op jit(solution)/shard_map/ppermute | solution.py:497
  54.1 1.9 %collective-permute-start.9 = (bf16[8,16,128]{2,1,0:T(8,128)(2,1)S(1)}, bf16[8,16,128]{2,1,0:T(8,128)(2,1)S(1)}, u32[]{:S(2)}, u32[]{:S(2)}) collective-permute-start(bf16[8,16,128]{2,1,0:T(8,128)(2,1)S(1)} %get-tuple-element.67), channel_id=1, source_target_pairs={{1,0},{2,1},{3,2},{5,4},{6,5},{7,6},{9,8},{10,9},{11,10},{13,12},{... | collective-permute-start | bytes 98312 | tf_op jit(solution)/shard_map/ppermute | solution.py:143
  56.0 3.9 %collective-permute-start.8 = (bf16[8,16,128]{2,1,0:T(8,128)(2,1)S(1)}, bf16[8,16,128]{2,1,0:T(8,128)(2,1)S(1)}, u32[]{:S(2)}, u32[]{:S(2)}) collective-permute-start(bf16[8,16,128]{2,1,0:T(8,128)(2,1)S(1)} %get-tuple-element.67), channel_id=1, source_target_pairs={{0,1},{1,2},{2,3},{4,5},{5,6},{6,7},{8,9},{9,10},{10,11},{12,13},{... | collective-permute-start | bytes 98312 | tf_op jit(solution)/shard_map/ppermute | solution.py:143
  59.9 2.1 %collective-permute-done.8.left_ref = bf16[8,16,128]{2,1,0:T(8,128)(2,1)S(1)} collective-permute-done((bf16[8,16,128]{2,1,0:T(8,128)(2,1)S(1)}, bf16[8,16,128]{2,1,0:T(8,128)(2,1)S(1)}, u32[]{:S(2)}, u32[]{:S(2)}) %collective-permute-start.8) | collective-permute-done | bytes 32800 | tf_op jit(solution)/shard_map/ppermute | solution.py:143
  62.5 1.9 %collective-permute-start.11 = (bf16[16,16,128]{2,1,0:T(8,128)(2,1)S(1)}, bf16[16,16,128]{2,1,0:T(8,128)(2,1)S(1)}, u32[]{:S(2)}, u32[]{:S(2)}) collective-permute-start(bf16[16,16,128]{2,1,0:T(8,128)(2,1)S(1)} %get-tuple-element.69), channel_id=1, source_target_pairs={{4,0},{8,4},{12,8},{16,12},{20,16},{24,20},{28,24},{5,1},{9,5},{13... | collective-permute-start | bytes 196616 | tf_op jit(solution)/shard_map/ppermute | solution.py:143
  64.4 2.4 %collective-permute-start.10 = (bf16[16,16,128]{2,1,0:T(8,128)(2,1)S(1)}, bf16[16,16,128]{2,1,0:T(8,128)(2,1)S(1)}, u32[]{:S(2)}, u32[]{:S(2)}) collective-permute-start(bf16[16,16,128]{2,1,0:T(8,128)(2,1)S(1)} %get-tuple-element.69), channel_id=1, source_target_pairs={{0,4},{4,8},{8,12},{12,16},{16,20},{20,24},{24,28},{1,5},{5,9},{9,... | collective-permute-start | bytes 196616 | tf_op jit(solution)/shard_map/ppermute | solution.py:143
  66.8 4.1 %collective-permute-done.10.above_ref = bf16[16,16,128]{2,1,0:T(8,128)(2,1)S(1)} collective-permute-done((bf16[16,16,128]{2,1,0:T(8,128)(2,1)S(1)}, bf16[16,16,128]{2,1,0:T(8,128)(2,1)S(1)}, u32[]{:S(2)}, u32[]{:S(2)}) %collective-permute-start.10) | collective-permute-done | bytes 65568 | tf_op jit(solution)/shard_map/ppermute | solution.py:143
  70.9 1.0 shard_map.68
  71.8 1.9 %collective-permute-start.12 = (bf16[17,16,128]{2,1,0:T(8,128)(2,1)S(1)}, bf16[17,16,128]{2,1,0:T(8,128)(2,1)S(1)}, u32[]{:S(2)}, u32[]{:S(2)}) collective-permute-start(bf16[17,16,128]{2,1,0:T(8,128)(2,1)S(1)} %get-tuple-element.76), channel_id=1, source_target_pairs={{0,4},{4,8},{8,12},{12,16},{16,20},{20,24},{24,28},{1,5},{5,9},{9,... | collective-permute-start | bytes 208904 | tf_op jit(solution)/shard_map/ppermute | solution.py:143
  73.8 4.5 %collective-permute-start.13 = (bf16[17,16,128]{2,1,0:T(8,128)(2,1)S(1)}, bf16[17,16,128]{2,1,0:T(8,128)(2,1)S(1)}, u32[]{:S(2)}, u32[]{:S(2)}) collective-permute-start(bf16[17,16,128]{2,1,0:T(8,128)(2,1)S(1)} %get-tuple-element.77), channel_id=1, source_target_pairs={{4,0},{8,4},{12,8},{16,12},{20,16},{24,20},{28,24},{5,1},{9,5},{13... | collective-permute-start | bytes 208904 | tf_op jit(solution)/shard_map/ppermute | solution.py:143
  78.3 2.5 %shard_map.69 = (f32[64,16,128]{2,1,0:T(8,128)S(1)}, f32[4,12,3,8,128]{4,3,2,1,0:T(8,128)S(1)}) custom-call(f32[64,128]{1,0:T(8,128)S(1)} %broadcast_in_dim.4.wx_ref, f32[64,128]{1,0:T(8,128)S(1)} %broadcast_in_dim.5.wy_ref, f32[64,16,128]{2,1,0:T(8,128)S(1)} %get-tuple-element.73.x_ref.residual_ref, f32[4,16,128]{2,1,0:T(8,128)S(1)} %get-tuple-element.75.beside_ref), custom_call_target="tpu_custom_call" | custom-call | tf_op jit(solution)/shard_map/pallas_call | solution.py:27
  80.9 2.8 %shard_map.70 = (f32[8,16,128]{2,1,0:T(8,128)S(1)}, bf16[8,16,128]{2,1,0:T(8,128)(2,1)S(1)}) custom-call(f32[64,128]{1,0:T(8,128)S(1)} %broadcast_in_dim.4.wx_ref, f32[64,128]{1,0:T(8,128)S(1)} %broadcast_in_dim.5.wy_ref, f32[64,16,128]{2,1,0:T(8,128)S(1)} %get-tuple-element.73.x_ref.residual_ref, f32[4,16,128]{2,1,0:T(8,128)S(1)} %get-tuple-element.75.beside_ref, ...), custom_call_target="tpu_custom_call" | custom-call | tf_op jit(solution)/shard_map/pallas_call | solution.py:27
  83.7 3.9 %collective-permute-start.15 = (bf16[8,16,128]{2,1,0:T(8,128)(2,1)S(1)}, bf16[8,16,128]{2,1,0:T(8,128)(2,1)S(1)}, u32[]{:S(2)}, u32[]{:S(2)}) collective-permute-start(bf16[8,16,128]{2,1,0:T(8,128)(2,1)S(1)} %get-tuple-element.80), channel_id=1, source_target_pairs={{1,0},{2,1},{3,2},{5,4},{6,5},{7,6},{9,8},{10,9},{11,10},{13,12},{... | collective-permute-start | bytes 98312 | tf_op jit(solution)/shard_map/ppermute | solution.py:143
  87.6 1.9 %collective-permute-start.14 = (bf16[8,16,128]{2,1,0:T(8,128)(2,1)S(1)}, bf16[8,16,128]{2,1,0:T(8,128)(2,1)S(1)}, u32[]{:S(2)}, u32[]{:S(2)}) collective-permute-start(bf16[8,16,128]{2,1,0:T(8,128)(2,1)S(1)} %get-tuple-element.80), channel_id=1, source_target_pairs={{0,1},{1,2},{2,3},{4,5},{5,6},{6,7},{8,9},{9,10},{10,11},{12,13},{... | collective-permute-start | bytes 98312 | tf_op jit(solution)/shard_map/ppermute | solution.py:143
  89.5 3.9 %collective-permute-done.14.left_ref = bf16[8,16,128]{2,1,0:T(8,128)(2,1)S(1)} collective-permute-done((bf16[8,16,128]{2,1,0:T(8,128)(2,1)S(1)}, bf16[8,16,128]{2,1,0:T(8,128)(2,1)S(1)}, u32[]{:S(2)}, u32[]{:S(2)}) %collective-permute-start.14) | collective-permute-done | bytes 32800 | tf_op jit(solution)/shard_map/ppermute | solution.py:143
  93.7 2.5 %collective-permute-start.17 = (bf16[8,16,128]{2,1,0:T(8,128)(2,1)S(1)}, bf16[8,16,128]{2,1,0:T(8,128)(2,1)S(1)}, u32[]{:S(2)}, u32[]{:S(2)}) collective-permute-start(bf16[8,16,128]{2,1,0:T(8,128)(2,1)S(1)} %get-tuple-element.82), channel_id=1, source_target_pairs={{4,0},{8,4},{12,8},{16,12},{20,16},{24,20},{28,24},{5,1},{9,5},{13... | collective-permute-start | bytes 98312 | tf_op jit(solution)/shard_map/ppermute | solution.py:143
  96.2 1.9 %collective-permute-start.16 = (bf16[8,16,128]{2,1,0:T(8,128)(2,1)S(1)}, bf16[8,16,128]{2,1,0:T(8,128)(2,1)S(1)}, u32[]{:S(2)}, u32[]{:S(2)}) collective-permute-start(bf16[8,16,128]{2,1,0:T(8,128)(2,1)S(1)} %get-tuple-element.82), channel_id=1, source_target_pairs={{0,4},{4,8},{8,12},{12,16},{16,20},{20,24},{24,28},{1,5},{5,9},{9,... | collective-permute-start | bytes 98312 | tf_op jit(solution)/shard_map/ppermute | solution.py:143
  98.2 4.2 %collective-permute-done.16.above_ref = bf16[8,16,128]{2,1,0:T(8,128)(2,1)S(1)} collective-permute-done((bf16[8,16,128]{2,1,0:T(8,128)(2,1)S(1)}, bf16[8,16,128]{2,1,0:T(8,128)(2,1)S(1)}, u32[]{:S(2)}, u32[]{:S(2)}) %collective-permute-start.16) | collective-permute-done | bytes 32800 | tf_op jit(solution)/shard_map/ppermute | solution.py:143
  102.4 1.6 %shard_map.72 = (f32[64,16,128]{2,1,0:T(8,128)}, f32[64,16,128]{2,1,0:T(8,128)}) custom-call(f32[64,16,128]{2,1,0:T(8,128)S(1)} %get-tuple-element.73.x_ref.residual_ref, f32[64,16,128]{2,1,0:T(8,128)S(1)} %get-tuple-element.74.before_ref, bf16[8,16,128]{2,1,0:T(8,128)(2,1)S(1)} %collective-permute-done.16.above_ref, ...), custom_call_target="tpu_custom_call" | custom-call | tf_op jit(solution)/shard_map/pallas_call | solution.py:552
  (32 shorter events, 2.7 us)
Async XLA Ops:
  0.6 1.6 %copy-start = (bf16[2,64,16,512]{3,2,1,0:T(8,128)(2,1)S(1)}, bf16[2,64,16,512]{3,2,1,0:T(8,128)(2,1)}, u32[]{:S(2)}) copy-start(bf16[2,64,16,512]{3,2,1,0:T(8,128)(2,1)} %in_ref.3) | copy-start | bytes 6291460
  2.2 9.1 %copy-start.1 = (bf16[2,64,16,512]{3,2,1,0:T(8,128)(2,1)S(1)}, bf16[2,64,16,512]{3,2,1,0:T(8,128)(2,1)}, u32[]{:S(2)}) copy-start(bf16[2,64,16,512]{3,2,1,0:T(8,128)(2,1)} %in_ref.3) | copy-start | bytes 6291460
  2.4 32.3 %collective-permute-start = (bf16[2,64,16,128]{3,2,1,0:T(8,128)(2,1)S(1)}, bf16[2,64,16,128]{3,2,1,0:T(8,128)(2,1)S(1)}, u32[]{:S(2)}, u32[]{:S(2)}) collective-permute-start(bf16[2,64,16,128]{3,2,1,0:T(8,128)(2,1)S(1)} %get-tuple-element.51), channel_id=1, source_target_pairs={{0,1},{1,2},{2,3},{3,0},{4,5},{5,6},{6,7},{7,4},{8,9},{9,10},{10,1... | collective-permute-start | bytes 1572872 | tf_op jit(solution)/shard_map/ppermute | solution.py:497
  4.0 1.0 %copy-start.2 = (f32[64,16,128]{2,1,0:T(8,128)S(1)}, f32[64,16,128]{2,1,0:T(8,128)}, u32[]{:S(2)}) copy-start(f32[64,16,128]{2,1,0:T(8,128)} %residual_ref) | copy-start | bytes 1572868
  5.4 29.3 %collective-permute-start.1 = (f32[4,16,128]{2,1,0:T(8,128)S(1)}, f32[4,16,128]{2,1,0:T(8,128)S(1)}, u32[]{:S(2)}, u32[]{:S(2)}) collective-permute-start(f32[4,16,128]{2,1,0:T(8,128)S(1)} %get-tuple-element.52), channel_id=1, source_target_pairs={{0,1},{1,2},{2,3},{4,5},{5,6},{6,7},{8,9},{9,10},{10,11},{12,13},{... | collective-permute-start | bytes 98312 | tf_op jit(solution)/shard_map/ppermute | solution.py:143
  7.7 36.1 %copy-start.4 = (f32[64]{0:T(128)S(1)}, f32[64]{0:T(128)}, u32[]{:S(2)}) copy-start(f32[64]{0:T(128)} %param.6) | copy-start | bytes 772
  7.7 36.2 %copy-start.5 = (f32[64]{0:T(128)S(1)}, f32[64]{0:T(128)}, u32[]{:S(2)}) copy-start(f32[64]{0:T(128)} %param.7) | copy-start | bytes 772
  7.7 27.0 %collective-permute-start.2 = (f32[4,16,128]{2,1,0:T(8,128)S(1)}, f32[4,16,128]{2,1,0:T(8,128)S(1)}, u32[]{:S(2)}, u32[]{:S(2)}) collective-permute-start(f32[4,16,128]{2,1,0:T(8,128)S(1)} %get-tuple-element.45), channel_id=1, source_target_pairs={{1,0},{2,1},{3,2},{5,4},{6,5},{7,6},{9,8},{10,9},{11,10},{13,12},{... | collective-permute-start | bytes 98312 | tf_op jit(solution)/shard_map/ppermute | solution.py:143
  12.3 41.0 %collective-permute-start.6 = (bf16[2,68,16,128]{3,2,1,0:T(8,128)(2,1)S(1)}, bf16[2,68,16,128]{3,2,1,0:T(8,128)(2,1)S(1)}, u32[]{:S(2)}, u32[]{:S(2)}) collective-permute-start(bf16[2,68,16,128]{3,2,1,0:T(8,128)(2,1)S(1)} %shard_map.61), channel_id=1, source_target_pairs={{0,3},{1,0},{2,1},{3,2},{4,7},{5,4},{6,5},{7,6},{8,11},{9,8},{10,9... | collective-permute-start | bytes 1671176 | tf_op jit(solution)/shard_map/ppermute | solution.py:497
  34.7 19.0 %collective-permute-start.7 = (bf16[2,68,16,128]{3,2,1,0:T(8,128)(2,1)S(1)}, bf16[2,68,16,128]{3,2,1,0:T(8,128)(2,1)S(1)}, u32[]{:S(2)}, u32[]{:S(2)}) collective-permute-start(bf16[2,68,16,128]{3,2,1,0:T(8,128)(2,1)S(1)} %get-tuple-element.66), channel_id=1, source_target_pairs={{0,2},{1,3},{2,0},{3,1},{4,6},{5,7},{6,4},{7,5},{8,10},{9,11},{10,... | collective-permute-start | bytes 1671176 | tf_op jit(solution)/shard_map/ppermute | solution.py:497
  34.8 7.3 %collective-permute-start.3 = (f32[34,8,128]{2,1,0:T(8,128)S(1)}, f32[34,8,128]{2,1,0:T(8,128)S(1)}, u32[]{:S(2)}, u32[]{:S(2)}) collective-permute-start(f32[34,8,128]{2,1,0:T(8,128)S(1)} %get-tuple-element.56), channel_id=1, source_target_pairs={{0,4},{4,8},{8,12},{12,16},{16,20},{20,24},{24,28},{1,5},{5,9},{9,... | collective-permute-start | bytes 417800 | tf_op jit(solution)/shard_map/ppermute | solution.py:143
  36.7 7.1 %collective-permute-start.4 = (f32[34,8,128]{2,1,0:T(8,128)S(1)}, f32[34,8,128]{2,1,0:T(8,128)S(1)}, u32[]{:S(2)}, u32[]{:S(2)}) collective-permute-start(f32[34,8,128]{2,1,0:T(8,128)S(1)} %get-tuple-element.57), channel_id=1, source_target_pairs={{4,0},{8,4},{12,8},{16,12},{20,16},{24,20},{28,24},{5,1},{9,5},{13... | collective-permute-start | bytes 417800 | tf_op jit(solution)/shard_map/ppermute | solution.py:143
  41.3 12.0 %collective-permute-start.5 = (bf16[2,4,16,128]{3,2,1,0:T(8,128)(2,1)S(1)}, bf16[2,4,16,128]{3,2,1,0:T(8,128)(2,1)S(1)}, u32[]{:S(2)}, u32[]{:S(2)}) collective-permute-start(bf16[2,4,16,128]{3,2,1,0:T(8,128)(2,1)S(1)} %get-tuple-element.59), channel_id=1, source_target_pairs={{0,1},{1,2},{2,3},{3,0},{4,5},{5,6},{6,7},{7,4},{8,9},{9,10},{10,1... | collective-permute-start | bytes 98312 | tf_op jit(solution)/shard_map/ppermute | solution.py:497
  44.0 26.9 %copy-start.3 = (f32[64,16,128]{2,1,0:T(8,128)S(1)}, f32[64,16,128]{2,1,0:T(8,128)}, u32[]{:S(2)}) copy-start(f32[64,16,128]{2,1,0:T(8,128)} %residual_ref) | copy-start | bytes 1572868
  54.1 5.9 %collective-permute-start.9 = (bf16[8,16,128]{2,1,0:T(8,128)(2,1)S(1)}, bf16[8,16,128]{2,1,0:T(8,128)(2,1)S(1)}, u32[]{:S(2)}, u32[]{:S(2)}) collective-permute-start(bf16[8,16,128]{2,1,0:T(8,128)(2,1)S(1)} %get-tuple-element.67), channel_id=1, source_target_pairs={{1,0},{2,1},{3,2},{5,4},{6,5},{7,6},{9,8},{10,9},{11,10},{13,12},{... | collective-permute-start | bytes 98312 | tf_op jit(solution)/shard_map/ppermute | solution.py:143
  56.0 6.1 %collective-permute-start.8 = (bf16[8,16,128]{2,1,0:T(8,128)(2,1)S(1)}, bf16[8,16,128]{2,1,0:T(8,128)(2,1)S(1)}, u32[]{:S(2)}, u32[]{:S(2)}) collective-permute-start(bf16[8,16,128]{2,1,0:T(8,128)(2,1)S(1)} %get-tuple-element.67), channel_id=1, source_target_pairs={{0,1},{1,2},{2,3},{4,5},{5,6},{6,7},{8,9},{9,10},{10,11},{12,13},{... | collective-permute-start | bytes 98312 | tf_op jit(solution)/shard_map/ppermute | solution.py:143
  62.5 4.3 %collective-permute-start.11 = (bf16[16,16,128]{2,1,0:T(8,128)(2,1)S(1)}, bf16[16,16,128]{2,1,0:T(8,128)(2,1)S(1)}, u32[]{:S(2)}, u32[]{:S(2)}) collective-permute-start(bf16[16,16,128]{2,1,0:T(8,128)(2,1)S(1)} %get-tuple-element.69), channel_id=1, source_target_pairs={{4,0},{8,4},{12,8},{16,12},{20,16},{24,20},{28,24},{5,1},{9,5},{13... | collective-permute-start | bytes 196616 | tf_op jit(solution)/shard_map/ppermute | solution.py:143
  64.4 6.5 %collective-permute-start.10 = (bf16[16,16,128]{2,1,0:T(8,128)(2,1)S(1)}, bf16[16,16,128]{2,1,0:T(8,128)(2,1)S(1)}, u32[]{:S(2)}, u32[]{:S(2)}) collective-permute-start(bf16[16,16,128]{2,1,0:T(8,128)(2,1)S(1)} %get-tuple-element.69), channel_id=1, source_target_pairs={{0,4},{4,8},{8,12},{12,16},{16,20},{20,24},{24,28},{1,5},{5,9},{9,... | collective-permute-start | bytes 196616 | tf_op jit(solution)/shard_map/ppermute | solution.py:143
  71.8 9.0 %collective-permute-start.12 = (bf16[17,16,128]{2,1,0:T(8,128)(2,1)S(1)}, bf16[17,16,128]{2,1,0:T(8,128)(2,1)S(1)}, u32[]{:S(2)}, u32[]{:S(2)}) collective-permute-start(bf16[17,16,128]{2,1,0:T(8,128)(2,1)S(1)} %get-tuple-element.76), channel_id=1, source_target_pairs={{0,4},{4,8},{8,12},{12,16},{16,20},{20,24},{24,28},{1,5},{5,9},{9,... | collective-permute-start | bytes 208904 | tf_op jit(solution)/shard_map/ppermute | solution.py:143
  73.8 7.1 %collective-permute-start.13 = (bf16[17,16,128]{2,1,0:T(8,128)(2,1)S(1)}, bf16[17,16,128]{2,1,0:T(8,128)(2,1)S(1)}, u32[]{:S(2)}, u32[]{:S(2)}) collective-permute-start(bf16[17,16,128]{2,1,0:T(8,128)(2,1)S(1)} %get-tuple-element.77), channel_id=1, source_target_pairs={{4,0},{8,4},{12,8},{16,12},{20,16},{24,20},{28,24},{5,1},{9,5},{13... | collective-permute-start | bytes 208904 | tf_op jit(solution)/shard_map/ppermute | solution.py:143
  83.7 5.9 %collective-permute-start.15 = (bf16[8,16,128]{2,1,0:T(8,128)(2,1)S(1)}, bf16[8,16,128]{2,1,0:T(8,128)(2,1)S(1)}, u32[]{:S(2)}, u32[]{:S(2)}) collective-permute-start(bf16[8,16,128]{2,1,0:T(8,128)(2,1)S(1)} %get-tuple-element.80), channel_id=1, source_target_pairs={{1,0},{2,1},{3,2},{5,4},{6,5},{7,6},{9,8},{10,9},{11,10},{13,12},{... | collective-permute-start | bytes 98312 | tf_op jit(solution)/shard_map/ppermute | solution.py:143
  87.6 5.8 %collective-permute-start.14 = (bf16[8,16,128]{2,1,0:T(8,128)(2,1)S(1)}, bf16[8,16,128]{2,1,0:T(8,128)(2,1)S(1)}, u32[]{:S(2)}, u32[]{:S(2)}) collective-permute-start(bf16[8,16,128]{2,1,0:T(8,128)(2,1)S(1)} %get-tuple-element.80), channel_id=1, source_target_pairs={{0,1},{1,2},{2,3},{4,5},{5,6},{6,7},{8,9},{9,10},{10,11},{12,13},{... | collective-permute-start | bytes 98312 | tf_op jit(solution)/shard_map/ppermute | solution.py:143
  93.7 4.5 %collective-permute-start.17 = (bf16[8,16,128]{2,1,0:T(8,128)(2,1)S(1)}, bf16[8,16,128]{2,1,0:T(8,128)(2,1)S(1)}, u32[]{:S(2)}, u32[]{:S(2)}) collective-permute-start(bf16[8,16,128]{2,1,0:T(8,128)(2,1)S(1)} %get-tuple-element.82), channel_id=1, source_target_pairs={{4,0},{8,4},{12,8},{16,12},{20,16},{24,20},{28,24},{5,1},{9,5},{13... | collective-permute-start | bytes 98312 | tf_op jit(solution)/shard_map/ppermute | solution.py:143
  96.2 6.1 %collective-permute-start.16 = (bf16[8,16,128]{2,1,0:T(8,128)(2,1)S(1)}, bf16[8,16,128]{2,1,0:T(8,128)(2,1)S(1)}, u32[]{:S(2)}, u32[]{:S(2)}) collective-permute-start(bf16[8,16,128]{2,1,0:T(8,128)(2,1)S(1)} %get-tuple-element.82), channel_id=1, source_target_pairs={{0,4},{4,8},{8,12},{12,16},{16,20},{20,24},{24,28},{1,5},{5,9},{9,... | collective-permute-start | bytes 98312 | tf_op jit(solution)/shard_map/ppermute | solution.py:143
